TPU v7x, 32 devices: a whole 2x2x4 slice. The times are simulated.
32 devices in a mesh: dp: 8 (over z, y), tensor: 4 (over x, core).
Axes of the slice: x: 2, y: 2, z: 4, core: 2. Of those that a mesh axis runs over, the one named last changes fastest.
Arguments:
- cotangent: bfloat16 [1024, 4096], P('dp', 'tensor'), may hold values from -6 to 6
- gate_pre: bfloat16 [1024, 14336], P('dp', 'tensor'), may hold values from -6 to 6
- up_pre: bfloat16 [1024, 14336], P('dp', 'tensor'), may hold values from -6 to 6
- down_weight: bfloat16 [14336, 4096], P('tensor', 'dp'), may hold values from -0.046875 to 0.046875
Outputs:
- grad_gate: bfloat16 [1024, 14336], P('dp', 'tensor')
- grad_up: bfloat16 [1024, 14336], P('dp', 'tensor')
- grad_down: float32 [14336, 4096], P('tensor', 'dp')
All inputs are finite; a program needn't handle non-finite values.
Results may differ from a plain program's by a relative error of at most 0.003.
Values may be sent and summed in bfloat16 or wider, within the bound.
No kernel may reach another device: no remote copies, remote signals or barrier semaphores. Data moves between devices by JAX's collectives and lax.ppermute only.
A program may use at most 128 MiB of HBM per device.

v0:
```python
import jax
import jax.numpy as jnp
from jax import lax
from jax.sharding import PartitionSpec as P


def shards(cotangent, gate_pre, up_pre, down_weight):
    gathered = lax.all_gather(cotangent, "tensor", axis=1, tiled=True)
    gate_vals = gate_pre.astype(jnp.float32)
    up_vals = up_pre.astype(jnp.float32)
    sigma = jax.nn.sigmoid(gate_vals)
    act_vals = gate_vals * sigma
    hidden = (act_vals * up_vals).astype(jnp.bfloat16)
    total_tokens = gathered.shape[0] * lax.axis_size("dp")
    dhid = lax.dot_general(
        gathered,
        lax.all_gather(down_weight, "dp", axis=1, tiled=True),
        (((1,), (1,)), ((), ())),
        preferred_element_type=jnp.float32,
    )
    feature_cols = lax.all_to_all(gathered, "dp", split_axis=1, concat_axis=0, tiled=True)
    summed = lax.dot_general(
        lax.all_gather(hidden, "dp", axis=0, tiled=True),
        feature_cols,
        (((0,), (0,)), ((), ())),
        preferred_element_type=jnp.float32,
    )
    grad_down = summed * total_tokens ** (-0.5)
    grad_up = (dhid * act_vals).astype(jnp.bfloat16)
    grad_gate = (dhid * up_vals * sigma * (1.0 + gate_vals * (1.0 - sigma))).astype(jnp.bfloat16)
    return (grad_gate, grad_up, grad_down)


def solution(mesh):
    in_specs = (P("dp", "tensor"), P("dp", "tensor"), P("dp", "tensor"), P("tensor", "dp"))
    out_specs = (P("dp", "tensor"), P("dp", "tensor"), P("tensor", "dp"))
    return jax.shard_map(shards, mesh=mesh, in_specs=in_specs, out_specs=out_specs, check_vma=False)
```

profile of v0, /device:TPU:0, one launch (start us, length us, event | category | flops | bytes accessed | tf_op | source)
XLA Modules:
  0.0 752.1 jit_solution(5535961966290955441)
XLA Ops:
  7.2 0.0 all-gather.4.cloned.1.call-start
  7.2 1.8 copy.7
  9.0 0.0 all-gather.4.cloned.1.call-update
  9.0 0.0 copy-start.1
  9.0 0.0 copy-start.2
  9.0 0.0 all-gather.6.cloned.1.call-start
  9.1 0.7 all-gather.6.cloned.1.call-update
  9.8 0.0 all-gather.8.cloned.1.call-start
  9.8 19.7 %all-gather.4.cloned.1.call-done = bf16[128,4096]{0,1:T(8,128)(2,1)} async-done(((bf16[128,1024]{0,1:T(8,128)(2,1)}), bf16[128,4096]{0,1:T(8,128)(2,1)}) %all-gather.4.cloned.1.call-update) | async-done | bytes 1048592 | tf_op jit(solution)/shard_map/all_gather | solution.py:8
  29.6 0.0 copy-start
  29.6 560.7 %all-gather.6.cloned.1.call-done = bf16[3584,4096]{1,0:T(8,128)(2,1)} async-done(((bf16[3584,512]{1,0:T(8,128)(2,1)}), bf16[3584,4096]{1,0:T(8,128)(2,1)}) %all-gather.6.cloned.1.call-update) | async-done | bytes 29360144 | tf_op jit(solution)/shard_map/all_gather | solution.py:17
  590.3 0.0 copy-done.1
  590.3 0.0 copy-done.2
  590.3 16.3 %multiply_convert_fusion = (bf16[128,3584]{1,0:T(8,128)(2,1)}, bf16[128,3584]{1,0:T(8,128)(2,1)}, bf16[128,3584]{1,0:T(8,128)(2,1)}) fusion(bf16[128,3584]{1,0:T(8,128)(2,1)S(1)} %copy-done.1, bf16[128,3584]{1,0:T(8,128)(2,1)S(1)} %copy-done.2, bf16[128,4096]{0,1:T(8,128)(2,1)} %all-gather.4.cloned.1.call-done, ...), kind=kOutput, calls=%fused_computation.14 | convolution fusion | flops 3765895168 | bytes 34996224 | tf_op jit(solution)/shard_map/dot_general | solution.py:15
  606.5 0.0 all-gather.8.cloned.1.call-update
  606.5 0.0 copy-done
  606.6 53.5 %all_to_all.19 = bf16[128,8,512]{0,2,1:T(8,128)(2,1)S(1)} all-to-all(bf16[128,8,512]{0,2,1:T(8,128)(2,1)S(1)} %bitcast.8), channel_id=1, replica_groups=mesh['dp'=8,'tensor'=4] {'dp'}, dimensions={1} | all-to-all | bytes 2097152 | tf_op jit(solution)/shard_map/all_to_all | solution.py:21
  660.1 0.5 copy.8
  660.6 75.8 %all-gather.8.cloned.1.call-done = bf16[1024,3584]{1,0:T(8,128)(2,1)} async-done(((bf16[128,3584]{1,0:T(8,128)(2,1)}), bf16[1024,3584]{1,0:T(8,128)(2,1)}) %all-gather.8.cloned.1.call-update) | async-done | bytes 7340048 | tf_op jit(solution)/shard_map/all_gather | solution.py:23
  736.4 9.2 %convolution_multiply_fusion = f32[3584,512]{1,0:T(8,128)} fusion(bf16[1024,3584]{1,0:T(8,128)(2,1)} %all-gather.8.cloned.1.call-done, bf16[1024,512]{1,0:T(8,128)(2,1)S(1)} %bitcast.9), kind=kOutput, calls=%fused_computation | convolution fusion | flops 3759931392 | bytes 15728640 | tf_op jit(solution)/shard_map/dot_general | solution.py:22
Async XLA Ops:
  7.2 22.4 %all-gather.4.cloned.1.call-start = ((), (), s32[]{:S(2)}) async-start(), calls=%async_computation.1 | async-start | bytes 1310720 | tf_op jit(solution)/shard_map/all_gather | solution.py:8
  9.0 581.2 %copy-start.1 = (bf16[128,3584]{1,0:T(8,128)(2,1)S(1)}, bf16[128,3584]{1,0:T(8,128)(2,1)}, u32[]{:S(2)}) copy-start(bf16[128,3584]{1,0:T(8,128)(2,1)} %param.5) | copy-start | bytes 2752516
  9.0 581.2 %copy-start.2 = (bf16[128,3584]{1,0:T(8,128)(2,1)S(1)}, bf16[128,3584]{1,0:T(8,128)(2,1)}, u32[]{:S(2)}) copy-start(bf16[128,3584]{1,0:T(8,128)(2,1)} %param.6) | copy-start | bytes 2752516
  9.0 581.2 %all-gather.6.cloned.1.call-start = ((), (), s32[]{:S(2)}) async-start(), calls=%async_computation.2 | async-start | bytes 33030144 | tf_op jit(solution)/shard_map/all_gather | solution.py:17
  9.8 726.6 %all-gather.8.cloned.1.call-start = ((), (), s32[]{:S(2)}) async-start(), calls=%async_computation.3 | async-start | bytes 8257536 | tf_op jit(solution)/shard_map/all_gather | solution.py:23
  29.6 577.0 %copy-start = (bf16[128,4096]{0,1:T(8,128)(2,1)S(1)}, bf16[128,4096]{0,1:T(8,128)(2,1)}, u32[]{:S(2)}) copy-start(bf16[128,4096]{0,1:T(8,128)(2,1)} %all-gather.4.cloned.1.call-done) | copy-start | bytes 3145732
Sparse Core Ops, SparseCore 0:
  10.1 19.4 all-gather.3
  31.1 559.0 all-gather.5
  606.7 129.7 all-gather.7
where the time goes:
time: 752 us
  waiting for transfers between devices  657 us (87%)
  blocking collectives  53.5 us (7%)
  matrix products  25.4 us (3%)
  between operations  13.8 us (2%)
    all_gather x1, waiting for transfers between devices, shards(): lax.all_gather(down_weight, 'dp', axis=1, tiled=True)  561 us
    all_gather x1, waiting for transfers between devices, shards(): lax.all_gather(hidden, 'dp', axis=0, tiled=True)  75.8 us
    all_to_all x1, blocking collectives, shards(): lax.all_to_all(gathered, 'dp', split_axis=1, concat_axis=0, tiled=True)  53.5 us
    all_gather x1, waiting for transfers between devices, shards(): gathered = lax.all_gather(cotangent, 'tensor', axis=1, tiled=True)  19.7 us
    dot_general x1, matrix products, shards(): lax.dot_general(gathered, lax.all_gather(down_weight, 'dp', axis=1, tiled...  16.3 us
  transfers between devices with their start and end apart: 3, of which 3 were waited for; matrix products, arithmetic and copies ran while one was open for 0% of the time, Pallas kernels for 0%

commit v1 on v0

v1 whole, which is shorter than its diff:
```python
import jax
import jax.numpy as jnp
from jax import lax
from jax.sharding import PartitionSpec as P

WIRE = jnp.float16
WIRE_SCALE = 16.0


def after(value, *others):
    return lax.optimization_barrier((value,) + others)[0]


def shards(cotangent, gate_pre, up_pre, down_weight):
    dp, tensor = lax.axis_size("dp"), lax.axis_size("tensor")
    line = dp // 2
    tokens, features = cotangent.shape
    hidden_units, half = down_weight.shape
    assert features == 2 * half and line == tensor and line % 2 == 0
    position, side = lax.axis_index("dp") // 2, lax.axis_index("dp") % 2
    shard = lax.axis_index("tensor")
    columns = hidden_units * 4 // 7

    def along(name, value, step, first, last):
        pairs = [(2 * at + s, 2 * (at + step) + s) for at in range(first, last + 1) for s in (0, 1)]
        with jax.named_scope(name):
            return lax.ppermute(value, "dp", pairs)

    def across(name, value):
        with jax.named_scope(name):
            return lax.ppermute(value, "dp", [(at, at ^ 1) for at in range(dp)])

    gate_vals = gate_pre.astype(jnp.float32)
    up_vals = up_pre.astype(jnp.float32)
    sigma = jax.nn.sigmoid(gate_vals)
    act_vals = gate_vals * sigma
    hidden = (act_vals * up_vals).astype(jnp.bfloat16)
    first, last = hidden[:, :columns], hidden[:, columns:]
    weight_first, weight_last = down_weight[:columns], down_weight[columns:]

    last_other = across("hidden_last_side", last)
    first_up = along("hidden_first_up1", first, 1, 0, line - 2)
    first_down = along("hidden_first_down1", first, -1, 1, line - 1)
    weight_other = across("weight_side", weight_first)

    block = after(cotangent, hidden)
    arrived = []
    for turn in range(tensor // 2):
        pairs = [
            ((2 * at + s) * tensor + owner, (2 * owner + s) * tensor + (at + 2 * turn) % tensor)
            for at in range(line)
            for s in (0, 1)
            for owner in range(tensor)
        ]
        with jax.named_scope("cotangent_spread"):
            arrived.append(lax.ppermute(block, ("dp", "tensor"), pairs))
    odd = (position - shard) % 2
    turned = ((shard - position + odd) % line) // 2
    row = lax.dynamic_slice_in_dim(jnp.stack(arrived + arrived), turned, line // 2, 0)
    mine = jnp.where(side == 0, row[..., :half], row[..., half:])
    other = jnp.where(side == 0, row[..., half:], row[..., :half])
    theirs = across("cotangent_side", after(other, last_other))

    both_last = jnp.stack([last, last_other])
    last_up = along("hidden_last_up1", both_last, 1, 0, line - 2)
    last_down = along("hidden_last_down1", both_last, -1, 1, line - 1)

    own = jnp.stack([mine, other, theirs])
    with jax.named_scope("cotangent_core"):
        swapped = lax.ppermute(
            after(own, first_up, first_down), "tensor", [(at, at ^ 1) for at in range(tensor)]
        )
    whole = jnp.stack([jnp.where(odd == 0, own, swapped), jnp.where(odd == 0, swapped, own)], axis=2)
    mine, other, theirs = whole.reshape(3, line, tokens, half)
    features_of_all = jnp.stack([mine, theirs], axis=1)

    def product(left, right):
        return jnp.einsum("...f,hf->...h", left, right, preferred_element_type=jnp.float32)

    parts = {"last": product(features_of_all, weight_last) * WIRE_SCALE}
    parts["first"] = (product(mine, weight_first) + product(other, weight_other)) * WIRE_SCALE

    rising = {"first": [first, first_up], "last": [both_last, last_up]}
    falling = {"first": [first, first_down], "last": [both_last, last_down]}
    up_sum = {"first": 0.0, "last": 0.0}
    down_sum = {"first": 0.0, "last": 0.0}
    sides = {}
    steps = [(first_up, first_down), (last_up, last_down)]

    def gather_step(which, step, waits):
        up = along(f"hidden_{which}_up{step}", after(rising[which][-1], *waits), 1, step - 1, line - 2)
        down = along(f"hidden_{which}_down{step}", after(falling[which][-1], *waits), -1, 1, line - step)
        rising[which].append(up)
        falling[which].append(down)
        return up, down

    def sum_step(which, step, waits):
        message = after((parts[which][step] + up_sum[which]).astype(WIRE), *waits)
        up = along(f"dhid_{which}_up{step}", message, 1, 0, step - 1)
        message = after((parts[which][line - step] + down_sum[which]).astype(WIRE), *waits)
        down = along(f"dhid_{which}_down{step}", message, -1, line - step, line - 1)
        up_sum[which], down_sum[which] = up.astype(jnp.float32), down.astype(jnp.float32)
        return up, down

    def gathered(which, k):
        if k == 0:
            return rising[which][0]
        return jnp.where(position >= k, rising[which][k], falling[which][line - k])

    def exchange(*ks):
        blocks = jnp.stack([gathered("first", k) for k in ks])
        swapped = across("hidden_first_side", after(blocks, weight_other))
        for n, k in enumerate(ks):
            sides[k] = blocks[n], swapped[n]
        return (swapped,)

    for step in range(1, line):
        for which, summed in (("first", "last"), ("last", "first")):
            waits, ended = steps[-2], ()
            if step + 1 < line:
                ended += gather_step(which, step + 1, waits)
            ended += sum_step(summed, step, waits)
            if which == "last":
                ready = [k for k in range(line) if max(k, line - k if k else 1) == step]
                if ready:
                    ended += exchange(*ready)
            steps.append(ended)

    def total(which):
        return parts[which][0] + up_sum[which] + down_sum[which]

    pair = total("last")
    dhid_last = pair[0] + across("dhid_last_side", pair[1].astype(WIRE)).astype(jnp.float32)
    dhid = jnp.concatenate([total("first"), dhid_last], axis=1) * (1.0 / WIRE_SCALE)

    grad_up = (dhid * act_vals).astype(jnp.bfloat16)
    grad_gate = (dhid * up_vals * sigma * (1.0 + gate_vals * (1.0 - sigma))).astype(jnp.bfloat16)

    hidden_first = jnp.stack([jnp.stack(sides[k]) for k in range(line)])
    hidden_last = jnp.stack([gathered("last", k) for k in range(line)])

    def weight_grad(values):
        return jnp.einsum("kstc,kstf->cf", values, features_of_all, preferred_element_type=jnp.float32)

    grad_down = jnp.concatenate([weight_grad(hidden_first), weight_grad(hidden_last)]) * (tokens * dp) ** (-0.5)
    return grad_gate, grad_up, grad_down


def solution(mesh):
    in_specs = (P("dp", "tensor"), P("dp", "tensor"), P("dp", "tensor"), P("tensor", "dp"))
    out_specs = (P("dp", "tensor"), P("dp", "tensor"), P("tensor", "dp"))
    return jax.shard_map(shards, mesh=mesh, in_specs=in_specs, out_specs=out_specs, check_vma=False)
```

time: 752 us -> 195 us (0.26)
  waiting for transfers between devices: 657 us -> 85.7 us
  starting transfers between devices: 0.12 us -> 74.7 us
  blocking collectives: 53.5 us -> 0 us
  other arithmetic: 0 us -> 20.2 us
  matrix products: 25.4 us -> 8.78 us
  between operations: 13.8 us -> 1.17 us
    all_gather x3 -> x0, waiting for transfers between devices: 656 us -> none  [the longest x1 561 us: shards(): lax.all_gather(down_weight, 'dp', axis=1, tiled=True)]
    ppermute x0 -> x34, waiting for transfers between devices: none -> 85.7 us  [the longest x24 55.3 us: along(): return lax.ppermute(value, 'dp', pairs)]
    ppermute x0 -> x34, starting transfers between devices: none -> 74.7 us  [the longest x24 57.2 us: along(): return lax.ppermute(value, 'dp', pairs)]
    all_to_all x1 -> x0, blocking collectives: 53.5 us -> none  [shards(): lax.all_to_all(gathered, 'dp', split_axis=1, concat_axis=0, tiled=True)]
    dot_general x2 -> x5, matrix products: 25.4 us -> 8.78 us  [the longest x3 4.5 us: product(): jnp.einsum('...f,hf->...h', left, right, preferred_element_type=jnp.float32)]
  transfers between devices with their start and end apart: 3 -> 34, of which waited for: 3 -> 15; matrix products, arithmetic and copies ran while one was open for 0% -> 14% of each run, Pallas kernels for 0% -> 0%
where the time goes in v1:
time: 195 us; the launch traced here: 194 us
  waiting for transfers between devices  85.7 us (44%)
  starting transfers between devices  74.7 us (38%)
  other arithmetic  20.2 us (10%)
  matrix products  8.78 us (5%)
  local copies, waits for them, and re-layouts  3.89 us (2%)
    ppermute x24, starting transfers between devices, along(): return lax.ppermute(value, 'dp', pairs)  57.2 us
    ppermute x24, waiting for transfers between devices, along(): return lax.ppermute(value, 'dp', pairs)  55.3 us
    ppermute x2, waiting for transfers between devices, shards(): arrived.append(lax.ppermute(block, ('dp', 'tensor'), pairs))  15.7 us
    ppermute x7, waiting for transfers between devices, across(): return lax.ppermute(value, 'dp', [(at, at ^ 1) for at in range(dp)])  14.8 us
    ppermute x7, starting transfers between devices, across(): return lax.ppermute(value, 'dp', [(at, at ^ 1) for at in range(dp)])  10 us
    ppermute x2, starting transfers between devices, shards(): arrived.append(lax.ppermute(block, ('dp', 'tensor'), pairs))  7.46 us
    dot_general x3, matrix products, product(): jnp.einsum('...f,hf->...h', left, right, preferred_element_type=jnp.float32)  4.5 us
    dot_general x2, matrix products, weight_grad(): jnp.einsum('kstc,kstf->cf', values, features_of_all, preferred_element_ty...  4.28 us
  transfers between devices with their start and end apart: 34, of which 15 were waited for; matrix products, arithmetic and copies ran while one was open for 14% of the time, Pallas kernels for 0%

profile of v1, /device:TPU:0, one launch (start us, length us, event | category | flops | bytes accessed | tf_op | source)
XLA Modules:
  0.0 194.5 jit_solution(6470589850557395239)
XLA Ops:
  0.6 2.0 %fusion.21 = bf16[128,3584]{1,0:T(8,128)(2,1)S(1)} fusion(bf16[128,3584]{1,0:T(8,128)(2,1)} %param.6, bf16[128,3584]{1,0:T(8,128)(2,1)} %param.5), kind=kLoop, calls=%fused_computation.28 | loop fusion | flops 3670016 | bytes 2752512 | tf_op jit(solution)/shard_map/convert_element_type | solution.py:37
  3.4 6.8 %collective-permute-start.1 = (bf16[128,1024]{1,0:T(8,128)(2,1)S(1)}, bf16[128,1024]{1,0:T(8,128)(2,1)S(1)}, u32[]{:S(2)}, u32[]{:S(2)}) collective-permute-start(bf16[128,1024]{1,0:T(8,128)(2,1)S(1)} %copy-done.4), channel_id=1, source_target_pairs={{0,2},{1,10},{2,18},{3,26},{4,6},{5,14},{6,22},{7,30},{8,3},{9,11}... | collective-permute-start | bytes 786440 | tf_op jit(solution)/shard_map/cotangent_spread/ppermute | solution.py:56
  10.3 4.9 %collective-permute-start.4 = (bf16[128,2048]{1,0:T(8,128)(2,1)S(1)}, bf16[128,2048]{1,0:T(8,128)(2,1)}, u32[]{:S(2)}, u32[]{:S(2)}) collective-permute-start(bf16[128,2048]{1,0:T(8,128)(2,1)S(1)} %get-tuple-element.77), channel_id=1, source_target_pairs={{0,8},{4,12},{8,16},{12,20},{16,24},{20,28},{1,9},{5,13},{9,17},{1... | collective-permute-start | bytes 1572872 | tf_op jit(solution)/shard_map/hidden_first_up1/ppermute | solution.py:27
  18.1 15.7 %collective-permute-done.1 = bf16[128,1024]{1,0:T(8,128)(2,1)S(1)} collective-permute-done((bf16[128,1024]{1,0:T(8,128)(2,1)S(1)}, bf16[128,1024]{1,0:T(8,128)(2,1)S(1)}, u32[]{:S(2)}, u32[]{:S(2)}) %collective-permute-start.1) | collective-permute-done | bytes 262176 | tf_op jit(solution)/shard_map/cotangent_spread/ppermute | solution.py:56
  35.8 2.5 %collective-permute-done.5 = bf16[128,2048]{1,0:T(8,128)(2,1)} collective-permute-done((bf16[128,2048]{1,0:T(8,128)(2,1)S(1)}, bf16[128,2048]{1,0:T(8,128)(2,1)}, u32[]{:S(2)}, u32[]{:S(2)}) %collective-permute-start.5) | collective-permute-done | bytes 524320 | tf_op jit(solution)/shard_map/hidden_first_down1/ppermute | solution.py:27
  42.3 10.3 %collective-permute-start.8 = (bf16[2,128,1536]{2,1,0:T(8,128)(2,1)}, bf16[2,128,1536]{2,1,0:T(8,128)(2,1)S(1)}, u32[]{:S(2)}, u32[]{:S(2)}) collective-permute-start(bf16[2,128,1536]{2,1,0:T(8,128)(2,1)} %get-tuple-element.81), channel_id=1, source_target_pairs={{0,8},{4,12},{8,16},{12,20},{16,24},{20,28},{1,9},{5,13},{9,17},{1... | collective-permute-start | bytes 2359304 | tf_op jit(solution)/shard_map/hidden_last_up1/ppermute | solution.py:27
  58.2 4.3 %collective-permute-done.20 = bf16[128,2048]{1,0:T(8,128)(2,1)} collective-permute-done((bf16[128,2048]{1,0:T(8,128)(2,1)}, bf16[128,2048]{1,0:T(8,128)(2,1)}, u32[]{:S(2)}, u32[]{:S(2)}) %collective-permute-start.20) | collective-permute-done | bytes 524320 | tf_op jit(solution)/shard_map/hidden_first_down2/ppermute | solution.py:27
  63.6 5.9 %collective-permute-done.8 = bf16[2,128,1536]{2,1,0:T(8,128)(2,1)S(1)} collective-permute-done((bf16[2,128,1536]{2,1,0:T(8,128)(2,1)}, bf16[2,128,1536]{2,1,0:T(8,128)(2,1)S(1)}, u32[]{:S(2)}, u32[]{:S(2)}) %collective-permute-start.8) | collective-permute-done | bytes 786464 | tf_op jit(solution)/shard_map/hidden_last_up1/ppermute | solution.py:27
  69.5 8.7 %collective-permute-done.9 = bf16[2,128,1536]{2,1,0:T(8,128)(2,1)S(1)} collective-permute-done((bf16[2,128,1536]{2,1,0:T(8,128)(2,1)}, bf16[2,128,1536]{2,1,0:T(8,128)(2,1)S(1)}, u32[]{:S(2)}, u32[]{:S(2)}) %collective-permute-start.9) | collective-permute-done | bytes 786464 | tf_op jit(solution)/shard_map/hidden_last_down1/ppermute | solution.py:27
  85.6 5.2 %collective-permute-start.24 = (f16[2,128,1536]{2,1,0:T(8,128)(2,1)S(1)}, f16[2,128,1536]{2,1,0:T(8,128)(2,1)S(1)}, u32[]{:S(2)}, u32[]{:S(2)}) collective-permute-start(f16[2,128,1536]{2,1,0:T(8,128)(2,1)S(1)} %get-tuple-element.46), channel_id=1, source_target_pairs={{0,8},{4,12},{1,9},{5,13},{2,10},{6,14},{3,11},{7,15}} | collective-permute-start | bytes 2359304 | tf_op jit(solution)/shard_map/dhid_last_up1/ppermute | solution.py:27
  92.9 6.8 %collective-permute-done.12 = bf16[2,128,1536]{2,1,0:T(8,128)(2,1)S(1)} collective-permute-done((bf16[2,128,1536]{2,1,0:T(8,128)(2,1)S(1)}, bf16[2,128,1536]{2,1,0:T(8,128)(2,1)S(1)}, u32[]{:S(2)}, u32[]{:S(2)}) %collective-permute-start.12) | collective-permute-done | bytes 786464 | tf_op jit(solution)/shard_map/hidden_last_down2/ppermute | solution.py:27
  99.8 4.9 %collective-permute-done.7 = bf16[2048,512]{1,0:T(8,128)(2,1)S(1)} collective-permute-done((bf16[2048,512]{1,0:T(8,128)(2,1)S(1)}, bf16[2048,512]{1,0:T(8,128)(2,1)S(1)}, u32[]{:S(2)}, u32[]{:S(2)}) %collective-permute-start.7) | collective-permute-done | bytes 2097184 | tf_op jit(solution)/shard_map/weight_side/ppermute | solution.py:31
  106.2 5.3 %collective-permute-start.10 = (f16[128,2048]{1,0:T(8,128)(2,1)S(1)}, f16[128,2048]{1,0:T(8,128)(2,1)S(1)}, u32[]{:S(2)}, u32[]{:S(2)}) collective-permute-start(f16[128,2048]{1,0:T(8,128)(2,1)S(1)} %get-tuple-element.32), channel_id=1, source_target_pairs={{0,8},{4,12},{1,9},{5,13},{2,10},{6,14},{3,11},{7,15}} | collective-permute-start | bytes 1572872 | tf_op jit(solution)/shard_map/dhid_first_up1/ppermute | solution.py:27
  116.1 7.7 %collective-permute-done.10 = f16[128,2048]{1,0:T(8,128)(2,1)S(1)} collective-permute-done((f16[128,2048]{1,0:T(8,128)(2,1)S(1)}, f16[128,2048]{1,0:T(8,128)(2,1)S(1)}, u32[]{:S(2)}, u32[]{:S(2)}) %collective-permute-start.10) | collective-permute-done | bytes 524320 | tf_op jit(solution)/shard_map/dhid_first_up1/ppermute | solution.py:27
  128.0 8.9 %collective-permute-done.21 = bf16[1,128,2048]{2,1,0:T(8,128)(2,1)S(1)} collective-permute-done((bf16[1,128,2048]{2,1,0:T(8,128)(2,1)S(1)}, bf16[1,128,2048]{2,1,0:T(8,128)(2,1)S(1)}, u32[]{:S(2)}, u32[]{:S(2)}) %collective-permute-start.21) | collective-permute-done | bytes 524320 | tf_op jit(solution)/shard_map/hidden_first_side/ppermute | solution.py:31
  145.0 5.7 %collective-permute-done.15 = f16[128,2048]{1,0:T(8,128)(2,1)S(1)} collective-permute-done((f16[128,2048]{1,0:T(8,128)(2,1)S(1)}, f16[128,2048]{1,0:T(8,128)(2,1)S(1)}, u32[]{:S(2)}, u32[]{:S(2)}) %collective-permute-start.15) | collective-permute-done | bytes 524320 | tf_op jit(solution)/shard_map/dhid_first_up2/ppermute | solution.py:27
  152.0 6.4 %collective-permute-start.30 = (f16[2,128,1536]{2,1,0:T(8,128)(2,1)S(1)}, f16[2,128,1536]{2,1,0:T(8,128)(2,1)S(1)}, u32[]{:S(2)}, u32[]{:S(2)}) collective-permute-start(f16[2,128,1536]{2,1,0:T(8,128)(2,1)S(1)} %get-tuple-element.52), channel_id=1, source_target_pairs={{0,8},{4,12},{8,16},{12,20},{16,24},{20,28},{1,9},{5,13},{9,17},{1... | collective-permute-start | bytes 2359304 | tf_op jit(solution)/shard_map/dhid_last_up3/ppermute | solution.py:27
  159.8 4.9 %collective-permute-done.17 = bf16[2,128,1536]{2,1,0:T(8,128)(2,1)S(1)} collective-permute-done((bf16[2,128,1536]{2,1,0:T(8,128)(2,1)S(1)}, bf16[2,128,1536]{2,1,0:T(8,128)(2,1)S(1)}, u32[]{:S(2)}, u32[]{:S(2)}) %collective-permute-start.17) | collective-permute-done | bytes 786464 | tf_op jit(solution)/shard_map/hidden_last_down3/ppermute | solution.py:27
  165.9 5.5 %collective-permute-start.22 = (f16[128,2048]{1,0:T(8,128)(2,1)}, f16[128,2048]{1,0:T(8,128)(2,1)}, u32[]{:S(2)}, u32[]{:S(2)}) collective-permute-start(f16[128,2048]{1,0:T(8,128)(2,1)} %get-tuple-element.44), channel_id=1, source_target_pairs={{0,8},{4,12},{8,16},{12,20},{16,24},{20,28},{1,9},{5,13},{9,17},{1... | collective-permute-start | bytes 1572872 | tf_op jit(solution)/shard_map/dhid_first_up3/ppermute | solution.py:27
  171.7 1.9 convolution_bitcast_fusion
  173.5 8.0 %collective-permute-done.31 = f16[2,128,1536]{2,1,0:T(8,128)(2,1)S(1)} collective-permute-done((f16[2,128,1536]{2,1,0:T(8,128)(2,1)S(1)}, f16[2,128,1536]{2,1,0:T(8,128)(2,1)S(1)}, u32[]{:S(2)}, u32[]{:S(2)}) %collective-permute-start.31) | collective-permute-done | bytes 786464 | tf_op jit(solution)/shard_map/dhid_last_down3/ppermute | solution.py:27
  183.7 2.4 %fusion.8 = f32[2048,512]{1,0:T(8,128)S(1)} fusion(bf16[1,2,128,2048]{3,2,1,0:T(8,128)(2,1)S(1)} %get-tuple-element.85, bf16[1,2,128,2048]{3,2,1,0:T(8,128)(2,1)S(1)} %maximum_bitcast_fusion.1, bf16[1,2,128,2048]{3,2,1,0:T(8,128)(2,1)S(1)} %get-tuple-element.84, bf16[1,2,128,2048]{3,2,1,0:T(8,128)(2,1)S(1)} %maximum_bitcast_fusion, ...), kind=kOutput, calls=%fused_computation.12 | convolution fusion | flops 2154299392 | bytes 9437184 | tf_op jit(solution)/shard_map/kstc,kstf->cf/dot_general | solution.py:143
  186.2 4.0 %maximum_multiply_fusion = f32[3584,512]{1,0:T(8,128)} fusion(f32[1536,512]{1,0:T(8,128)S(1)} %convolution_bitcast_fusion, f32[2048,512]{1,0:T(8,128)S(1)} %fusion.8), kind=kLoop, calls=%fused_computation | loop fusion | flops 3670016 | bytes 14680064 | tf_op jit(solution)/shard_map/mul | solution.py:145
  192.2 2.2 %multiply_convert_fusion = (bf16[128,3584]{1,0:T(8,128)(2,1)}, bf16[128,3584]{1,0:T(8,128)(2,1)}) fusion(f32[128,1536]{1,0:T(8,128)S(1)} %fusion.40, f32[128,2048]{1,0:T(8,128)S(1)} %fusion.37, bf16[128,3584]{1,0:T(8,128)(2,1)S(1)} %copy-done.1, bf16[128,3584]{1,0:T(8,128)(2,1)S(1)} %copy-done.2), kind=kLoop, calls=%fused_computation.37 | loop fusion | flops 7798784 | bytes 5505024 | tf_op jit(solution)/shard_map/convert_element_type | solution.py:136
  (95 shorter events, 52.4 us)
Async XLA Ops:
  3.4 30.4 %collective-permute-start.1 = (bf16[128,1024]{1,0:T(8,128)(2,1)S(1)}, bf16[128,1024]{1,0:T(8,128)(2,1)S(1)}, u32[]{:S(2)}, u32[]{:S(2)}) collective-permute-start(bf16[128,1024]{1,0:T(8,128)(2,1)S(1)} %copy-done.4), channel_id=1, source_target_pairs={{0,2},{1,10},{2,18},{3,26},{4,6},{5,14},{6,22},{7,30},{8,3},{9,11}... | collective-permute-start | bytes 786440 | tf_op jit(solution)/shard_map/cotangent_spread/ppermute | solution.py:56
  10.3 25.5 %collective-permute-start.4 = (bf16[128,2048]{1,0:T(8,128)(2,1)S(1)}, bf16[128,2048]{1,0:T(8,128)(2,1)}, u32[]{:S(2)}, u32[]{:S(2)}) collective-permute-start(bf16[128,2048]{1,0:T(8,128)(2,1)S(1)} %get-tuple-element.77), channel_id=1, source_target_pairs={{0,8},{4,12},{8,16},{12,20},{16,24},{20,28},{1,9},{5,13},{9,17},{1... | collective-permute-start | bytes 1572872 | tf_op jit(solution)/shard_map/hidden_first_up1/ppermute | solution.py:27
  15.2 23.1 %collective-permute-start.5 = (bf16[128,2048]{1,0:T(8,128)(2,1)S(1)}, bf16[128,2048]{1,0:T(8,128)(2,1)}, u32[]{:S(2)}, u32[]{:S(2)}) collective-permute-start(bf16[128,2048]{1,0:T(8,128)(2,1)S(1)} %get-tuple-element.77), channel_id=1, source_target_pairs={{8,0},{12,4},{16,8},{20,12},{24,16},{28,20},{9,1},{13,5},{17,9},{2... | collective-permute-start | bytes 1572872 | tf_op jit(solution)/shard_map/hidden_first_down1/ppermute | solution.py:27
  16.5 17.7 %collective-permute-start.2 = (bf16[128,1536]{1,0:T(8,128)(2,1)S(1)}, bf16[128,1536]{1,0:T(8,128)(2,1)S(1)}, u32[]{:S(2)}, u32[]{:S(2)}) collective-permute-start(bf16[128,1536]{1,0:T(8,128)(2,1)S(1)} %get-tuple-element.79), channel_id=1, source_target_pairs={{0,4},{4,0},{8,12},{12,8},{16,20},{20,16},{24,28},{28,24},{1,5},{5... | collective-permute-start | bytes 1179656 | tf_op jit(solution)/shard_map/hidden_last_side/ppermute | solution.py:31
  34.2 19.7 %collective-permute-start.3 = (bf16[2,128,512]{2,1,0:T(8,128)(2,1)S(1)}, bf16[2,128,512]{2,1,0:T(8,128)(2,1)S(1)}, u32[]{:S(2)}, u32[]{:S(2)}) collective-permute-start(bf16[2,128,512]{2,1,0:T(8,128)(2,1)S(1)} %get-tuple-element.30), channel_id=1, source_target_pairs={{0,4},{4,0},{8,12},{12,8},{16,20},{20,16},{24,28},{28,24},{1,5},{5... | collective-permute-start | bytes 786440 | tf_op jit(solution)/shard_map/cotangent_side/ppermute | solution.py:31
  38.3 18.3 %collective-permute-start.19 = (bf16[128,2048]{1,0:T(8,128)(2,1)}, bf16[128,2048]{1,0:T(8,128)(2,1)}, u32[]{:S(2)}, u32[]{:S(2)}) collective-permute-start(bf16[128,2048]{1,0:T(8,128)(2,1)} %collective-permute-done.4), channel_id=1, source_target_pairs={{8,16},{12,20},{16,24},{20,28},{9,17},{13,21},{17,25},{21,29},{10,... | collective-permute-start | bytes 1572872 | tf_op jit(solution)/shard_map/hidden_first_up2/ppermute | solution.py:27
  39.7 22.7 %collective-permute-start.20 = (bf16[128,2048]{1,0:T(8,128)(2,1)}, bf16[128,2048]{1,0:T(8,128)(2,1)}, u32[]{:S(2)}, u32[]{:S(2)}) collective-permute-start(bf16[128,2048]{1,0:T(8,128)(2,1)} %collective-permute-done.5), channel_id=1, source_target_pairs={{8,0},{12,4},{16,8},{20,12},{9,1},{13,5},{17,9},{21,13},{10,2},{14... | collective-permute-start | bytes 1572872 | tf_op jit(solution)/shard_map/hidden_first_down2/ppermute | solution.py:27
  42.3 27.2 %collective-permute-start.8 = (bf16[2,128,1536]{2,1,0:T(8,128)(2,1)}, bf16[2,128,1536]{2,1,0:T(8,128)(2,1)S(1)}, u32[]{:S(2)}, u32[]{:S(2)}) collective-permute-start(bf16[2,128,1536]{2,1,0:T(8,128)(2,1)} %get-tuple-element.81), channel_id=1, source_target_pairs={{0,8},{4,12},{8,16},{12,20},{16,24},{20,28},{1,9},{5,13},{9,17},{1... | collective-permute-start | bytes 2359304 | tf_op jit(solution)/shard_map/hidden_last_up1/ppermute | solution.py:27
  52.6 25.6 %collective-permute-start.9 = (bf16[2,128,1536]{2,1,0:T(8,128)(2,1)}, bf16[2,128,1536]{2,1,0:T(8,128)(2,1)S(1)}, u32[]{:S(2)}, u32[]{:S(2)}) collective-permute-start(bf16[2,128,1536]{2,1,0:T(8,128)(2,1)} %get-tuple-element.81), channel_id=1, source_target_pairs={{8,0},{12,4},{16,8},{20,12},{24,16},{28,20},{9,1},{13,5},{17,9},{2... | collective-permute-start | bytes 2359304 | tf_op jit(solution)/shard_map/hidden_last_down1/ppermute | solution.py:27
  54.9 25.4 %collective-permute-start.6 = (bf16[3,2,128,512]{3,2,1,0:T(8,128)(2,1)}, bf16[3,2,128,512]{3,2,1,0:T(8,128)(2,1)}, u32[]{:S(2)}, u32[]{:S(2)}) collective-permute-start(bf16[3,2,128,512]{3,2,1,0:T(8,128)(2,1)} %pad_maximum_fusion.3), channel_id=1, source_target_pairs={{0,1},{1,0},{2,3},{3,2},{4,5},{5,4},{6,7},{7,6},{8,9},{9,8},{10,11... | collective-permute-start | bytes 2359304 | tf_op jit(solution)/shard_map/cotangent_core/ppermute | solution.py:70
  56.6 48.1 %collective-permute-start.7 = (bf16[2048,512]{1,0:T(8,128)(2,1)S(1)}, bf16[2048,512]{1,0:T(8,128)(2,1)S(1)}, u32[]{:S(2)}, u32[]{:S(2)}) collective-permute-start(bf16[2048,512]{1,0:T(8,128)(2,1)S(1)} %slice.70), channel_id=1, source_target_pairs={{0,4},{4,0},{8,12},{12,8},{16,20},{20,16},{24,28},{28,24},{1,5},{5... | collective-permute-start | bytes 6291464 | tf_op jit(solution)/shard_map/weight_side/ppermute | solution.py:31
  78.9 20.8 %collective-permute-start.12 = (bf16[2,128,1536]{2,1,0:T(8,128)(2,1)S(1)}, bf16[2,128,1536]{2,1,0:T(8,128)(2,1)S(1)}, u32[]{:S(2)}, u32[]{:S(2)}) collective-permute-start(bf16[2,128,1536]{2,1,0:T(8,128)(2,1)S(1)} %collective-permute-done.9), channel_id=1, source_target_pairs={{8,0},{12,4},{16,8},{20,12},{9,1},{13,5},{17,9},{21,13},{10,2},{14... | collective-permute-start | bytes 2359304 | tf_op jit(solution)/shard_map/hidden_last_down2/ppermute | solution.py:27
  85.6 28.2 %collective-permute-start.24 = (f16[2,128,1536]{2,1,0:T(8,128)(2,1)S(1)}, f16[2,128,1536]{2,1,0:T(8,128)(2,1)S(1)}, u32[]{:S(2)}, u32[]{:S(2)}) collective-permute-start(f16[2,128,1536]{2,1,0:T(8,128)(2,1)S(1)} %get-tuple-element.46), channel_id=1, source_target_pairs={{0,8},{4,12},{1,9},{5,13},{2,10},{6,14},{3,11},{7,15}} | collective-permute-start | bytes 2359304 | tf_op jit(solution)/shard_map/dhid_last_up1/ppermute | solution.py:27
  90.8 23.5 %collective-permute-start.25 = (f16[2,128,1536]{2,1,0:T(8,128)(2,1)S(1)}, f16[2,128,1536]{2,1,0:T(8,128)(2,1)S(1)}, u32[]{:S(2)}, u32[]{:S(2)}) collective-permute-start(f16[2,128,1536]{2,1,0:T(8,128)(2,1)S(1)} %get-tuple-element.47), channel_id=1, source_target_pairs={{24,16},{28,20},{25,17},{29,21},{26,18},{30,22},{27,19},{31,23}} | collective-permute-start | bytes 2359304 | tf_op jit(solution)/shard_map/dhid_last_down1/ppermute | solution.py:27
  113.9 23.0 %collective-permute-start.21 = (bf16[1,128,2048]{2,1,0:T(8,128)(2,1)S(1)}, bf16[1,128,2048]{2,1,0:T(8,128)(2,1)S(1)}, u32[]{:S(2)}, u32[]{:S(2)}) collective-permute-start(bf16[1,128,2048]{2,1,0:T(8,128)(2,1)S(1)} %select_bitcast_fusion.7), channel_id=1, source_target_pairs={{0,4},{4,0},{8,12},{12,8},{16,20},{20,16},{24,28},{28,24},{1,5},{5... | collective-permute-start | bytes 1572872 | tf_op jit(solution)/shard_map/hidden_first_side/ppermute | solution.py:31
  114.8 26.7 %collective-permute-start.26 = (f16[2,128,1536]{2,1,0:T(8,128)(2,1)S(1)}, f16[2,128,1536]{2,1,0:T(8,128)(2,1)S(1)}, u32[]{:S(2)}, u32[]{:S(2)}) collective-permute-start(f16[2,128,1536]{2,1,0:T(8,128)(2,1)S(1)} %get-tuple-element.48), channel_id=1, source_target_pairs={{0,8},{4,12},{8,16},{12,20},{1,9},{5,13},{9,17},{13,21},{2,10},{6,... | collective-permute-start | bytes 2359304 | tf_op jit(solution)/shard_map/dhid_last_up2/ppermute | solution.py:27
  123.9 19.0 %collective-permute-start.29 = (f16[2,128,1536]{2,1,0:T(8,128)(2,1)S(1)}, f16[2,128,1536]{2,1,0:T(8,128)(2,1)S(1)}, u32[]{:S(2)}, u32[]{:S(2)}) collective-permute-start(f16[2,128,1536]{2,1,0:T(8,128)(2,1)S(1)} %get-tuple-element.51), channel_id=1, source_target_pairs={{16,8},{20,12},{24,16},{28,20},{17,9},{21,13},{25,17},{29,21},{18,... | collective-permute-start | bytes 2359304 | tf_op jit(solution)/shard_map/dhid_last_down2/ppermute | solution.py:27
  139.6 20.2 %collective-permute-start.16 = (bf16[2,128,1536]{2,1,0:T(8,128)(2,1)S(1)}, bf16[2,128,1536]{2,1,0:T(8,128)(2,1)S(1)}, u32[]{:S(2)}, u32[]{:S(2)}) collective-permute-start(bf16[2,128,1536]{2,1,0:T(8,128)(2,1)S(1)} %collective-permute-done.11), channel_id=1, source_target_pairs={{16,24},{20,28},{17,25},{21,29},{18,26},{22,30},{19,27},{23,31}} | collective-permute-start | bytes 2359304 | tf_op jit(solution)/shard_map/hidden_last_up3/ppermute | solution.py:27
  141.5 23.1 %collective-permute-start.17 = (bf16[2,128,1536]{2,1,0:T(8,128)(2,1)S(1)}, bf16[2,128,1536]{2,1,0:T(8,128)(2,1)S(1)}, u32[]{:S(2)}, u32[]{:S(2)}) collective-permute-start(bf16[2,128,1536]{2,1,0:T(8,128)(2,1)S(1)} %collective-permute-done.12), channel_id=1, source_target_pairs={{8,0},{12,4},{9,1},{13,5},{10,2},{14,6},{11,3},{15,7}} | collective-permute-start | bytes 2359304 | tf_op jit(solution)/shard_map/hidden_last_down3/ppermute | solution.py:27
  142.8 40.6 %collective-permute-start.33 = (bf16[2,128,2048]{2,1,0:T(8,128)(2,1)S(1)}, bf16[2,128,2048]{2,1,0:T(8,128)(2,1)S(1)}, u32[]{:S(2)}, u32[]{:S(2)}) collective-permute-start(bf16[2,128,2048]{2,1,0:T(8,128)(2,1)S(1)} %pad_maximum_fusion), channel_id=1, source_target_pairs={{0,4},{4,0},{8,12},{12,8},{16,20},{20,16},{24,28},{28,24},{1,5},{5... | collective-permute-start | bytes 3145736 | tf_op jit(solution)/shard_map/hidden_first_side/ppermute | solution.py:31
  150.7 30.8 %collective-permute-start.31 = (f16[2,128,1536]{2,1,0:T(8,128)(2,1)S(1)}, f16[2,128,1536]{2,1,0:T(8,128)(2,1)S(1)}, u32[]{:S(2)}, u32[]{:S(2)}) collective-permute-start(f16[2,128,1536]{2,1,0:T(8,128)(2,1)S(1)} %get-tuple-element.53), channel_id=1, source_target_pairs={{8,0},{12,4},{16,8},{20,12},{24,16},{28,20},{9,1},{13,5},{17,9},{2... | collective-permute-start | bytes 2359304 | tf_op jit(solution)/shard_map/dhid_last_down3/ppermute | solution.py:27
  152.0 29.5 %collective-permute-start.30 = (f16[2,128,1536]{2,1,0:T(8,128)(2,1)S(1)}, f16[2,128,1536]{2,1,0:T(8,128)(2,1)S(1)}, u32[]{:S(2)}, u32[]{:S(2)}) collective-permute-start(f16[2,128,1536]{2,1,0:T(8,128)(2,1)S(1)} %get-tuple-element.52), channel_id=1, source_target_pairs={{0,8},{4,12},{8,16},{12,20},{16,24},{20,28},{1,9},{5,13},{9,17},{1... | collective-permute-start | bytes 2359304 | tf_op jit(solution)/shard_map/dhid_last_up3/ppermute | solution.py:27
  164.6 26.0 %collective-permute-start.23 = (f16[128,2048]{1,0:T(8,128)(2,1)}, f16[128,2048]{1,0:T(8,128)(2,1)}, u32[]{:S(2)}, u32[]{:S(2)}) collective-permute-start(f16[128,2048]{1,0:T(8,128)(2,1)} %get-tuple-element.45), channel_id=1, source_target_pairs={{8,0},{12,4},{16,8},{20,12},{24,16},{28,20},{9,1},{13,5},{17,9},{2... | collective-permute-start | bytes 1572872 | tf_op jit(solution)/shard_map/dhid_first_down3/ppermute | solution.py:27
  165.9 24.7 %collective-permute-start.22 = (f16[128,2048]{1,0:T(8,128)(2,1)}, f16[128,2048]{1,0:T(8,128)(2,1)}, u32[]{:S(2)}, u32[]{:S(2)}) collective-permute-start(f16[128,2048]{1,0:T(8,128)(2,1)} %get-tuple-element.44), channel_id=1, source_target_pairs={{0,8},{4,12},{8,16},{12,20},{16,24},{20,28},{1,9},{5,13},{9,17},{1... | collective-permute-start | bytes 1572872 | tf_op jit(solution)/shard_map/dhid_first_up3/ppermute | solution.py:27
  (15 other events, 153.6 us)

commit v2 on v1

v2 whole, which is shorter than its diff:
```python
import jax
import jax.numpy as jnp
from jax import lax
from jax.sharding import PartitionSpec as P

WIRE = jnp.float16
WIRE_SCALE = 16.0


def after(value, *others):
    return lax.optimization_barrier((value,) + others)[0]


def together(*values):
    return list(lax.optimization_barrier(values))


def shards(cotangent, gate_pre, up_pre, down_weight):
    dp, tensor = lax.axis_size("dp"), lax.axis_size("tensor")
    line = dp // 2
    tokens, features = cotangent.shape
    hidden_units, half = down_weight.shape
    assert features == 2 * half and line == tensor and line % 2 == 0
    position, side = lax.axis_index("dp") // 2, lax.axis_index("dp") % 2
    shard = lax.axis_index("tensor")
    columns = hidden_units * 4 // 7

    def along(name, value, step, first, last):
        pairs = [(2 * at + s, 2 * (at + step) + s) for at in range(first, last + 1) for s in (0, 1)]
        with jax.named_scope(name):
            return lax.ppermute(value, "dp", pairs)

    def across(name, value):
        with jax.named_scope(name):
            return lax.ppermute(value, "dp", [(at, at ^ 1) for at in range(dp)])

    gate_vals = gate_pre.astype(jnp.float32)
    up_vals = up_pre.astype(jnp.float32)
    sigma = jax.nn.sigmoid(gate_vals)
    act_vals = gate_vals * sigma
    hidden = (act_vals * up_vals).astype(jnp.bfloat16)
    first, last = hidden[:, :columns], hidden[:, columns:]
    weight_first, weight_last = down_weight[:columns], down_weight[columns:]

    middle = columns // 4
    weight_other = [across("weight_side", weight_first[:middle])]

    share = 2 * tokens // tensor
    arrived = []
    for turn in range(tensor // 2):
        piece = lax.dynamic_slice_in_dim(cotangent, (position + 2 * turn) % tensor // 2 * share, share, 0)
        pairs = [
            ((2 * at + s) * tensor + owner, (2 * owner + s) * tensor + (at + 2 * turn) % tensor)
            for at in range(line)
            for s in (0, 1)
            for owner in range(tensor)
        ]
        with jax.named_scope("cotangent_spread"):
            arrived.append(lax.ppermute(piece, ("dp", "tensor"), pairs))
    odd = (position - shard) % 2
    turned = ((shard - position + odd) % line) // 2
    row = lax.dynamic_slice_in_dim(jnp.stack(arrived + arrived), turned, line // 2, 0)
    mine = jnp.where(side == 0, row[..., :half], row[..., half:])
    other = jnp.where(side == 0, row[..., half:], row[..., :half])

    last_other = across("hidden_last_side", last)
    first_sent = after(first, *arrived)
    first_up = along("hidden_first_up1", first_sent, 1, 0, line - 2)
    first_down = along("hidden_first_down1", first_sent, -1, 1, line - 1)
    theirs = across("cotangent_side", after(other, last_other))
    first_up, first_down = together(first_up, first_down)

    both_last = jnp.stack([last, last_other])
    last_up = along("hidden_last_up1", both_last, 1, 0, line - 2)
    last_down = along("hidden_last_down1", both_last, -1, 1, line - 1)
    weight_other.append(across("weight_side", after(weight_first[middle:], theirs)))
    last_up, last_down = together(last_up, last_down)

    own = after(jnp.stack([mine, other, theirs])[:, :, None], weight_other[0])
    bit = tensor // 2
    while bit > 1:
        with jax.named_scope("cotangent_shares"):
            swapped = lax.ppermute(own, "tensor", [(at, at ^ bit) for at in range(tensor)])
        low = (shard // bit) % 2 == 0
        own = jnp.stack([jnp.where(low, own, swapped), jnp.where(low, swapped, own)], axis=3)
        own = own.reshape(3, line // 2, -1, share, half)
        bit //= 2
    own = after(own, first_up)
    with jax.named_scope("cotangent_core"):
        swapped = lax.ppermute(own, "tensor", [(at, at ^ 1) for at in range(tensor)])
    whole = jnp.stack([jnp.where(odd == 0, own, swapped), jnp.where(odd == 0, swapped, own)], axis=2)
    mine, other, theirs = whole.reshape(3, line, tokens, half)
    features_of_all = jnp.stack([mine, theirs], axis=1)

    def product(left, right):
        return jnp.einsum("...f,hf->...h", left, right, preferred_element_type=jnp.float32)

    parts = {"last": product(features_of_all, weight_last) * WIRE_SCALE}

    rising = {"first": [first, first_up], "last": [both_last, last_up]}
    falling = {"first": [first, first_down], "last": [both_last, last_down]}
    up_sum = {"first": 0.0, "last": 0.0}
    down_sum = {"first": 0.0, "last": 0.0}
    sides = {}

    def gather_step(which, step, waits):
        up = along(f"hidden_{which}_up{step}", after(rising[which][-1], *waits), 1, step - 1, line - 2)
        down = along(f"hidden_{which}_down{step}", after(falling[which][-1], *waits), -1, 1, line - step)
        return [up, down]

    def sum_step(which, step, waits):
        message = after((parts[which][step] + up_sum[which]).astype(WIRE), *waits)
        up = along(f"dhid_{which}_up{step}", message, 1, 0, step - 1)
        message = after((parts[which][line - step] + down_sum[which]).astype(WIRE), *waits)
        down = along(f"dhid_{which}_down{step}", message, -1, line - step, line - 1)
        return [up, down]

    def gathered(which, k):
        if k == 0:
            return rising[which][0]
        return jnp.where(position >= k, rising[which][k], falling[which][line - k])

    def exchange(k, waits):
        block = gathered("first", k)
        return block, across("hidden_first_side", after(block, *waits))

    rounds = [first_up, last_up]
    waiting, sent = [0], []
    for step in range(1, line):
        for which, summed in (("first", "last"), ("last", "first")):
            begin = step == 1 and which == "first"
            if step == 1 and summed == "first":
                weight_other = jnp.concatenate(weight_other)
                parts["first"] = (product(mine, weight_first) + product(other, weight_other)) * WIRE_SCALE
            moved = sum_step(summed, step, rounds[-2:-1])
            if step + 1 < line:
                moved += gather_step(which, step + 1, rounds[-2:-1])
            ahead = []
            if not begin:
                ahead = [(k,) + exchange(k, rounds[-2:-1]) for k in waiting]
                waiting = []
            if begin:
                moved.append(weight_other[1])
            moved = together(*moved, *[swapped for _, _, swapped in sent])
            for k, block, _ in reversed(sent):
                sides[k] = block, moved.pop()
            if begin:
                weight_other[1] = moved.pop()
            if step + 1 < line:
                falling[which].append(moved.pop())
                rising[which].append(moved.pop())
                if which == "first":
                    waiting = waiting + [k for k in range(1, line) if max(k, line - k) == step + 1]
            sent = ahead
            up_sum[summed], down_sum[summed] = (value.astype(jnp.float32) for value in moved)
            rounds.append(moved[0])
    for k, *blocks in sent:
        sides[k] = blocks

    def total(which):
        return parts[which][0] + up_sum[which] + down_sum[which]

    pair = total("last")
    dhid_last = pair[0] + across("dhid_last_side", pair[1].astype(WIRE)).astype(jnp.float32)
    dhid = jnp.concatenate([total("first"), dhid_last], axis=1) * (1.0 / WIRE_SCALE)

    grad_up = (dhid * act_vals).astype(jnp.bfloat16)
    grad_gate = (dhid * up_vals * sigma * (1.0 + gate_vals * (1.0 - sigma))).astype(jnp.bfloat16)

    hidden_first = jnp.stack([jnp.stack(sides[k]) for k in range(line)])
    hidden_last = jnp.stack([gathered("last", k) for k in range(line)])

    def weight_grad(values):
        summed = jnp.einsum("kstc,kstf->cf", values, features_of_all, preferred_element_type=jnp.float32)
        return summed * (tokens * dp) ** (-0.5)

    grad_down = jnp.zeros(down_weight.shape, jnp.float32)
    grad_down = lax.dynamic_update_slice_in_dim(grad_down, weight_grad(hidden_last), columns, 0)
    grad_down = lax.dynamic_update_slice_in_dim(grad_down, weight_grad(hidden_first), 0, 0)
    return grad_gate, grad_up, grad_down


def solution(mesh):
    in_specs = (P("dp", "tensor"), P("dp", "tensor"), P("dp", "tensor"), P("tensor", "dp"))
    out_specs = (P("dp", "tensor"), P("dp", "tensor"), P("tensor", "dp"))
    return jax.shard_map(shards, mesh=mesh, in_specs=in_specs, out_specs=out_specs, check_vma=False)
```

time: 195 us -> 183 us (0.938)
  waiting for transfers between devices: 85.7 us -> 61.9 us
  matrix products: 8.78 us -> 13.6 us
  local copies, waits for them, and re-layouts: 3.89 us -> 7.7 us
    ppermute x24, waiting for transfers between devices: 55.3 us -> 38.6 us  [along(): return lax.ppermute(value, 'dp', pairs)]
    dot_general x3, matrix products: 4.5 us -> 9.31 us  [product(): jnp.einsum('...f,hf->...h', left, right, preferred_element_type=jnp.float32)]
    ppermute x7 -> x9, waiting for transfers between devices: 14.8 us -> 10.8 us  [across(): return lax.ppermute(value, 'dp', [(at, at ^ 1) for at in range(dp)])]
    mul x1 -> x0, other arithmetic: 3.95 us -> none  [shards(): jnp.concatenate([weight_grad(hidden_first), weight_grad(hidden_last)])]
    dynamic_update_slice x0 -> x1, other arithmetic: none -> 3.91 us  [shards(): lax.dynamic_update_slice_in_dim(grad_down, weight_grad(hidden_first), 0, 0)]
    another operation x6 -> x2, other arithmetic: 3.4 us -> 0.08 us  [the longest x1 0.06 us: shards(): jnp.stack([jnp.where(low, own, swapped), jnp.where(low, swapped, own)], a...]
    ppermute x3 -> x4, waiting for transfers between devices: 15.7 us -> 12.5 us  [the longest x2 6.73 us: shards(): arrived.append(lax.ppermute(piece, ('dp', 'tensor'), pairs))]
    ppermute x24, starting transfers between devices: 57.2 us -> 54.2 us  [along(): return lax.ppermute(value, 'dp', pairs)]
  transfers between devices with their start and end apart: 34 -> 37, of which waited for: 15 -> 15; matrix products, arithmetic and copies ran while one was open for 14% -> 20% of each run, Pallas kernels for 0% -> 0%
where the time goes in v2:
time: 183 us; the launch traced here: 182 us
  starting transfers between devices  75.1 us (41%)
  waiting for transfers between devices  61.9 us (34%)
  other arithmetic  22.1 us (12%)
  matrix products  13.6 us (7%)
  local copies, waits for them, and re-layouts  7.7 us (4%)
    ppermute x24, starting transfers between devices, along(): return lax.ppermute(value, 'dp', pairs)  54.2 us
    ppermute x24, waiting for transfers between devices, along(): return lax.ppermute(value, 'dp', pairs)  38.6 us
    ppermute x9, starting transfers between devices, across(): return lax.ppermute(value, 'dp', [(at, at ^ 1) for at in range(dp)])  12.1 us
    ppermute x9, waiting for transfers between devices, across(): return lax.ppermute(value, 'dp', [(at, at ^ 1) for at in range(dp)])  10.8 us
    dot_general x3, matrix products, product(): jnp.einsum('...f,hf->...h', left, right, preferred_element_type=jnp.float32)  9.31 us
    ppermute x2, starting transfers between devices, shards(): arrived.append(lax.ppermute(piece, ('dp', 'tensor'), pairs))  7.46 us
    ppermute x2, waiting for transfers between devices, shards(): arrived.append(lax.ppermute(piece, ('dp', 'tensor'), pairs))  6.73 us
    ppermute x1, waiting for transfers between devices, shards(): lax.ppermute(own, 'tensor', [(at, at ^ bit) for at in range(tensor)])  5.81 us
  transfers between devices with their start and end apart: 37, of which 15 were waited for; matrix products, arithmetic and copies ran while one was open for 20% of the time, Pallas kernels for 0%

profile of v2, /device:TPU:0, one launch (start us, length us, event | category | flops | bytes accessed | tf_op | source)
XLA Modules:
  0.0 181.8 jit_solution(2088063167661594403)
XLA Ops:
  2.4 6.8 %collective-permute-start.1 = (bf16[64,1024]{1,0:T(8,128)(2,1)S(1)}, bf16[64,1024]{1,0:T(8,128)(2,1)S(1)}, u32[]{:S(2)}, u32[]{:S(2)}) collective-permute-start(bf16[64,1024]{1,0:T(8,128)(2,1)S(1)} %get-tuple-element.148), channel_id=1, source_target_pairs={{0,2},{1,10},{2,18},{3,26},{4,6},{5,14},{6,22},{7,30},{8,3},{9,11}... | collective-permute-start | bytes 393224 | tf_op jit(solution)/shard_map/cotangent_spread/ppermute | solution.py:59
  14.5 6.7 %collective-permute-done.1 = bf16[64,1024]{1,0:T(8,128)(2,1)S(1)} collective-permute-done((bf16[64,1024]{1,0:T(8,128)(2,1)S(1)}, bf16[64,1024]{1,0:T(8,128)(2,1)S(1)}, u32[]{:S(2)}, u32[]{:S(2)}) %collective-permute-start.1) | collective-permute-done | bytes 131104 | tf_op jit(solution)/shard_map/cotangent_spread/ppermute | solution.py:59
  25.1 4.9 %collective-permute-start.6 = (bf16[128,2048]{1,0:T(8,128)(2,1)S(1)}, bf16[128,2048]{1,0:T(8,128)(2,1)}, u32[]{:S(2)}, u32[]{:S(2)}) collective-permute-start(bf16[128,2048]{1,0:T(8,128)(2,1)S(1)} %get-tuple-element.101), channel_id=1, source_target_pairs={{0,8},{4,12},{8,16},{12,20},{16,24},{20,28},{1,9},{5,13},{9,17},{1... | collective-permute-start | bytes 1572872 | tf_op jit(solution)/shard_map/hidden_first_up1/ppermute | solution.py:31
  31.3 4.6 %collective-permute-done.3 = bf16[2,64,512]{2,1,0:T(8,128)(2,1)S(1)} collective-permute-done((bf16[2,64,512]{2,1,0:T(8,128)(2,1)S(1)}, bf16[2,64,512]{2,1,0:T(8,128)(2,1)S(1)}, u32[]{:S(2)}, u32[]{:S(2)}) %collective-permute-start.3) | collective-permute-done | bytes 131104 | tf_op jit(solution)/shard_map/cotangent_side/ppermute | solution.py:35
  37.3 3.9 %collective-permute-done.7 = bf16[128,2048]{1,0:T(8,128)(2,1)} collective-permute-done((bf16[128,2048]{1,0:T(8,128)(2,1)S(1)}, bf16[128,2048]{1,0:T(8,128)(2,1)}, u32[]{:S(2)}, u32[]{:S(2)}) %collective-permute-start.7) | collective-permute-done | bytes 524320 | tf_op jit(solution)/shard_map/hidden_first_down1/ppermute | solution.py:31
  41.2 5.8 %collective-permute-done.5 = bf16[3,2,1,64,512]{4,3,1,0,2:T(8,128)(2,1)S(1)} collective-permute-done((bf16[3,2,1,64,512]{4,3,1,0,2:T(8,128)(2,1)S(1)}, bf16[3,2,1,64,512]{4,3,1,0,2:T(8,128)(2,1)S(1)}, u32[]{:S(2)}, u32[]{:S(2)}) %collective-permute-start.5) | collective-permute-done | bytes 393248 | tf_op jit(solution)/shard_map/cotangent_shares/ppermute | solution.py:83
  50.8 2.2 %collective-permute-start.14 = (bf16[2,128,1536]{2,1,0:T(8,128)(2,1)S(1)}, bf16[2,128,1536]{2,1,0:T(8,128)(2,1)}, u32[]{:S(2)}, u32[]{:S(2)}) collective-permute-start(bf16[2,128,1536]{2,1,0:T(8,128)(2,1)S(1)} %get-tuple-element.143), channel_id=1, source_target_pairs={{0,8},{4,12},{8,16},{12,20},{16,24},{20,28},{1,9},{5,13},{9,17},{1... | collective-permute-start | bytes 2359304 | tf_op jit(solution)/shard_map/hidden_last_up1/ppermute | solution.py:31
  57.3 3.4 %convolution_multiply_fusion = f32[4,2,128,1536]{3,2,1,0:T(8,128)S(1)} fusion(bf16[3584,512]{1,0:T(8,128)(2,1)} %param.7, bf16[4,1,128,512]{3,2,1,0:T(8,128)(2,1)S(1)} %bitcast.137, bf16[4,1,128,512]{3,2,1,0:T(8,128)(2,1)S(1)} %bitcast.131), kind=kOutput, calls=%fused_computation.1 | convolution fusion | flops 1612709888 | bytes 8912896 | tf_op jit(solution)/shard_map/...f,hf->...h/dot_general | solution.py:96
  60.7 2.7 %copy-done = f32[4,2,128,1536]{3,2,1,0:T(8,128)} copy-done((f32[4,2,128,1536]{3,2,1,0:T(8,128)}, f32[4,2,128,1536]{3,2,1,0:T(8,128)S(1)}, u32[]{:S(2)}) %copy-start) | copy-done | bytes 6291480
  64.8 5.4 %collective-permute-start.9 = (f16[2,128,1536]{2,1,0:T(8,128)(2,1)}, f16[2,128,1536]{2,1,0:T(8,128)(2,1)}, u32[]{:S(2)}, u32[]{:S(2)}) collective-permute-start(f16[2,128,1536]{2,1,0:T(8,128)(2,1)} %get-tuple-element.66), channel_id=1, source_target_pairs={{0,8},{4,12},{1,9},{5,13},{2,10},{6,14},{3,11},{7,15}} | collective-permute-start | bytes 2359304 | tf_op jit(solution)/shard_map/dhid_last_up1/ppermute | solution.py:31
  76.2 3.0 %fusion.20 = f32[4,128,2048]{2,1,0:T(8,128)S(1)} fusion(bf16[4,128,512]{2,1,0:T(8,128)(2,1)S(1)} %bitcast.132, bf16[3584,512]{1,0:T(8,128)(2,1)} %param.7), kind=kOutput, calls=%fused_computation.29 | convolution fusion | flops 1073741824 | bytes 6815744 | tf_op jit(solution)/shard_map/...f,hf->...h/dot_general | solution.py:96
  80.9 9.7 %collective-permute-done.12 = bf16[128,2048]{1,0:T(8,128)(2,1)} collective-permute-done((bf16[128,2048]{1,0:T(8,128)(2,1)}, bf16[128,2048]{1,0:T(8,128)(2,1)}, u32[]{:S(2)}, u32[]{:S(2)}) %collective-permute-start.12) | collective-permute-done | bytes 524320 | tf_op jit(solution)/shard_map/hidden_first_down2/ppermute | solution.py:31
  92.9 2.9 %add_multiply_fusion = f32[4,128,2048]{2,1,0:T(8,128)S(1)} fusion(f32[4,128,2048]{2,1,0:T(8,128)S(1)} %fusion.20, bf16[4,128,512]{2,1,0:T(8,128)(2,1)S(1)} %bitcast.136, bf16[1536,512]{1,0:T(8,128)(2,1)} %collective-permute-done.13, bf16[512,512]{1,0:T(8,128)(2,1)S(1)} %copy-done.9), kind=kOutput, calls=%fused_computation.11 | convolution fusion | flops 1080033280 | bytes 11010048 | tf_op jit(solution)/shard_map/...f,hf->...h/dot_general | solution.py:96
  96.0 5.2 %collective-permute-start.16 = (f16[128,2048]{1,0:T(8,128)(2,1)S(1)}, f16[128,2048]{1,0:T(8,128)(2,1)S(1)}, u32[]{:S(2)}, u32[]{:S(2)}) collective-permute-start(f16[128,2048]{1,0:T(8,128)(2,1)S(1)} %get-tuple-element.74), channel_id=1, source_target_pairs={{0,8},{4,12},{1,9},{5,13},{2,10},{6,14},{3,11},{7,15}} | collective-permute-start | bytes 1572872 | tf_op jit(solution)/shard_map/dhid_first_up1/ppermute | solution.py:31
  104.9 6.6 %collective-permute-start.26 = (f16[2,128,1536]{2,1,0:T(8,128)(2,1)S(1)}, f16[2,128,1536]{2,1,0:T(8,128)(2,1)S(1)}, u32[]{:S(2)}, u32[]{:S(2)}) collective-permute-start(f16[2,128,1536]{2,1,0:T(8,128)(2,1)S(1)} %get-tuple-element.94), channel_id=1, source_target_pairs={{0,8},{4,12},{8,16},{12,20},{1,9},{5,13},{9,17},{13,21},{2,10},{6,... | collective-permute-start | bytes 2359304 | tf_op jit(solution)/shard_map/dhid_last_up2/ppermute | solution.py:31
  117.4 4.6 %collective-permute-start.20 = (f16[128,2048]{1,0:T(8,128)(2,1)S(1)}, f16[128,2048]{1,0:T(8,128)(2,1)S(1)}, u32[]{:S(2)}, u32[]{:S(2)}) collective-permute-start(f16[128,2048]{1,0:T(8,128)(2,1)S(1)} %get-tuple-element.80), channel_id=1, source_target_pairs={{0,8},{4,12},{8,16},{12,20},{1,9},{5,13},{9,17},{13,21},{2,10},{6,... | collective-permute-start | bytes 1572872 | tf_op jit(solution)/shard_map/dhid_first_up2/ppermute | solution.py:31
  122.1 6.0 %collective-permute-done.29 = bf16[128,2048]{1,0:T(8,128)(2,1)S(1)} collective-permute-done((bf16[128,2048]{1,0:T(8,128)(2,1)}, bf16[128,2048]{1,0:T(8,128)(2,1)S(1)}, u32[]{:S(2)}, u32[]{:S(2)}) %collective-permute-start.29) | collective-permute-done | bytes 524320 | tf_op jit(solution)/shard_map/hidden_first_down3/ppermute | solution.py:31
  131.8 6.0 %collective-permute-start.32 = (f16[2,128,1536]{2,1,0:T(8,128)(2,1)S(1)}, f16[2,128,1536]{2,1,0:T(8,128)(2,1)S(1)}, u32[]{:S(2)}, u32[]{:S(2)}) collective-permute-start(f16[2,128,1536]{2,1,0:T(8,128)(2,1)S(1)} %get-tuple-element.104), channel_id=1, source_target_pairs={{0,8},{4,12},{8,16},{12,20},{16,24},{20,28},{1,9},{5,13},{9,17},{1... | collective-permute-start | bytes 2359304 | tf_op jit(solution)/shard_map/dhid_last_up3/ppermute | solution.py:31
  144.5 8.2 %collective-permute-done.23 = bf16[2,128,1536]{2,1,0:T(8,128)(2,1)S(1)} collective-permute-done((bf16[2,128,1536]{2,1,0:T(8,128)(2,1)S(1)}, bf16[2,128,1536]{2,1,0:T(8,128)(2,1)S(1)}, u32[]{:S(2)}, u32[]{:S(2)}) %collective-permute-start.23) | collective-permute-done | bytes 786464 | tf_op jit(solution)/shard_map/hidden_last_down3/ppermute | solution.py:31
  160.2 3.8 %collective-permute-done.35 = bf16[128,2048]{1,0:T(8,128)(2,1)S(1)} collective-permute-done((bf16[128,2048]{1,0:T(8,128)(2,1)S(1)}, bf16[128,2048]{1,0:T(8,128)(2,1)S(1)}, u32[]{:S(2)}, u32[]{:S(2)}) %collective-permute-start.35) | collective-permute-done | bytes 524320 | tf_op jit(solution)/shard_map/hidden_first_side/ppermute | solution.py:35
  164.0 5.6 %collective-permute-done.33 = f16[2,128,1536]{2,1,0:T(8,128)(2,1)S(1)} collective-permute-done((f16[2,128,1536]{2,1,0:T(8,128)(2,1)S(1)}, f16[2,128,1536]{2,1,0:T(8,128)(2,1)S(1)}, u32[]{:S(2)}, u32[]{:S(2)}) %collective-permute-start.33) | collective-permute-done | bytes 786464 | tf_op jit(solution)/shard_map/dhid_last_down3/ppermute | solution.py:31
  171.8 2.4 %bitcast_multiply_fusion = f32[2048,512]{1,0:T(8,128)S(1)} fusion(bf16[1,2,128,2048]{3,2,1,0:T(8,128)(2,1)S(1)} %maximum_bitcast_fusion.5, bf16[1,2,128,2048]{3,2,1,0:T(8,128)(2,1)S(1)} %get-tuple-element.155, bf16[1,2,128,2048]{3,2,1,0:T(8,128)(2,1)S(1)} %maximum_bitcast_fusion.3, bf16[1,2,128,2048]{3,2,1,0:T(8,128)(2,1)S(1)} %get-tuple-element.154, ...), kind=kOutput, calls=%fused_computation.10 | convolution fusion | flops 2155347968 | bytes 9437184 | tf_op jit(solution)/shard_map/kstc,kstf->cf/dot_general | solution.py:174
  174.3 3.9 %pad_maximum_fusion = f32[3584,512]{1,0:T(8,128)} fusion(f32[1536,512]{1,0:T(8,128)S(1)} %fusion.8, f32[2048,512]{1,0:T(8,128)S(1)} %bitcast_multiply_fusion), kind=kLoop, calls=%fused_computation | loop fusion | flops 1835008 | bytes 14680064 | tf_op jit(solution)/shard_map/dynamic_update_slice | solution.py:179
  179.6 2.2 %multiply_convert_fusion = (bf16[128,3584]{1,0:T(8,128)(2,1)}, bf16[128,3584]{1,0:T(8,128)(2,1)}) fusion(f32[128,1536]{1,0:T(8,128)S(1)} %fusion.41, f32[128,2048]{1,0:T(8,128)S(1)} %fusion.38, bf16[128,3584]{1,0:T(8,128)(2,1)S(1)} %copy-done.1, bf16[128,3584]{1,0:T(8,128)(2,1)S(1)} %copy-done.2), kind=kLoop, calls=%fused_computation.41 | loop fusion | flops 7798784 | bytes 5505024 | tf_op jit(solution)/shard_map/convert_element_type | solution.py:167
  (116 shorter events, 63.8 us)
Async XLA Ops:
  2.4 18.8 %collective-permute-start.1 = (bf16[64,1024]{1,0:T(8,128)(2,1)S(1)}, bf16[64,1024]{1,0:T(8,128)(2,1)S(1)}, u32[]{:S(2)}, u32[]{:S(2)}) collective-permute-start(bf16[64,1024]{1,0:T(8,128)(2,1)S(1)} %get-tuple-element.148), channel_id=1, source_target_pairs={{0,2},{1,10},{2,18},{3,26},{4,6},{5,14},{6,22},{7,30},{8,3},{9,11}... | collective-permute-start | bytes 393224 | tf_op jit(solution)/shard_map/cotangent_spread/ppermute | solution.py:59
  13.9 22.1 %collective-permute-start.4 = (bf16[512,512]{1,0:T(8,128)(2,1)S(1)}, bf16[512,512]{1,0:T(8,128)(2,1)S(1)}, u32[]{:S(2)}, u32[]{:S(2)}) collective-permute-start(bf16[512,512]{1,0:T(8,128)(2,1)S(1)} %slice.71), channel_id=1, source_target_pairs={{0,4},{4,0},{8,12},{12,8},{16,20},{20,16},{24,28},{28,24},{1,5},{5... | collective-permute-start | bytes 1572872 | tf_op jit(solution)/shard_map/weight_side/ppermute | solution.py:35
  50.8 21.0 %collective-permute-start.14 = (bf16[2,128,1536]{2,1,0:T(8,128)(2,1)S(1)}, bf16[2,128,1536]{2,1,0:T(8,128)(2,1)}, u32[]{:S(2)}, u32[]{:S(2)}) collective-permute-start(bf16[2,128,1536]{2,1,0:T(8,128)(2,1)S(1)} %get-tuple-element.143), channel_id=1, source_target_pairs={{0,8},{4,12},{8,16},{12,20},{16,24},{20,28},{1,9},{5,13},{9,17},{1... | collective-permute-start | bytes 2359304 | tf_op jit(solution)/shard_map/hidden_last_up1/ppermute | solution.py:31
  52.9 21.9 %collective-permute-start.15 = (bf16[2,128,1536]{2,1,0:T(8,128)(2,1)S(1)}, bf16[2,128,1536]{2,1,0:T(8,128)(2,1)}, u32[]{:S(2)}, u32[]{:S(2)}) collective-permute-start(bf16[2,128,1536]{2,1,0:T(8,128)(2,1)S(1)} %get-tuple-element.143), channel_id=1, source_target_pairs={{8,0},{12,4},{16,8},{20,12},{24,16},{28,20},{9,1},{13,5},{17,9},{2... | collective-permute-start | bytes 2359304 | tf_op jit(solution)/shard_map/hidden_last_down1/ppermute | solution.py:31
  54.2 37.4 %collective-permute-start.13 = (bf16[1536,512]{1,0:T(8,128)(2,1)S(1)}, bf16[1536,512]{1,0:T(8,128)(2,1)}, u32[]{:S(2)}, u32[]{:S(2)}) collective-permute-start(bf16[1536,512]{1,0:T(8,128)(2,1)S(1)} %slice.77), channel_id=1, source_target_pairs={{0,4},{4,0},{8,12},{12,8},{16,20},{20,16},{24,28},{28,24},{1,5},{5... | collective-permute-start | bytes 4718600 | tf_op jit(solution)/shard_map/weight_side/ppermute | solution.py:35
  64.8 28.1 %collective-permute-start.9 = (f16[2,128,1536]{2,1,0:T(8,128)(2,1)}, f16[2,128,1536]{2,1,0:T(8,128)(2,1)}, u32[]{:S(2)}, u32[]{:S(2)}) collective-permute-start(f16[2,128,1536]{2,1,0:T(8,128)(2,1)} %get-tuple-element.66), channel_id=1, source_target_pairs={{0,8},{4,12},{1,9},{5,13},{2,10},{6,14},{3,11},{7,15}} | collective-permute-start | bytes 2359304 | tf_op jit(solution)/shard_map/dhid_last_up1/ppermute | solution.py:31
  70.2 22.7 %collective-permute-start.10 = (f16[2,128,1536]{2,1,0:T(8,128)(2,1)}, f16[2,128,1536]{2,1,0:T(8,128)(2,1)}, u32[]{:S(2)}, u32[]{:S(2)}) collective-permute-start(f16[2,128,1536]{2,1,0:T(8,128)(2,1)} %get-tuple-element.67), channel_id=1, source_target_pairs={{24,16},{28,20},{25,17},{29,21},{26,18},{30,22},{27,19},{31,23}} | collective-permute-start | bytes 2359304 | tf_op jit(solution)/shard_map/dhid_last_down1/ppermute | solution.py:31
  74.9 15.7 %collective-permute-start.12 = (bf16[128,2048]{1,0:T(8,128)(2,1)}, bf16[128,2048]{1,0:T(8,128)(2,1)}, u32[]{:S(2)}, u32[]{:S(2)}) collective-permute-start(bf16[128,2048]{1,0:T(8,128)(2,1)} %collective-permute-done.7), channel_id=1, source_target_pairs={{8,0},{12,4},{16,8},{20,12},{9,1},{13,5},{17,9},{21,13},{10,2},{14... | collective-permute-start | bytes 1572872 | tf_op jit(solution)/shard_map/hidden_first_down2/ppermute | solution.py:31
  79.3 36.5 %collective-permute-start.30 = (bf16[128,2048]{1,0:T(8,128)(2,1)S(1)}, bf16[128,2048]{1,0:T(8,128)(2,1)S(1)}, u32[]{:S(2)}, u32[]{:S(2)}) collective-permute-start(bf16[128,2048]{1,0:T(8,128)(2,1)S(1)} %copy-done.5), channel_id=1, source_target_pairs={{0,4},{4,0},{8,12},{12,8},{16,20},{20,16},{24,28},{28,24},{1,5},{5... | collective-permute-start | bytes 1572872 | tf_op jit(solution)/shard_map/hidden_first_side/ppermute | solution.py:35
  90.6 14.3 %collective-permute-start.18 = (bf16[2,128,1536]{2,1,0:T(8,128)(2,1)}, bf16[2,128,1536]{2,1,0:T(8,128)(2,1)S(1)}, u32[]{:S(2)}, u32[]{:S(2)}) collective-permute-start(bf16[2,128,1536]{2,1,0:T(8,128)(2,1)} %collective-permute-done.14), channel_id=1, source_target_pairs={{8,16},{12,20},{16,24},{20,28},{9,17},{13,21},{17,25},{21,29},{10,... | collective-permute-start | bytes 2359304 | tf_op jit(solution)/shard_map/hidden_last_up2/ppermute | solution.py:31
  91.6 21.1 %collective-permute-start.19 = (bf16[2,128,1536]{2,1,0:T(8,128)(2,1)}, bf16[2,128,1536]{2,1,0:T(8,128)(2,1)S(1)}, u32[]{:S(2)}, u32[]{:S(2)}) collective-permute-start(bf16[2,128,1536]{2,1,0:T(8,128)(2,1)} %collective-permute-done.15), channel_id=1, source_target_pairs={{8,0},{12,4},{16,8},{20,12},{9,1},{13,5},{17,9},{21,13},{10,2},{14... | collective-permute-start | bytes 2359304 | tf_op jit(solution)/shard_map/hidden_last_down2/ppermute | solution.py:31
  96.0 17.4 %collective-permute-start.16 = (f16[128,2048]{1,0:T(8,128)(2,1)S(1)}, f16[128,2048]{1,0:T(8,128)(2,1)S(1)}, u32[]{:S(2)}, u32[]{:S(2)}) collective-permute-start(f16[128,2048]{1,0:T(8,128)(2,1)S(1)} %get-tuple-element.74), channel_id=1, source_target_pairs={{0,8},{4,12},{1,9},{5,13},{2,10},{6,14},{3,11},{7,15}} | collective-permute-start | bytes 1572872 | tf_op jit(solution)/shard_map/dhid_first_up1/ppermute | solution.py:31
  104.9 25.0 %collective-permute-start.26 = (f16[2,128,1536]{2,1,0:T(8,128)(2,1)S(1)}, f16[2,128,1536]{2,1,0:T(8,128)(2,1)S(1)}, u32[]{:S(2)}, u32[]{:S(2)}) collective-permute-start(f16[2,128,1536]{2,1,0:T(8,128)(2,1)S(1)} %get-tuple-element.94), channel_id=1, source_target_pairs={{0,8},{4,12},{8,16},{12,20},{1,9},{5,13},{9,17},{13,21},{2,10},{6,... | collective-permute-start | bytes 2359304 | tf_op jit(solution)/shard_map/dhid_last_up2/ppermute | solution.py:31
  112.7 18.5 %collective-permute-start.27 = (f16[2,128,1536]{2,1,0:T(8,128)(2,1)S(1)}, f16[2,128,1536]{2,1,0:T(8,128)(2,1)S(1)}, u32[]{:S(2)}, u32[]{:S(2)}) collective-permute-start(f16[2,128,1536]{2,1,0:T(8,128)(2,1)S(1)} %get-tuple-element.96), channel_id=1, source_target_pairs={{16,8},{20,12},{24,16},{28,20},{17,9},{21,13},{25,17},{29,21},{18,... | collective-permute-start | bytes 2359304 | tf_op jit(solution)/shard_map/dhid_last_down2/ppermute | solution.py:31
  117.4 23.7 %collective-permute-start.20 = (f16[128,2048]{1,0:T(8,128)(2,1)S(1)}, f16[128,2048]{1,0:T(8,128)(2,1)S(1)}, u32[]{:S(2)}, u32[]{:S(2)}) collective-permute-start(f16[128,2048]{1,0:T(8,128)(2,1)S(1)} %get-tuple-element.80), channel_id=1, source_target_pairs={{0,8},{4,12},{8,16},{12,20},{1,9},{5,13},{9,17},{13,21},{2,10},{6,... | collective-permute-start | bytes 1572872 | tf_op jit(solution)/shard_map/dhid_first_up2/ppermute | solution.py:31
  128.1 14.4 %collective-permute-start.21 = (f16[128,2048]{1,0:T(8,128)(2,1)S(1)}, f16[128,2048]{1,0:T(8,128)(2,1)S(1)}, u32[]{:S(2)}, u32[]{:S(2)}) collective-permute-start(f16[128,2048]{1,0:T(8,128)(2,1)S(1)} %get-tuple-element.82), channel_id=1, source_target_pairs={{16,8},{20,12},{24,16},{28,20},{17,9},{21,13},{25,17},{29,21},{18,... | collective-permute-start | bytes 1572872 | tf_op jit(solution)/shard_map/dhid_first_down2/ppermute | solution.py:31
  128.8 15.3 %collective-permute-start.22 = (bf16[2,128,1536]{2,1,0:T(8,128)(2,1)S(1)}, bf16[2,128,1536]{2,1,0:T(8,128)(2,1)S(1)}, u32[]{:S(2)}, u32[]{:S(2)}) collective-permute-start(bf16[2,128,1536]{2,1,0:T(8,128)(2,1)S(1)} %collective-permute-done.18), channel_id=1, source_target_pairs={{16,24},{20,28},{17,25},{21,29},{18,26},{22,30},{19,27},{23,31}} | collective-permute-start | bytes 2359304 | tf_op jit(solution)/shard_map/hidden_last_up3/ppermute | solution.py:31
  129.9 22.9 %collective-permute-start.23 = (bf16[2,128,1536]{2,1,0:T(8,128)(2,1)S(1)}, bf16[2,128,1536]{2,1,0:T(8,128)(2,1)S(1)}, u32[]{:S(2)}, u32[]{:S(2)}) collective-permute-start(bf16[2,128,1536]{2,1,0:T(8,128)(2,1)S(1)} %collective-permute-done.19), channel_id=1, source_target_pairs={{8,0},{12,4},{9,1},{13,5},{10,2},{14,6},{11,3},{15,7}} | collective-permute-start | bytes 2359304 | tf_op jit(solution)/shard_map/hidden_last_down3/ppermute | solution.py:31
  131.8 32.2 %collective-permute-start.32 = (f16[2,128,1536]{2,1,0:T(8,128)(2,1)S(1)}, f16[2,128,1536]{2,1,0:T(8,128)(2,1)S(1)}, u32[]{:S(2)}, u32[]{:S(2)}) collective-permute-start(f16[2,128,1536]{2,1,0:T(8,128)(2,1)S(1)} %get-tuple-element.104), channel_id=1, source_target_pairs={{0,8},{4,12},{8,16},{12,20},{16,24},{20,28},{1,9},{5,13},{9,17},{1... | collective-permute-start | bytes 2359304 | tf_op jit(solution)/shard_map/dhid_last_up3/ppermute | solution.py:31
  141.1 28.5 %collective-permute-start.33 = (f16[2,128,1536]{2,1,0:T(8,128)(2,1)S(1)}, f16[2,128,1536]{2,1,0:T(8,128)(2,1)S(1)}, u32[]{:S(2)}, u32[]{:S(2)}) collective-permute-start(f16[2,128,1536]{2,1,0:T(8,128)(2,1)S(1)} %get-tuple-element.106), channel_id=1, source_target_pairs={{8,0},{12,4},{16,8},{20,12},{24,16},{28,20},{9,1},{13,5},{17,9},{2... | collective-permute-start | bytes 2359304 | tf_op jit(solution)/shard_map/dhid_last_down3/ppermute | solution.py:31
  142.4 16.5 %collective-permute-start.34 = (bf16[128,2048]{1,0:T(8,128)(2,1)S(1)}, bf16[128,2048]{1,0:T(8,128)(2,1)S(1)}, u32[]{:S(2)}, u32[]{:S(2)}) collective-permute-start(bf16[128,2048]{1,0:T(8,128)(2,1)S(1)} %get-tuple-element.108), channel_id=1, source_target_pairs={{0,4},{4,0},{8,12},{12,8},{16,20},{20,16},{24,28},{28,24},{1,5},{5... | collective-permute-start | bytes 1572872 | tf_op jit(solution)/shard_map/hidden_first_side/ppermute | solution.py:35
  144.0 20.0 %collective-permute-start.35 = (bf16[128,2048]{1,0:T(8,128)(2,1)S(1)}, bf16[128,2048]{1,0:T(8,128)(2,1)S(1)}, u32[]{:S(2)}, u32[]{:S(2)}) collective-permute-start(bf16[128,2048]{1,0:T(8,128)(2,1)S(1)} %get-tuple-element.110), channel_id=1, source_target_pairs={{0,4},{4,0},{8,12},{12,8},{16,20},{20,16},{24,28},{28,24},{1,5},{5... | collective-permute-start | bytes 1572872 | tf_op jit(solution)/shard_map/hidden_first_side/ppermute | solution.py:35
  153.9 24.3 %collective-permute-start.24 = (f16[128,2048]{1,0:T(8,128)(2,1)}, f16[128,2048]{1,0:T(8,128)(2,1)S(1)}, u32[]{:S(2)}, u32[]{:S(2)}) collective-permute-start(f16[128,2048]{1,0:T(8,128)(2,1)} %get-tuple-element.88), channel_id=1, source_target_pairs={{0,8},{4,12},{8,16},{12,20},{16,24},{20,28},{1,9},{5,13},{9,17},{1... | collective-permute-start | bytes 1572872 | tf_op jit(solution)/shard_map/dhid_first_up3/ppermute | solution.py:31
  158.9 19.3 %collective-permute-start.25 = (f16[128,2048]{1,0:T(8,128)(2,1)S(1)}, f16[128,2048]{1,0:T(8,128)(2,1)S(1)}, u32[]{:S(2)}, u32[]{:S(2)}) collective-permute-start(f16[128,2048]{1,0:T(8,128)(2,1)S(1)} %get-tuple-element.90), channel_id=1, source_target_pairs={{8,0},{12,4},{16,8},{20,12},{24,16},{28,20},{9,1},{13,5},{17,9},{2... | collective-permute-start | bytes 1572872 | tf_op jit(solution)/shard_map/dhid_first_down3/ppermute | solution.py:31
  (25 other events, 243.2 us)

commit v3 on v2

--- a/solution.py
+++ b/solution.py
@@ -73,7 +73,9 @@
     both_last = jnp.stack([last, last_other])
     last_up = along("hidden_last_up1", both_last, 1, 0, line - 2)
     last_down = along("hidden_last_down1", both_last, -1, 1, line - 1)
-    weight_other.append(across("weight_side", after(weight_first[middle:], theirs)))
+    bounds = [columns // 4, columns // 2, columns]
+    weight_other.append(across("weight_side", after(weight_first[bounds[0] : bounds[1]], theirs)))
+    weight_other.append(across("weight_side", after(weight_first[bounds[1] :], weight_other[1])))
     last_up, last_down = together(last_up, last_down)
 
     own = after(jnp.stack([mine, other, theirs])[:, :, None], weight_other[0])
@@ -85,7 +87,7 @@
         own = jnp.stack([jnp.where(low, own, swapped), jnp.where(low, swapped, own)], axis=3)
         own = own.reshape(3, line // 2, -1, share, half)
         bit //= 2
-    own = after(own, first_up)
+    own = after(own, first_up, weight_other[1])
     with jax.named_scope("cotangent_core"):
         swapped = lax.ppermute(own, "tensor", [(at, at ^ 1) for at in range(tensor)])
     whole = jnp.stack([jnp.where(odd == 0, own, swapped), jnp.where(odd == 0, swapped, own)], axis=2)
@@ -97,86 +99,74 @@
 
     parts = {"last": product(features_of_all, weight_last) * WIRE_SCALE}
 
+    weight_other = jnp.concatenate(weight_other)
+    parts["first"] = (product(mine, weight_first) + product(other, weight_other)) * WIRE_SCALE
+
     rising = {"first": [first, first_up], "last": [both_last, last_up]}
     falling = {"first": [first, first_down], "last": [both_last, last_down]}
-    up_sum = {"first": 0.0, "last": 0.0}
-    down_sum = {"first": 0.0, "last": 0.0}
-    sides = {}
 
-    def gather_step(which, step, waits):
+    def gather_step(which, step, *waits):
         up = along(f"hidden_{which}_up{step}", after(rising[which][-1], *waits), 1, step - 1, line - 2)
         down = along(f"hidden_{which}_down{step}", after(falling[which][-1], *waits), -1, 1, line - step)
-        return [up, down]
+        up, down = together(up, down)
+        rising[which].append(up)
+        falling[which].append(down)
 
-    def sum_step(which, step, waits):
-        message = after((parts[which][step] + up_sum[which]).astype(WIRE), *waits)
+    gather_step("first", 2)
+
+    sums, arrived = {"last": (0.0, 0.0), "first": (0.0, 0.0)}, {}
+    before, sent = {}, {}
+
+    def sum_step(which, step, *waits):
+        up, down = sums[which]
+        message = sent[which] = after((parts[which][step] + up).astype(WIRE), *waits)
         up = along(f"dhid_{which}_up{step}", message, 1, 0, step - 1)
-        message = after((parts[which][line - step] + down_sum[which]).astype(WIRE), *waits)
+        message = after((parts[which][line - step] + down).astype(WIRE), *waits)
         down = along(f"dhid_{which}_down{step}", message, -1, line - step, line - 1)
-        return [up, down]
+        up, down = together(up, down)
+        before[which], arrived[which] = arrived.get(which), up
+        sums[which] = up.astype(jnp.float32), down.astype(jnp.float32)
+
+    sum_step("last", 1)
+    for step in range(2, line):
+        if step > 2:
+            gather_step("first", step, sent["last"])
+        gather_step("last", step, sent["last"])
 
     def gathered(which, k):
         if k == 0:
             return rising[which][0]
         return jnp.where(position >= k, rising[which][k], falling[which][line - k])
 
-    def exchange(k, waits):
-        block = gathered("first", k)
-        return block, across("hidden_first_side", after(block, *waits))
+    blocks = jnp.stack([gathered("first", k) for k in range(line)])
+    exchanged = across("hidden_first_side", after(blocks, weight_other))
 
-    rounds = [first_up, last_up]
-    waiting, sent = [0], []
-    for step in range(1, line):
-        for which, summed in (("first", "last"), ("last", "first")):
-            begin = step == 1 and which == "first"
-            if step == 1 and summed == "first":
-                weight_other = jnp.concatenate(weight_other)
-                parts["first"] = (product(mine, weight_first) + product(other, weight_other)) * WIRE_SCALE
-            moved = sum_step(summed, step, rounds[-2:-1])
-            if step + 1 < line:
-                moved += gather_step(which, step + 1, rounds[-2:-1])
-            ahead = []
-            if not begin:
-                ahead = [(k,) + exchange(k, rounds[-2:-1]) for k in waiting]
-                waiting = []
-            if begin:
-                moved.append(weight_other[1])
-            moved = together(*moved, *[swapped for _, _, swapped in sent])
-            for k, block, _ in reversed(sent):
-                sides[k] = block, moved.pop()
-            if begin:
-                weight_other[1] = moved.pop()
-            if step + 1 < line:
-                falling[which].append(moved.pop())
-                rising[which].append(moved.pop())
-                if which == "first":
-                    waiting = waiting + [k for k in range(1, line) if max(k, line - k) == step + 1]
-            sent = ahead
-            up_sum[summed], down_sum[summed] = (value.astype(jnp.float32) for value in moved)
-            rounds.append(moved[0])
-    for k, *blocks in sent:
-        sides[k] = blocks
+    for step in range(2, line):
+        if step < line - 1:
+            sum_step("last", step, weight_other, rising["first"][step])
+            sum_step("first", step - 1, rising["first"][step])
+        else:
+            sum_step("last", step, rising["first"][step], rising["last"][step - 1])
+            sum_step("first", step - 1, rising["first"][step], before["last"])
+            exchanged = after(exchanged, arrived["last"])
+            sum_step("first", step, rising["last"][step], arrived["last"], exchanged)
 
-    def total(which):
-        return parts[which][0] + up_sum[which] + down_sum[which]
-
-    pair = total("last")
-    dhid_last = pair[0] + across("dhid_last_side", pair[1].astype(WIRE)).astype(jnp.float32)
-    dhid = jnp.concatenate([total("first"), dhid_last], axis=1) * (1.0 / WIRE_SCALE)
+    pair = parts["last"][0] + sums["last"][0] + sums["last"][1]
+    up, down, from_side = together(*sums["first"], across("dhid_last_side", pair[1].astype(WIRE)))
+    dhid = [parts["first"][0] + up + down, pair[0] + from_side.astype(jnp.float32)]
+    dhid = jnp.concatenate(dhid, axis=1) * (1.0 / WIRE_SCALE)
 
     grad_up = (dhid * act_vals).astype(jnp.bfloat16)
     grad_gate = (dhid * up_vals * sigma * (1.0 + gate_vals * (1.0 - sigma))).astype(jnp.bfloat16)
 
-    hidden_first = jnp.stack([jnp.stack(sides[k]) for k in range(line)])
+    hidden_first = jnp.stack([blocks, exchanged], axis=1)
     hidden_last = jnp.stack([gathered("last", k) for k in range(line)])
 
     def weight_grad(values):
         summed = jnp.einsum("kstc,kstf->cf", values, features_of_all, preferred_element_type=jnp.float32)
         return summed * (tokens * dp) ** (-0.5)
 
-    grad_down = jnp.zeros(down_weight.shape, jnp.float32)
-    grad_down = lax.dynamic_update_slice_in_dim(grad_down, weight_grad(hidden_last), columns, 0)
-    grad_down = lax.dynamic_update_slice_in_dim(grad_down, weight_grad(hidden_first), 0, 0)
+    grad_down = jnp.concatenate([weight_grad(hidden_first), weight_grad(hidden_last)])
     return grad_gate, grad_up, grad_down
 
 

time: 183 us -> 189 us (1.033)
  waiting for transfers between devices: 61.9 us -> 70.6 us
  matrix products: 13.6 us -> 8.68 us
  local copies, waits for them, and re-layouts: 7.7 us -> 9.91 us
  starting transfers between devices: 75.1 us -> 77.3 us
  other arithmetic: 22.1 us -> 20.1 us
    ppermute x24, waiting for transfers between devices: 38.6 us -> 54.1 us  [along(): return lax.ppermute(value, 'dp', pairs)]
    ppermute x24, starting transfers between devices: 54.2 us -> 60.7 us  [along(): return lax.ppermute(value, 'dp', pairs)]
    ppermute x1, waiting for transfers between devices: 5.81 us -> 0.84 us  [shards(): lax.ppermute(own, 'tensor', [(at, at ^ bit) for at in range(tensor)])]
    dot_general x3, matrix products: 9.31 us -> 4.39 us  [product(): jnp.einsum('...f,hf->...h', left, right, preferred_element_type=jnp.float32)]
    ppermute x9 -> x7, starting transfers between devices: 12.1 us -> 7.85 us  [across(): return lax.ppermute(value, 'dp', [(at, at ^ 1) for at in range(dp)])]
    dynamic_update_slice x1 -> x0, other arithmetic: 3.91 us -> none  [shards(): lax.dynamic_update_slice_in_dim(grad_down, weight_grad(hidden_first), 0, 0)]
    concatenate x0 -> x1, other arithmetic: none -> 3.89 us  [shards(): jnp.concatenate([weight_grad(hidden_first), weight_grad(hidden_last)])]
    select_n x2 -> x0, other arithmetic: 2.3 us -> none  [gathered(): return jnp.where(position >= k, rising[which][k], falling[which][line - k])]
  transfers between devices with their start and end apart: 37 -> 35, of which waited for: 15 -> 11; matrix products, arithmetic and copies ran while one was open for 20% -> 17% of each run, Pallas kernels for 0% -> 0%
where the time goes in v3:
time: 189 us; the launch traced here: 188 us
  starting transfers between devices  77.3 us (41%)
  waiting for transfers between devices  70.6 us (37%)
  other arithmetic  20.1 us (11%)
  local copies, waits for them, and re-layouts  9.91 us (5%)
  matrix products  8.68 us (5%)
    ppermute x24, starting transfers between devices, along(): return lax.ppermute(value, 'dp', pairs)  60.7 us
    ppermute x24, waiting for transfers between devices, along(): return lax.ppermute(value, 'dp', pairs)  54.1 us
    ppermute x7, waiting for transfers between devices, across(): return lax.ppermute(value, 'dp', [(at, at ^ 1) for at in range(dp)])  9.81 us
    ppermute x7, starting transfers between devices, across(): return lax.ppermute(value, 'dp', [(at, at ^ 1) for at in range(dp)])  7.85 us
    ppermute x2, starting transfers between devices, shards(): arrived.append(lax.ppermute(piece, ('dp', 'tensor'), pairs))  7.46 us
    ppermute x2, waiting for transfers between devices, shards(): arrived.append(lax.ppermute(piece, ('dp', 'tensor'), pairs))  5.82 us
    unnamed x12, local copies, waits for them, and re-layouts  5.21 us
    dot_general x3, matrix products, product(): jnp.einsum('...f,hf->...h', left, right, preferred_element_type=jnp.float32)  4.39 us
  transfers between devices with their start and end apart: 35, of which 11 were waited for; matrix products, arithmetic and copies ran while one was open for 17% of the time, Pallas kernels for 0%

profile of v3, /device:TPU:0, one launch (start us, length us, event | category | flops | bytes accessed | tf_op | source)
XLA Modules:
  0.0 187.9 jit_solution(7184365061434669933)
XLA Ops:
  2.4 6.8 %collective-permute-start.1 = (bf16[64,1024]{1,0:T(8,128)(2,1)S(1)}, bf16[64,1024]{1,0:T(8,128)(2,1)S(1)}, u32[]{:S(2)}, u32[]{:S(2)}) collective-permute-start(bf16[64,1024]{1,0:T(8,128)(2,1)S(1)} %get-tuple-element.138), channel_id=1, source_target_pairs={{0,2},{1,10},{2,18},{3,26},{4,6},{5,14},{6,22},{7,30},{8,3},{9,11}... | collective-permute-start | bytes 393224 | tf_op jit(solution)/shard_map/cotangent_spread/ppermute | solution.py:59
  12.8 2.1 %fusion.46 = (bf16[512,512]{1,0:T(8,128)(2,1)}, bf16[512,512]{1,0:T(8,128)(2,1)S(1)}) fusion(bf16[3584,512]{1,0:T(8,128)(2,1)} %param.7), kind=kLoop, calls=%fused_computation.108 | loop fusion | bytes 2097152 | tf_op jit(solution)/shard_map/slice | solution.py:77
  15.4 5.8 %collective-permute-done.1 = bf16[64,1024]{1,0:T(8,128)(2,1)S(1)} collective-permute-done((bf16[64,1024]{1,0:T(8,128)(2,1)S(1)}, bf16[64,1024]{1,0:T(8,128)(2,1)S(1)}, u32[]{:S(2)}, u32[]{:S(2)}) %collective-permute-start.1) | collective-permute-done | bytes 131104 | tf_op jit(solution)/shard_map/cotangent_spread/ppermute | solution.py:59
  21.4 2.0 %collective-permute-done.2 = bf16[128,1536]{1,0:T(8,128)(2,1)} collective-permute-done((bf16[128,1536]{1,0:T(8,128)(2,1)S(1)}, bf16[128,1536]{1,0:T(8,128)(2,1)}, u32[]{:S(2)}, u32[]{:S(2)}) %collective-permute-start.2) | collective-permute-done | bytes 393248 | tf_op jit(solution)/shard_map/hidden_last_side/ppermute | solution.py:35
  25.1 4.9 %collective-permute-start.6 = (bf16[128,2048]{1,0:T(8,128)(2,1)S(1)}, bf16[128,2048]{1,0:T(8,128)(2,1)}, u32[]{:S(2)}, u32[]{:S(2)}) collective-permute-start(bf16[128,2048]{1,0:T(8,128)(2,1)S(1)} %get-tuple-element.56), channel_id=1, source_target_pairs={{0,8},{4,12},{8,16},{12,20},{16,24},{20,28},{1,9},{5,13},{9,17},{1... | collective-permute-start | bytes 1572872 | tf_op jit(solution)/shard_map/hidden_first_up1/ppermute | solution.py:31
  31.3 4.6 %collective-permute-done.3 = bf16[2,64,512]{2,1,0:T(8,128)(2,1)S(1)} collective-permute-done((bf16[2,64,512]{2,1,0:T(8,128)(2,1)S(1)}, bf16[2,64,512]{2,1,0:T(8,128)(2,1)S(1)}, u32[]{:S(2)}, u32[]{:S(2)}) %collective-permute-start.3) | collective-permute-done | bytes 131104 | tf_op jit(solution)/shard_map/cotangent_side/ppermute | solution.py:35
  38.8 2.2 %fusion.44 = (bf16[1,2,128,1536]{3,2,1,0:T(8,128)(2,1)}, bf16[2,128,1536]{2,1,0:T(8,128)(2,1)}) fusion(bf16[1,128,1536]{2,1,0:T(8,128)(2,1)} %bitcast.27, bf16[1,128,1536]{2,1,0:T(8,128)(2,1)S(1)} %get-tuple-element.130), kind=kLoop, calls=%fused_computation.106 | loop fusion | flops 393216 | bytes 2359296 | tf_op jit(solution)/shard_map/stack | solution.py:163
  41.1 2.3 %collective-permute-start.23 = (bf16[2,128,1536]{2,1,0:T(8,128)(2,1)}, bf16[2,128,1536]{2,1,0:T(8,128)(2,1)S(1)}, u32[]{:S(2)}, u32[]{:S(2)}) collective-permute-start(bf16[2,128,1536]{2,1,0:T(8,128)(2,1)} %get-tuple-element.133), channel_id=1, source_target_pairs={{0,8},{4,12},{8,16},{12,20},{16,24},{20,28},{1,9},{5,13},{9,17},{1... | collective-permute-start | bytes 2359304 | tf_op jit(solution)/shard_map/hidden_last_up1/ppermute | solution.py:31
  48.5 3.2 %collective-permute-done.8 = bf16[512,512]{1,0:T(8,128)(2,1)} collective-permute-done((bf16[512,512]{1,0:T(8,128)(2,1)}, bf16[512,512]{1,0:T(8,128)(2,1)}, u32[]{:S(2)}, u32[]{:S(2)}) %collective-permute-start.8) | collective-permute-done | bytes 524320 | tf_op jit(solution)/shard_map/weight_side/ppermute | solution.py:35
  56.7 18.5 %collective-permute-done.12 = bf16[128,2048]{1,0:T(8,128)(2,1)} collective-permute-done((bf16[128,2048]{1,0:T(8,128)(2,1)}, bf16[128,2048]{1,0:T(8,128)(2,1)}, u32[]{:S(2)}, u32[]{:S(2)}) %collective-permute-start.12) | collective-permute-done | bytes 524320 | tf_op jit(solution)/shard_map/hidden_first_down2/ppermute | solution.py:31
  81.7 3.6 %collective-permute-start.17 = (f16[2,128,1536]{2,1,0:T(8,128)(2,1)S(1)}, f16[2,128,1536]{2,1,0:T(8,128)(2,1)S(1)}, u32[]{:S(2)}, u32[]{:S(2)}) collective-permute-start(f16[2,128,1536]{2,1,0:T(8,128)(2,1)S(1)} %get-tuple-element.110), channel_id=1, source_target_pairs={{0,8},{4,12},{1,9},{5,13},{2,10},{6,14},{3,11},{7,15}} | collective-permute-start | bytes 2359304 | tf_op jit(solution)/shard_map/dhid_last_up1/ppermute | solution.py:31
  92.9 7.5 %collective-permute-done.16 = bf16[128,2048]{1,0:T(8,128)(2,1)S(1)} collective-permute-done((bf16[128,2048]{1,0:T(8,128)(2,1)}, bf16[128,2048]{1,0:T(8,128)(2,1)S(1)}, u32[]{:S(2)}, u32[]{:S(2)}) %collective-permute-start.16) | collective-permute-done | bytes 524320 | tf_op jit(solution)/shard_map/hidden_first_down3/ppermute | solution.py:31
  100.4 5.5 %collective-permute-start.13 = (f16[128,2048]{1,0:T(8,128)(2,1)S(1)}, f16[128,2048]{1,0:T(8,128)(2,1)S(1)}, u32[]{:S(2)}, u32[]{:S(2)}) collective-permute-start(f16[128,2048]{1,0:T(8,128)(2,1)S(1)} %get-tuple-element.63), channel_id=1, source_target_pairs={{0,8},{4,12},{1,9},{5,13},{2,10},{6,14},{3,11},{7,15}} | collective-permute-start | bytes 1572872 | tf_op jit(solution)/shard_map/dhid_first_up1/ppermute | solution.py:31
  109.3 7.4 %collective-permute-start.19 = (f16[2,128,1536]{2,1,0:T(8,128)(2,1)S(1)}, f16[2,128,1536]{2,1,0:T(8,128)(2,1)S(1)}, u32[]{:S(2)}, u32[]{:S(2)}) collective-permute-start(f16[2,128,1536]{2,1,0:T(8,128)(2,1)S(1)} %get-tuple-element.71), channel_id=1, source_target_pairs={{0,8},{4,12},{8,16},{12,20},{1,9},{5,13},{9,17},{13,21},{2,10},{6,... | collective-permute-start | bytes 2359304 | tf_op jit(solution)/shard_map/dhid_last_up2/ppermute | solution.py:31
  116.7 2.2 %collective-permute-done.26 = bf16[2,128,1536]{2,1,0:T(8,128)(2,1)S(1)} collective-permute-done((bf16[2,128,1536]{2,1,0:T(8,128)(2,1)}, bf16[2,128,1536]{2,1,0:T(8,128)(2,1)S(1)}, u32[]{:S(2)}, u32[]{:S(2)}) %collective-permute-start.26) | collective-permute-done | bytes 786464 | tf_op jit(solution)/shard_map/hidden_last_down2/ppermute | solution.py:31
  122.1 9.0 %collective-permute-done.19 = f16[2,128,1536]{2,1,0:T(8,128)(2,1)S(1)} collective-permute-done((f16[2,128,1536]{2,1,0:T(8,128)(2,1)S(1)}, f16[2,128,1536]{2,1,0:T(8,128)(2,1)S(1)}, u32[]{:S(2)}, u32[]{:S(2)}) %collective-permute-start.19) | collective-permute-done | bytes 786464 | tf_op jit(solution)/shard_map/dhid_last_up2/ppermute | solution.py:31
  131.7 9.0 %collective-permute-start.29 = (f16[2,128,1536]{2,1,0:T(8,128)(2,1)S(1)}, f16[2,128,1536]{2,1,0:T(8,128)(2,1)S(1)}, u32[]{:S(2)}, u32[]{:S(2)}) collective-permute-start(f16[2,128,1536]{2,1,0:T(8,128)(2,1)S(1)} %get-tuple-element.88), channel_id=1, source_target_pairs={{0,8},{4,12},{8,16},{12,20},{16,24},{20,28},{1,9},{5,13},{9,17},{1... | collective-permute-start | bytes 2359304 | tf_op jit(solution)/shard_map/dhid_last_up3/ppermute | solution.py:31
  142.0 4.7 %collective-permute-start.21 = (f16[128,2048]{1,0:T(8,128)(2,1)S(1)}, f16[128,2048]{1,0:T(8,128)(2,1)S(1)}, u32[]{:S(2)}, u32[]{:S(2)}) collective-permute-start(f16[128,2048]{1,0:T(8,128)(2,1)S(1)} %get-tuple-element.75), channel_id=1, source_target_pairs={{0,8},{4,12},{8,16},{12,20},{1,9},{5,13},{9,17},{13,21},{2,10},{6,... | collective-permute-start | bytes 1572872 | tf_op jit(solution)/shard_map/dhid_first_up2/ppermute | solution.py:31
  150.9 13.2 %collective-permute-done.21 = f16[128,2048]{1,0:T(8,128)(2,1)S(1)} collective-permute-done((f16[128,2048]{1,0:T(8,128)(2,1)S(1)}, f16[128,2048]{1,0:T(8,128)(2,1)S(1)}, u32[]{:S(2)}, u32[]{:S(2)}) %collective-permute-start.21) | collective-permute-done | bytes 524320 | tf_op jit(solution)/shard_map/dhid_first_up2/ppermute | solution.py:31
  166.4 6.3 %collective-permute-start.32 = (f16[128,2048]{1,0:T(8,128)(2,1)}, f16[128,2048]{1,0:T(8,128)(2,1)S(1)}, u32[]{:S(2)}, u32[]{:S(2)}) collective-permute-start(f16[128,2048]{1,0:T(8,128)(2,1)} %get-tuple-element.95), channel_id=1, source_target_pairs={{0,8},{4,12},{8,16},{12,20},{16,24},{20,28},{1,9},{5,13},{9,17},{1... | collective-permute-start | bytes 1572872 | tf_op jit(solution)/shard_map/dhid_first_up3/ppermute | solution.py:31
  174.0 2.4 %bitcast_multiply_fusion = f32[2048,512]{1,0:T(8,128)S(1)} fusion(bf16[4,1,128,512]{3,2,1,0:T(8,128)(2,1)S(1)} %bitcast.128, bf16[4,1,128,512]{3,2,1,0:T(8,128)(2,1)S(1)} %bitcast.124, bf16[4,1,128,2048]{3,2,0,1:T(8,128)(2,1)S(1)} %bitcast.133, bf16[4,1,128,2048]{3,2,0,1:T(8,128)(2,1)S(1)} %get-tuple-element.121), kind=kOutput, calls=%fused_computation.3 | convolution fusion | flops 2151153664 | bytes 9437184 | tf_op jit(solution)/shard_map/kstc,kstf->cf/dot_general | solution.py:166
  176.4 3.9 %pad_maximum_fusion = f32[3584,512]{1,0:T(8,128)} fusion(f32[1536,512]{1,0:T(8,128)S(1)} %fusion.2, f32[2048,512]{1,0:T(8,128)S(1)} %bitcast_multiply_fusion), kind=kLoop, calls=%fused_computation | loop fusion | flops 1835008 | bytes 14680064 | tf_op jit(solution)/shard_map/concatenate | solution.py:169
  180.3 3.7 %collective-permute-done.33 = f16[128,2048]{1,0:T(8,128)(2,1)S(1)} collective-permute-done((f16[128,2048]{1,0:T(8,128)(2,1)}, f16[128,2048]{1,0:T(8,128)(2,1)S(1)}, u32[]{:S(2)}, u32[]{:S(2)}) %collective-permute-start.33) | collective-permute-done | bytes 524320 | tf_op jit(solution)/shard_map/dhid_first_down3/ppermute | solution.py:31
  185.7 2.2 %multiply_convert_fusion = (bf16[128,3584]{1,0:T(8,128)(2,1)}, bf16[128,3584]{1,0:T(8,128)(2,1)}) fusion(f32[128,1536]{1,0:T(8,128)S(1)} %fusion.34, f32[128,2048]{1,0:T(8,128)S(1)} %fusion.31, bf16[128,3584]{1,0:T(8,128)(2,1)S(1)} %copy-done.1, bf16[128,3584]{1,0:T(8,128)(2,1)S(1)} %copy-done.2), kind=kLoop, calls=%fused_computation.35 | loop fusion | flops 7798784 | bytes 5505024 | tf_op jit(solution)/shard_map/convert_element_type | solution.py:159
  (100 shorter events, 53.5 us)
Async XLA Ops:
  2.4 18.8 %collective-permute-start.1 = (bf16[64,1024]{1,0:T(8,128)(2,1)S(1)}, bf16[64,1024]{1,0:T(8,128)(2,1)S(1)}, u32[]{:S(2)}, u32[]{:S(2)}) collective-permute-start(bf16[64,1024]{1,0:T(8,128)(2,1)S(1)} %get-tuple-element.138), channel_id=1, source_target_pairs={{0,2},{1,10},{2,18},{3,26},{4,6},{5,14},{6,22},{7,30},{8,3},{9,11}... | collective-permute-start | bytes 393224 | tf_op jit(solution)/shard_map/cotangent_spread/ppermute | solution.py:59
  14.9 21.1 %collective-permute-start.4 = (bf16[512,512]{1,0:T(8,128)(2,1)S(1)}, bf16[512,512]{1,0:T(8,128)(2,1)S(1)}, u32[]{:S(2)}, u32[]{:S(2)}) collective-permute-start(bf16[512,512]{1,0:T(8,128)(2,1)S(1)} %get-tuple-element.118), channel_id=1, source_target_pairs={{0,4},{4,0},{8,12},{12,8},{16,20},{20,16},{24,28},{28,24},{1,5},{5... | collective-permute-start | bytes 1572872 | tf_op jit(solution)/shard_map/weight_side/ppermute | solution.py:35
  25.1 18.3 %collective-permute-start.6 = (bf16[128,2048]{1,0:T(8,128)(2,1)S(1)}, bf16[128,2048]{1,0:T(8,128)(2,1)}, u32[]{:S(2)}, u32[]{:S(2)}) collective-permute-start(bf16[128,2048]{1,0:T(8,128)(2,1)S(1)} %get-tuple-element.56), channel_id=1, source_target_pairs={{0,8},{4,12},{8,16},{12,20},{16,24},{20,28},{1,9},{5,13},{9,17},{1... | collective-permute-start | bytes 1572872 | tf_op jit(solution)/shard_map/hidden_first_up1/ppermute | solution.py:31
  30.0 14.7 %collective-permute-start.7 = (bf16[128,2048]{1,0:T(8,128)(2,1)S(1)}, bf16[128,2048]{1,0:T(8,128)(2,1)}, u32[]{:S(2)}, u32[]{:S(2)}) collective-permute-start(bf16[128,2048]{1,0:T(8,128)(2,1)S(1)} %get-tuple-element.56), channel_id=1, source_target_pairs={{8,0},{12,4},{16,8},{20,12},{24,16},{28,20},{9,1},{13,5},{17,9},{2... | collective-permute-start | bytes 1572872 | tf_op jit(solution)/shard_map/hidden_first_down1/ppermute | solution.py:31
  37.3 14.3 %collective-permute-start.8 = (bf16[512,512]{1,0:T(8,128)(2,1)}, bf16[512,512]{1,0:T(8,128)(2,1)}, u32[]{:S(2)}, u32[]{:S(2)}) collective-permute-start(bf16[512,512]{1,0:T(8,128)(2,1)} %get-tuple-element.58), channel_id=1, source_target_pairs={{0,4},{4,0},{8,12},{12,8},{16,20},{20,16},{24,28},{28,24},{1,5},{5... | collective-permute-start | bytes 1572872 | tf_op jit(solution)/shard_map/weight_side/ppermute | solution.py:35
  41.1 35.2 %collective-permute-start.23 = (bf16[2,128,1536]{2,1,0:T(8,128)(2,1)}, bf16[2,128,1536]{2,1,0:T(8,128)(2,1)S(1)}, u32[]{:S(2)}, u32[]{:S(2)}) collective-permute-start(bf16[2,128,1536]{2,1,0:T(8,128)(2,1)} %get-tuple-element.133), channel_id=1, source_target_pairs={{0,8},{4,12},{8,16},{12,20},{16,24},{20,28},{1,9},{5,13},{9,17},{1... | collective-permute-start | bytes 2359304 | tf_op jit(solution)/shard_map/hidden_last_up1/ppermute | solution.py:31
  43.4 32.9 %collective-permute-start.24 = (bf16[2,128,1536]{2,1,0:T(8,128)(2,1)}, bf16[2,128,1536]{2,1,0:T(8,128)(2,1)}, u32[]{:S(2)}, u32[]{:S(2)}) collective-permute-start(bf16[2,128,1536]{2,1,0:T(8,128)(2,1)} %get-tuple-element.133), channel_id=1, source_target_pairs={{8,0},{12,4},{16,8},{20,12},{24,16},{28,20},{9,1},{13,5},{17,9},{2... | collective-permute-start | bytes 2359304 | tf_op jit(solution)/shard_map/hidden_last_down1/ppermute | solution.py:31
  47.0 28.2 %collective-permute-start.12 = (bf16[128,2048]{1,0:T(8,128)(2,1)}, bf16[128,2048]{1,0:T(8,128)(2,1)}, u32[]{:S(2)}, u32[]{:S(2)}) collective-permute-start(bf16[128,2048]{1,0:T(8,128)(2,1)} %collective-permute-done.7), channel_id=1, source_target_pairs={{8,0},{12,4},{16,8},{20,12},{9,1},{13,5},{17,9},{21,13},{10,2},{14... | collective-permute-start | bytes 1572872 | tf_op jit(solution)/shard_map/hidden_first_down2/ppermute | solution.py:31
  51.6 24.7 %collective-permute-start.9 = (bf16[3,2,2,64,512]{4,3,1,0,2:T(8,128)(2,1)S(1)}, bf16[3,2,2,64,512]{4,3,1,0,2:T(8,128)(2,1)}, u32[]{:S(2)}, u32[]{:S(2)}) collective-permute-start(bf16[3,2,2,64,512]{4,3,1,0,2:T(8,128)(2,1)S(1)} %maximum_bitcast_fusion), channel_id=1, source_target_pairs={{0,1},{1,0},{2,3},{3,2},{4,5},{5,4},{6,7},{7,6},{8,9},{9,8},{10,11... | collective-permute-start | bytes 2359304 | tf_op jit(solution)/shard_map/cotangent_core/ppermute | solution.py:92
  55.1 34.3 %collective-permute-start.10 = (bf16[1024,512]{1,0:T(8,128)(2,1)S(1)}, bf16[1024,512]{1,0:T(8,128)(2,1)S(1)}, u32[]{:S(2)}, u32[]{:S(2)}) collective-permute-start(bf16[1024,512]{1,0:T(8,128)(2,1)S(1)} %slice.79), channel_id=1, source_target_pairs={{0,4},{4,0},{8,12},{12,8},{16,20},{20,16},{24,28},{28,24},{1,5},{5... | collective-permute-start | bytes 3145736 | tf_op jit(solution)/shard_map/weight_side/ppermute | solution.py:35
  81.7 25.9 %collective-permute-start.17 = (f16[2,128,1536]{2,1,0:T(8,128)(2,1)S(1)}, f16[2,128,1536]{2,1,0:T(8,128)(2,1)S(1)}, u32[]{:S(2)}, u32[]{:S(2)}) collective-permute-start(f16[2,128,1536]{2,1,0:T(8,128)(2,1)S(1)} %get-tuple-element.110), channel_id=1, source_target_pairs={{0,8},{4,12},{1,9},{5,13},{2,10},{6,14},{3,11},{7,15}} | collective-permute-start | bytes 2359304 | tf_op jit(solution)/shard_map/dhid_last_up1/ppermute | solution.py:31
  85.3 22.9 %collective-permute-start.18 = (f16[2,128,1536]{2,1,0:T(8,128)(2,1)S(1)}, f16[2,128,1536]{2,1,0:T(8,128)(2,1)S(1)}, u32[]{:S(2)}, u32[]{:S(2)}) collective-permute-start(f16[2,128,1536]{2,1,0:T(8,128)(2,1)S(1)} %get-tuple-element.109), channel_id=1, source_target_pairs={{24,16},{28,20},{25,17},{29,21},{26,18},{30,22},{27,19},{31,23}} | collective-permute-start | bytes 2359304 | tf_op jit(solution)/shard_map/dhid_last_down1/ppermute | solution.py:31
  89.4 19.9 %collective-permute-start.25 = (bf16[2,128,1536]{2,1,0:T(8,128)(2,1)S(1)}, bf16[2,128,1536]{2,1,0:T(8,128)(2,1)S(1)}, u32[]{:S(2)}, u32[]{:S(2)}) collective-permute-start(bf16[2,128,1536]{2,1,0:T(8,128)(2,1)S(1)} %collective-permute-done.23), channel_id=1, source_target_pairs={{8,16},{12,20},{16,24},{20,28},{9,17},{13,21},{17,25},{21,29},{10,... | collective-permute-start | bytes 2359304 | tf_op jit(solution)/shard_map/hidden_last_up2/ppermute | solution.py:31
  91.6 27.3 %collective-permute-start.26 = (bf16[2,128,1536]{2,1,0:T(8,128)(2,1)}, bf16[2,128,1536]{2,1,0:T(8,128)(2,1)S(1)}, u32[]{:S(2)}, u32[]{:S(2)}) collective-permute-start(bf16[2,128,1536]{2,1,0:T(8,128)(2,1)} %collective-permute-done.24), channel_id=1, source_target_pairs={{8,0},{12,4},{16,8},{20,12},{9,1},{13,5},{17,9},{21,13},{10,2},{14... | collective-permute-start | bytes 2359304 | tf_op jit(solution)/shard_map/hidden_last_down2/ppermute | solution.py:31
  100.4 19.4 %collective-permute-start.13 = (f16[128,2048]{1,0:T(8,128)(2,1)S(1)}, f16[128,2048]{1,0:T(8,128)(2,1)S(1)}, u32[]{:S(2)}, u32[]{:S(2)}) collective-permute-start(f16[128,2048]{1,0:T(8,128)(2,1)S(1)} %get-tuple-element.63), channel_id=1, source_target_pairs={{0,8},{4,12},{1,9},{5,13},{2,10},{6,14},{3,11},{7,15}} | collective-permute-start | bytes 1572872 | tf_op jit(solution)/shard_map/dhid_first_up1/ppermute | solution.py:31
  108.3 58.1 %collective-permute-start.31 = (bf16[4,128,2048]{2,1,0:T(8,128)(2,1)S(1)}, bf16[4,128,2048]{2,1,0:T(8,128)(2,1)S(1)}, u32[]{:S(2)}, u32[]{:S(2)}) collective-permute-start(bf16[4,128,2048]{2,1,0:T(8,128)(2,1)S(1)} %get-tuple-element.93), channel_id=1, source_target_pairs={{0,4},{4,0},{8,12},{12,8},{16,20},{20,16},{24,28},{28,24},{1,5},{5... | collective-permute-start | bytes 6291464 | tf_op jit(solution)/shard_map/hidden_first_side/ppermute | solution.py:35
  109.3 21.9 %collective-permute-start.19 = (f16[2,128,1536]{2,1,0:T(8,128)(2,1)S(1)}, f16[2,128,1536]{2,1,0:T(8,128)(2,1)S(1)}, u32[]{:S(2)}, u32[]{:S(2)}) collective-permute-start(f16[2,128,1536]{2,1,0:T(8,128)(2,1)S(1)} %get-tuple-element.71), channel_id=1, source_target_pairs={{0,8},{4,12},{8,16},{12,20},{1,9},{5,13},{9,17},{13,21},{2,10},{6,... | collective-permute-start | bytes 2359304 | tf_op jit(solution)/shard_map/dhid_last_up2/ppermute | solution.py:31
  119.8 22.2 %collective-permute-start.27 = (bf16[2,128,1536]{2,1,0:T(8,128)(2,1)S(1)}, bf16[2,128,1536]{2,1,0:T(8,128)(2,1)S(1)}, u32[]{:S(2)}, u32[]{:S(2)}) collective-permute-start(bf16[2,128,1536]{2,1,0:T(8,128)(2,1)S(1)} %collective-permute-done.25), channel_id=1, source_target_pairs={{16,24},{20,28},{17,25},{21,29},{18,26},{22,30},{19,27},{23,31}} | collective-permute-start | bytes 2359304 | tf_op jit(solution)/shard_map/hidden_last_up3/ppermute | solution.py:31
  120.5 26.2 %collective-permute-start.28 = (bf16[2,128,1536]{2,1,0:T(8,128)(2,1)S(1)}, bf16[2,128,1536]{2,1,0:T(8,128)(2,1)S(1)}, u32[]{:S(2)}, u32[]{:S(2)}) collective-permute-start(bf16[2,128,1536]{2,1,0:T(8,128)(2,1)S(1)} %collective-permute-done.26), channel_id=1, source_target_pairs={{8,0},{12,4},{9,1},{13,5},{10,2},{14,6},{11,3},{15,7}} | collective-permute-start | bytes 2359304 | tf_op jit(solution)/shard_map/hidden_last_down3/ppermute | solution.py:31
  131.7 33.7 %collective-permute-start.29 = (f16[2,128,1536]{2,1,0:T(8,128)(2,1)S(1)}, f16[2,128,1536]{2,1,0:T(8,128)(2,1)S(1)}, u32[]{:S(2)}, u32[]{:S(2)}) collective-permute-start(f16[2,128,1536]{2,1,0:T(8,128)(2,1)S(1)} %get-tuple-element.88), channel_id=1, source_target_pairs={{0,8},{4,12},{8,16},{12,20},{16,24},{20,28},{1,9},{5,13},{9,17},{1... | collective-permute-start | bytes 2359304 | tf_op jit(solution)/shard_map/dhid_last_up3/ppermute | solution.py:31
  140.7 24.7 %collective-permute-start.30 = (f16[2,128,1536]{2,1,0:T(8,128)(2,1)S(1)}, f16[2,128,1536]{2,1,0:T(8,128)(2,1)S(1)}, u32[]{:S(2)}, u32[]{:S(2)}) collective-permute-start(f16[2,128,1536]{2,1,0:T(8,128)(2,1)S(1)} %get-tuple-element.90), channel_id=1, source_target_pairs={{8,0},{12,4},{16,8},{20,12},{24,16},{28,20},{9,1},{13,5},{17,9},{2... | collective-permute-start | bytes 2359304 | tf_op jit(solution)/shard_map/dhid_last_down3/ppermute | solution.py:31
  142.0 22.1 %collective-permute-start.21 = (f16[128,2048]{1,0:T(8,128)(2,1)S(1)}, f16[128,2048]{1,0:T(8,128)(2,1)S(1)}, u32[]{:S(2)}, u32[]{:S(2)}) collective-permute-start(f16[128,2048]{1,0:T(8,128)(2,1)S(1)} %get-tuple-element.75), channel_id=1, source_target_pairs={{0,8},{4,12},{8,16},{12,20},{1,9},{5,13},{9,17},{13,21},{2,10},{6,... | collective-permute-start | bytes 1572872 | tf_op jit(solution)/shard_map/dhid_first_up2/ppermute | solution.py:31
  146.8 17.3 %collective-permute-start.22 = (f16[128,2048]{1,0:T(8,128)(2,1)S(1)}, f16[128,2048]{1,0:T(8,128)(2,1)S(1)}, u32[]{:S(2)}, u32[]{:S(2)}) collective-permute-start(f16[128,2048]{1,0:T(8,128)(2,1)S(1)} %get-tuple-element.77), channel_id=1, source_target_pairs={{16,8},{20,12},{24,16},{28,20},{17,9},{21,13},{25,17},{29,21},{18,... | collective-permute-start | bytes 1572872 | tf_op jit(solution)/shard_map/dhid_first_down2/ppermute | solution.py:31
  165.8 18.3 %collective-permute-start.34 = (f16[128,1536]{1,0:T(8,128)(2,1)S(1)}, f16[128,1536]{1,0:T(8,128)(2,1)S(1)}, u32[]{:S(2)}, u32[]{:S(2)}) collective-permute-start(f16[128,1536]{1,0:T(8,128)(2,1)S(1)} %fusion.37), channel_id=1, source_target_pairs={{0,4},{4,0},{8,12},{12,8},{16,20},{20,16},{24,28},{28,24},{1,5},{5... | collective-permute-start | bytes 1179656 | tf_op jit(solution)/shard_map/dhid_last_side/ppermute | solution.py:35
  (16 other events, 152.8 us)

commit v4 on v3

--- a/solution.py
+++ b/solution.py
@@ -108,7 +108,6 @@
     def gather_step(which, step, *waits):
         up = along(f"hidden_{which}_up{step}", after(rising[which][-1], *waits), 1, step - 1, line - 2)
         down = along(f"hidden_{which}_down{step}", after(falling[which][-1], *waits), -1, 1, line - step)
-        up, down = together(up, down)
         rising[which].append(up)
         falling[which].append(down)
 
@@ -128,26 +127,35 @@
         sums[which] = up.astype(jnp.float32), down.astype(jnp.float32)
 
     sum_step("last", 1)
-    for step in range(2, line):
-        if step > 2:
-            gather_step("first", step, sent["last"])
-        gather_step("last", step, sent["last"])
+    rising["first"][2], falling["first"][2], _ = together(rising["first"][2], falling["first"][2], sent["last"])
+    gather_step("first", 3, sent["last"])
+    gather_step("last", 2, sent["last"])
 
     def gathered(which, k):
         if k == 0:
             return rising[which][0]
         return jnp.where(position >= k, rising[which][k], falling[which][line - k])
 
-    blocks = jnp.stack([gathered("first", k) for k in range(line)])
-    exchanged = across("hidden_first_side", after(blocks, weight_other))
+    def settle(which, step):
+        up, down, _ = together(rising[which][step], falling[which][step], sent["last"])
+        rising[which][step], falling[which][step] = up, down
 
     for step in range(2, line):
         if step < line - 1:
             sum_step("last", step, weight_other, rising["first"][step])
+            settle("first", step + 1)
+            settle("last", step)
+            if step + 2 < line:
+                gather_step("first", step + 2)
+            else:
+                blocks = jnp.stack([gathered("first", k) for k in range(line)])
+                exchanged = across("hidden_first_side", after(blocks, weight_other))
+            gather_step("last", step + 1)
             sum_step("first", step - 1, rising["first"][step])
         else:
-            sum_step("last", step, rising["first"][step], rising["last"][step - 1])
-            sum_step("first", step - 1, rising["first"][step], before["last"])
+            sum_step("last", step)
+            settle("last", step)
+            sum_step("first", step - 1, before["last"])
             exchanged = after(exchanged, arrived["last"])
             sum_step("first", step, rising["last"][step], arrived["last"], exchanged)
 

time: 189 us -> 176 us (0.931)
  starting transfers between devices: 77.3 us -> 66.1 us
  waiting for transfers between devices: 70.6 us -> 68.3 us
    ppermute x24, starting transfers between devices: 60.7 us -> 46.8 us  [along(): return lax.ppermute(value, 'dp', pairs)]
    ppermute x24, waiting for transfers between devices: 54.1 us -> 40.2 us  [along(): return lax.ppermute(value, 'dp', pairs)]
    ppermute x7, waiting for transfers between devices: 9.81 us -> 20 us  [across(): return lax.ppermute(value, 'dp', [(at, at ^ 1) for at in range(dp)])]
    ppermute x7, starting transfers between devices: 7.85 us -> 10.6 us  [across(): return lax.ppermute(value, 'dp', [(at, at ^ 1) for at in range(dp)])]
    unnamed x12 -> x18, local copies, waits for them, and re-layouts: 5.21 us -> 5.95 us
  transfers between devices with their start and end apart: 35 -> 35, of which waited for: 11 -> 15; matrix products, arithmetic and copies ran while one was open for 17% -> 18% of each run, Pallas kernels for 0% -> 0%
where the time goes in v4:
time: 176 us; the launch traced here: 175 us
  waiting for transfers between devices  68.3 us (39%)
  starting transfers between devices  66.1 us (38%)
  other arithmetic  19.7 us (11%)
  local copies, waits for them, and re-layouts  10.8 us (6%)
  matrix products  8.69 us (5%)
    ppermute x24, starting transfers between devices, along(): return lax.ppermute(value, 'dp', pairs)  46.8 us
    ppermute x24, waiting for transfers between devices, along(): return lax.ppermute(value, 'dp', pairs)  40.2 us
    ppermute x7, waiting for transfers between devices, across(): return lax.ppermute(value, 'dp', [(at, at ^ 1) for at in range(dp)])  20 us
    ppermute x7, starting transfers between devices, across(): return lax.ppermute(value, 'dp', [(at, at ^ 1) for at in range(dp)])  10.6 us
    ppermute x2, starting transfers between devices, shards(): arrived.append(lax.ppermute(piece, ('dp', 'tensor'), pairs))  7.46 us
    unnamed x18, local copies, waits for them, and re-layouts  5.95 us
    ppermute x2, waiting for transfers between devices, shards(): arrived.append(lax.ppermute(piece, ('dp', 'tensor'), pairs))  5.65 us
    dot_general x3, matrix products, product(): jnp.einsum('...f,hf->...h', left, right, preferred_element_type=jnp.float32)  4.39 us
  transfers between devices with their start and end apart: 35, of which 15 were waited for; matrix products, arithmetic and copies ran while one was open for 18% of the time, Pallas kernels for 0%

profile of v4, /device:TPU:0, one launch (start us, length us, event | category | flops | bytes accessed | tf_op | source)
XLA Modules:
  0.0 175.0 jit_solution(17867577069814204414)
XLA Ops:
  2.4 6.8 %collective-permute-start.1 = (bf16[64,1024]{1,0:T(8,128)(2,1)S(1)}, bf16[64,1024]{1,0:T(8,128)(2,1)S(1)}, u32[]{:S(2)}, u32[]{:S(2)}) collective-permute-start(bf16[64,1024]{1,0:T(8,128)(2,1)S(1)} %get-tuple-element.130), channel_id=1, source_target_pairs={{0,2},{1,10},{2,18},{3,26},{4,6},{5,14},{6,22},{7,30},{8,3},{9,11}... | collective-permute-start | bytes 393224 | tf_op jit(solution)/shard_map/cotangent_spread/ppermute | solution.py:59
  15.6 5.6 %collective-permute-done.1 = bf16[64,1024]{1,0:T(8,128)(2,1)S(1)} collective-permute-done((bf16[64,1024]{1,0:T(8,128)(2,1)S(1)}, bf16[64,1024]{1,0:T(8,128)(2,1)S(1)}, u32[]{:S(2)}, u32[]{:S(2)}) %collective-permute-start.1) | collective-permute-done | bytes 131104 | tf_op jit(solution)/shard_map/cotangent_spread/ppermute | solution.py:59
  25.7 4.1 %collective-permute-start.6 = (bf16[128,2048]{1,0:T(8,128)(2,1)S(1)}, bf16[128,2048]{1,0:T(8,128)(2,1)S(1)}, u32[]{:S(2)}, u32[]{:S(2)}) collective-permute-start(bf16[128,2048]{1,0:T(8,128)(2,1)S(1)} %get-tuple-element.52), channel_id=1, source_target_pairs={{0,8},{4,12},{8,16},{12,20},{16,24},{20,28},{1,9},{5,13},{9,17},{1... | collective-permute-start | bytes 1572872 | tf_op jit(solution)/shard_map/hidden_first_up1/ppermute | solution.py:31
  31.2 4.8 %collective-permute-done.3 = bf16[2,64,512]{2,1,0:T(8,128)(2,1)S(1)} collective-permute-done((bf16[2,64,512]{2,1,0:T(8,128)(2,1)S(1)}, bf16[2,64,512]{2,1,0:T(8,128)(2,1)S(1)}, u32[]{:S(2)}, u32[]{:S(2)}) %collective-permute-start.3) | collective-permute-done | bytes 131104 | tf_op jit(solution)/shard_map/cotangent_side/ppermute | solution.py:35
  44.7 2.4 %collective-permute-done.5 = bf16[3,2,1,64,512]{4,3,1,0,2:T(8,128)(2,1)} collective-permute-done((bf16[3,2,1,64,512]{4,3,1,0,2:T(8,128)(2,1)S(1)}, bf16[3,2,1,64,512]{4,3,1,0,2:T(8,128)(2,1)}, u32[]{:S(2)}, u32[]{:S(2)}) %collective-permute-start.5) | collective-permute-done | bytes 393248 | tf_op jit(solution)/shard_map/cotangent_shares/ppermute | solution.py:85
  48.3 3.3 %collective-permute-done.8 = bf16[512,512]{1,0:T(8,128)(2,1)} collective-permute-done((bf16[512,512]{1,0:T(8,128)(2,1)}, bf16[512,512]{1,0:T(8,128)(2,1)}, u32[]{:S(2)}, u32[]{:S(2)}) %collective-permute-start.8) | collective-permute-done | bytes 524320 | tf_op jit(solution)/shard_map/weight_side/ppermute | solution.py:35
  57.1 2.7 %collective-permute-done.21 = bf16[2,128,1536]{2,1,0:T(8,128)(2,1)S(1)} collective-permute-done((bf16[2,128,1536]{2,1,0:T(8,128)(2,1)}, bf16[2,128,1536]{2,1,0:T(8,128)(2,1)S(1)}, u32[]{:S(2)}, u32[]{:S(2)}) %collective-permute-start.21) | collective-permute-done | bytes 786464 | tf_op jit(solution)/shard_map/hidden_last_up1/ppermute | solution.py:31
  60.3 5.8 %collective-permute-done.22 = bf16[2,128,1536]{2,1,0:T(8,128)(2,1)} collective-permute-done((bf16[2,128,1536]{2,1,0:T(8,128)(2,1)}, bf16[2,128,1536]{2,1,0:T(8,128)(2,1)}, u32[]{:S(2)}, u32[]{:S(2)}) %collective-permute-start.22) | collective-permute-done | bytes 786464 | tf_op jit(solution)/shard_map/hidden_last_down1/ppermute | solution.py:31
  71.4 3.6 %collective-permute-start.15 = (f16[2,128,1536]{2,1,0:T(8,128)(2,1)S(1)}, f16[2,128,1536]{2,1,0:T(8,128)(2,1)S(1)}, u32[]{:S(2)}, u32[]{:S(2)}) collective-permute-start(f16[2,128,1536]{2,1,0:T(8,128)(2,1)S(1)} %get-tuple-element.102), channel_id=1, source_target_pairs={{0,8},{4,12},{1,9},{5,13},{2,10},{6,14},{3,11},{7,15}} | collective-permute-start | bytes 2359304 | tf_op jit(solution)/shard_map/dhid_last_up1/ppermute | solution.py:31
  79.2 3.9 %collective-permute-done.10 = bf16[1024,512]{1,0:T(8,128)(2,1)S(1)} collective-permute-done((bf16[1024,512]{1,0:T(8,128)(2,1)S(1)}, bf16[1024,512]{1,0:T(8,128)(2,1)S(1)}, u32[]{:S(2)}, u32[]{:S(2)}) %collective-permute-start.10) | collective-permute-done | bytes 1048608 | tf_op jit(solution)/shard_map/weight_side/ppermute | solution.py:35
  85.3 3.0 %collective-permute-done.15 = f16[2,128,1536]{2,1,0:T(8,128)(2,1)S(1)} collective-permute-done((f16[2,128,1536]{2,1,0:T(8,128)(2,1)S(1)}, f16[2,128,1536]{2,1,0:T(8,128)(2,1)S(1)}, u32[]{:S(2)}, u32[]{:S(2)}) %collective-permute-start.15) | collective-permute-done | bytes 786464 | tf_op jit(solution)/shard_map/dhid_last_up1/ppermute | solution.py:31
  88.3 4.4 %collective-permute-start.13 = (f16[128,2048]{1,0:T(8,128)(2,1)S(1)}, f16[128,2048]{1,0:T(8,128)(2,1)S(1)}, u32[]{:S(2)}, u32[]{:S(2)}) collective-permute-start(f16[128,2048]{1,0:T(8,128)(2,1)S(1)} %get-tuple-element.59), channel_id=1, source_target_pairs={{0,8},{4,12},{1,9},{5,13},{2,10},{6,14},{3,11},{7,15}} | collective-permute-start | bytes 1572872 | tf_op jit(solution)/shard_map/dhid_first_up1/ppermute | solution.py:31
  93.9 5.5 %collective-permute-done.13 = f16[128,2048]{1,0:T(8,128)(2,1)S(1)} collective-permute-done((f16[128,2048]{1,0:T(8,128)(2,1)S(1)}, f16[128,2048]{1,0:T(8,128)(2,1)S(1)}, u32[]{:S(2)}, u32[]{:S(2)}) %collective-permute-start.13) | collective-permute-done | bytes 524320 | tf_op jit(solution)/shard_map/dhid_first_up1/ppermute | solution.py:31
  100.7 4.6 %collective-permute-start.17 = (f16[2,128,1536]{2,1,0:T(8,128)(2,1)S(1)}, f16[2,128,1536]{2,1,0:T(8,128)(2,1)S(1)}, u32[]{:S(2)}, u32[]{:S(2)}) collective-permute-start(f16[2,128,1536]{2,1,0:T(8,128)(2,1)S(1)} %get-tuple-element.63), channel_id=1, source_target_pairs={{0,8},{4,12},{8,16},{12,20},{1,9},{5,13},{9,17},{13,21},{2,10},{6,... | collective-permute-start | bytes 2359304 | tf_op jit(solution)/shard_map/dhid_last_up2/ppermute | solution.py:31
  108.2 7.6 %collective-permute-done.30 = bf16[128,2048]{1,0:T(8,128)(2,1)S(1)} collective-permute-done((bf16[128,2048]{1,0:T(8,128)(2,1)S(1)}, bf16[128,2048]{1,0:T(8,128)(2,1)S(1)}, u32[]{:S(2)}, u32[]{:S(2)}) %collective-permute-start.30) | collective-permute-done | bytes 524320 | tf_op jit(solution)/shard_map/hidden_first_down3/ppermute | solution.py:31
  118.2 4.9 %collective-permute-start.27 = (f16[2,128,1536]{2,1,0:T(8,128)(2,1)S(1)}, f16[2,128,1536]{2,1,0:T(8,128)(2,1)S(1)}, u32[]{:S(2)}, u32[]{:S(2)}) collective-permute-start(f16[2,128,1536]{2,1,0:T(8,128)(2,1)S(1)} %get-tuple-element.98), channel_id=1, source_target_pairs={{0,8},{4,12},{8,16},{12,20},{16,24},{20,28},{1,9},{5,13},{9,17},{1... | collective-permute-start | bytes 2359304 | tf_op jit(solution)/shard_map/dhid_last_up3/ppermute | solution.py:31
  124.5 4.7 %collective-permute-start.19 = (f16[128,2048]{1,0:T(8,128)(2,1)S(1)}, f16[128,2048]{1,0:T(8,128)(2,1)S(1)}, u32[]{:S(2)}, u32[]{:S(2)}) collective-permute-start(f16[128,2048]{1,0:T(8,128)(2,1)S(1)} %get-tuple-element.67), channel_id=1, source_target_pairs={{0,8},{4,12},{8,16},{12,20},{1,9},{5,13},{9,17},{13,21},{2,10},{6,... | collective-permute-start | bytes 1572872 | tf_op jit(solution)/shard_map/dhid_first_up2/ppermute | solution.py:31
  129.2 3.4 %collective-permute-done.26 = bf16[2,128,1536]{2,1,0:T(8,128)(2,1)S(1)} collective-permute-done((bf16[2,128,1536]{2,1,0:T(8,128)(2,1)S(1)}, bf16[2,128,1536]{2,1,0:T(8,128)(2,1)S(1)}, u32[]{:S(2)}, u32[]{:S(2)}) %collective-permute-start.26) | collective-permute-done | bytes 786464 | tf_op jit(solution)/shard_map/hidden_last_down3/ppermute | solution.py:31
  136.7 7.7 %collective-permute-done.19 = f16[128,2048]{1,0:T(8,128)(2,1)S(1)} collective-permute-done((f16[128,2048]{1,0:T(8,128)(2,1)S(1)}, f16[128,2048]{1,0:T(8,128)(2,1)S(1)}, u32[]{:S(2)}, u32[]{:S(2)}) %collective-permute-start.19) | collective-permute-done | bytes 524320 | tf_op jit(solution)/shard_map/dhid_first_up2/ppermute | solution.py:31
  146.0 4.9 %collective-permute-start.34 = (f16[128,1536]{1,0:T(8,128)(2,1)S(1)}, f16[128,1536]{1,0:T(8,128)(2,1)S(1)}, u32[]{:S(2)}, u32[]{:S(2)}) collective-permute-start(f16[128,1536]{1,0:T(8,128)(2,1)S(1)} %fusion.37), channel_id=1, source_target_pairs={{0,4},{4,0},{8,12},{12,8},{16,20},{20,16},{24,28},{28,24},{1,5},{5... | collective-permute-start | bytes 1179656 | tf_op jit(solution)/shard_map/dhid_last_side/ppermute | solution.py:35
  150.9 6.0 %collective-permute-done.31 = bf16[4,128,2048]{2,1,0:T(8,128)(2,1)S(1)} collective-permute-done((bf16[4,128,2048]{2,1,0:T(8,128)(2,1)S(1)}, bf16[4,128,2048]{2,1,0:T(8,128)(2,1)S(1)}, u32[]{:S(2)}, u32[]{:S(2)}) %collective-permute-start.31) | collective-permute-done | bytes 2097184 | tf_op jit(solution)/shard_map/hidden_first_side/ppermute | solution.py:35
  160.2 2.4 %bitcast_multiply_fusion = f32[2048,512]{1,0:T(8,128)S(1)} fusion(bf16[4,1,128,512]{3,2,1,0:T(8,128)(2,1)S(1)} %bitcast.128, bf16[4,1,128,512]{3,2,1,0:T(8,128)(2,1)S(1)} %bitcast.124, bf16[4,1,128,2048]{3,2,0,1:T(8,128)(2,1)S(1)} %bitcast.134, bf16[4,1,128,2048]{3,2,0,1:T(8,128)(2,1)S(1)} %get-tuple-element.113), kind=kOutput, calls=%fused_computation.3 | convolution fusion | flops 2151153664 | bytes 9437184 | tf_op jit(solution)/shard_map/kstc,kstf->cf/dot_general | solution.py:174
  162.6 3.9 %pad_maximum_fusion = f32[3584,512]{1,0:T(8,128)} fusion(f32[1536,512]{1,0:T(8,128)S(1)} %fusion.2, f32[2048,512]{1,0:T(8,128)S(1)} %bitcast_multiply_fusion), kind=kLoop, calls=%fused_computation | loop fusion | flops 1835008 | bytes 14680064 | tf_op jit(solution)/shard_map/concatenate | solution.py:177
  166.5 4.5 %collective-permute-done.33 = f16[128,2048]{1,0:T(8,128)(2,1)S(1)} collective-permute-done((f16[128,2048]{1,0:T(8,128)(2,1)S(1)}, f16[128,2048]{1,0:T(8,128)(2,1)S(1)}, u32[]{:S(2)}, u32[]{:S(2)}) %collective-permute-start.33) | collective-permute-done | bytes 524320 | tf_op jit(solution)/shard_map/dhid_first_down3/ppermute | solution.py:31
  (106 shorter events, 62.9 us)
Async XLA Ops:
  2.4 18.8 %collective-permute-start.1 = (bf16[64,1024]{1,0:T(8,128)(2,1)S(1)}, bf16[64,1024]{1,0:T(8,128)(2,1)S(1)}, u32[]{:S(2)}, u32[]{:S(2)}) collective-permute-start(bf16[64,1024]{1,0:T(8,128)(2,1)S(1)} %get-tuple-element.130), channel_id=1, source_target_pairs={{0,2},{1,10},{2,18},{3,26},{4,6},{5,14},{6,22},{7,30},{8,3},{9,11}... | collective-permute-start | bytes 393224 | tf_op jit(solution)/shard_map/cotangent_spread/ppermute | solution.py:59
  15.1 20.9 %collective-permute-start.4 = (bf16[512,512]{1,0:T(8,128)(2,1)}, bf16[512,512]{1,0:T(8,128)(2,1)S(1)}, u32[]{:S(2)}, u32[]{:S(2)}) collective-permute-start(bf16[512,512]{1,0:T(8,128)(2,1)} %get-tuple-element.110), channel_id=1, source_target_pairs={{0,4},{4,0},{8,12},{12,8},{16,20},{20,16},{24,28},{28,24},{1,5},{5... | collective-permute-start | bytes 1572872 | tf_op jit(solution)/shard_map/weight_side/ppermute | solution.py:35
  25.7 17.6 %collective-permute-start.6 = (bf16[128,2048]{1,0:T(8,128)(2,1)S(1)}, bf16[128,2048]{1,0:T(8,128)(2,1)S(1)}, u32[]{:S(2)}, u32[]{:S(2)}) collective-permute-start(bf16[128,2048]{1,0:T(8,128)(2,1)S(1)} %get-tuple-element.52), channel_id=1, source_target_pairs={{0,8},{4,12},{8,16},{12,20},{16,24},{20,28},{1,9},{5,13},{9,17},{1... | collective-permute-start | bytes 1572872 | tf_op jit(solution)/shard_map/hidden_first_up1/ppermute | solution.py:31
  29.9 14.8 %collective-permute-start.7 = (bf16[128,2048]{1,0:T(8,128)(2,1)S(1)}, bf16[128,2048]{1,0:T(8,128)(2,1)}, u32[]{:S(2)}, u32[]{:S(2)}) collective-permute-start(bf16[128,2048]{1,0:T(8,128)(2,1)S(1)} %get-tuple-element.52), channel_id=1, source_target_pairs={{8,0},{12,4},{16,8},{20,12},{24,16},{28,20},{9,1},{13,5},{17,9},{2... | collective-permute-start | bytes 1572872 | tf_op jit(solution)/shard_map/hidden_first_down1/ppermute | solution.py:31
  41.1 18.7 %collective-permute-start.21 = (bf16[2,128,1536]{2,1,0:T(8,128)(2,1)}, bf16[2,128,1536]{2,1,0:T(8,128)(2,1)S(1)}, u32[]{:S(2)}, u32[]{:S(2)}) collective-permute-start(bf16[2,128,1536]{2,1,0:T(8,128)(2,1)} %get-tuple-element.125), channel_id=1, source_target_pairs={{0,8},{4,12},{8,16},{12,20},{16,24},{20,28},{1,9},{5,13},{9,17},{1... | collective-permute-start | bytes 2359304 | tf_op jit(solution)/shard_map/hidden_last_up1/ppermute | solution.py:31
  43.4 22.7 %collective-permute-start.22 = (bf16[2,128,1536]{2,1,0:T(8,128)(2,1)}, bf16[2,128,1536]{2,1,0:T(8,128)(2,1)}, u32[]{:S(2)}, u32[]{:S(2)}) collective-permute-start(bf16[2,128,1536]{2,1,0:T(8,128)(2,1)} %get-tuple-element.125), channel_id=1, source_target_pairs={{8,0},{12,4},{16,8},{20,12},{24,16},{28,20},{9,1},{13,5},{17,9},{2... | collective-permute-start | bytes 2359304 | tf_op jit(solution)/shard_map/hidden_last_down1/ppermute | solution.py:31
  51.6 14.5 %collective-permute-start.9 = (bf16[3,2,2,64,512]{4,3,1,0,2:T(8,128)(2,1)S(1)}, bf16[3,2,2,64,512]{4,3,1,0,2:T(8,128)(2,1)}, u32[]{:S(2)}, u32[]{:S(2)}) collective-permute-start(bf16[3,2,2,64,512]{4,3,1,0,2:T(8,128)(2,1)S(1)} %maximum_bitcast_fusion), channel_id=1, source_target_pairs={{0,1},{1,0},{2,3},{3,2},{4,5},{5,4},{6,7},{7,6},{8,9},{9,8},{10,11... | collective-permute-start | bytes 2359304 | tf_op jit(solution)/shard_map/cotangent_core/ppermute | solution.py:92
  54.0 21.8 %collective-permute-start.11 = (bf16[128,2048]{1,0:T(8,128)(2,1)}, bf16[128,2048]{1,0:T(8,128)(2,1)S(1)}, u32[]{:S(2)}, u32[]{:S(2)}) collective-permute-start(bf16[128,2048]{1,0:T(8,128)(2,1)} %copy-done.5), channel_id=1, source_target_pairs={{8,16},{12,20},{16,24},{20,28},{9,17},{13,21},{17,25},{21,29},{10,... | collective-permute-start | bytes 1572872 | tf_op jit(solution)/shard_map/hidden_first_up2/ppermute | solution.py:31
  54.7 21.1 %collective-permute-start.12 = (bf16[128,2048]{1,0:T(8,128)(2,1)}, bf16[128,2048]{1,0:T(8,128)(2,1)S(1)}, u32[]{:S(2)}, u32[]{:S(2)}) collective-permute-start(bf16[128,2048]{1,0:T(8,128)(2,1)} %collective-permute-done.7), channel_id=1, source_target_pairs={{8,0},{12,4},{16,8},{20,12},{9,1},{13,5},{17,9},{21,13},{10,2},{14... | collective-permute-start | bytes 1572872 | tf_op jit(solution)/shard_map/hidden_first_down2/ppermute | solution.py:31
  59.8 23.3 %collective-permute-start.10 = (bf16[1024,512]{1,0:T(8,128)(2,1)S(1)}, bf16[1024,512]{1,0:T(8,128)(2,1)S(1)}, u32[]{:S(2)}, u32[]{:S(2)}) collective-permute-start(bf16[1024,512]{1,0:T(8,128)(2,1)S(1)} %slice.79), channel_id=1, source_target_pairs={{0,4},{4,0},{8,12},{12,8},{16,20},{20,16},{24,28},{28,24},{1,5},{5... | collective-permute-start | bytes 3145736 | tf_op jit(solution)/shard_map/weight_side/ppermute | solution.py:35
  71.4 16.9 %collective-permute-start.15 = (f16[2,128,1536]{2,1,0:T(8,128)(2,1)S(1)}, f16[2,128,1536]{2,1,0:T(8,128)(2,1)S(1)}, u32[]{:S(2)}, u32[]{:S(2)}) collective-permute-start(f16[2,128,1536]{2,1,0:T(8,128)(2,1)S(1)} %get-tuple-element.102), channel_id=1, source_target_pairs={{0,8},{4,12},{1,9},{5,13},{2,10},{6,14},{3,11},{7,15}} | collective-permute-start | bytes 2359304 | tf_op jit(solution)/shard_map/dhid_last_up1/ppermute | solution.py:31
  75.0 17.7 %collective-permute-start.16 = (f16[2,128,1536]{2,1,0:T(8,128)(2,1)S(1)}, f16[2,128,1536]{2,1,0:T(8,128)(2,1)S(1)}, u32[]{:S(2)}, u32[]{:S(2)}) collective-permute-start(f16[2,128,1536]{2,1,0:T(8,128)(2,1)S(1)} %get-tuple-element.101), channel_id=1, source_target_pairs={{24,16},{28,20},{25,17},{29,21},{26,18},{30,22},{27,19},{31,23}} | collective-permute-start | bytes 2359304 | tf_op jit(solution)/shard_map/dhid_last_down1/ppermute | solution.py:31
  75.8 29.5 %collective-permute-start.23 = (bf16[2,128,1536]{2,1,0:T(8,128)(2,1)S(1)}, bf16[2,128,1536]{2,1,0:T(8,128)(2,1)S(1)}, u32[]{:S(2)}, u32[]{:S(2)}) collective-permute-start(bf16[2,128,1536]{2,1,0:T(8,128)(2,1)S(1)} %collective-permute-done.21), channel_id=1, source_target_pairs={{8,16},{12,20},{16,24},{20,28},{9,17},{13,21},{17,25},{21,29},{10,... | collective-permute-start | bytes 2359304 | tf_op jit(solution)/shard_map/hidden_last_up2/ppermute | solution.py:31
  76.5 29.5 %collective-permute-start.24 = (bf16[2,128,1536]{2,1,0:T(8,128)(2,1)}, bf16[2,128,1536]{2,1,0:T(8,128)(2,1)S(1)}, u32[]{:S(2)}, u32[]{:S(2)}) collective-permute-start(bf16[2,128,1536]{2,1,0:T(8,128)(2,1)} %collective-permute-done.22), channel_id=1, source_target_pairs={{8,0},{12,4},{16,8},{20,12},{9,1},{13,5},{17,9},{21,13},{10,2},{14... | collective-permute-start | bytes 2359304 | tf_op jit(solution)/shard_map/hidden_last_down2/ppermute | solution.py:31
  83.1 23.8 %collective-permute-start.29 = (bf16[128,2048]{1,0:T(8,128)(2,1)S(1)}, bf16[128,2048]{1,0:T(8,128)(2,1)S(1)}, u32[]{:S(2)}, u32[]{:S(2)}) collective-permute-start(bf16[128,2048]{1,0:T(8,128)(2,1)S(1)} %collective-permute-done.11), channel_id=1, source_target_pairs={{16,24},{20,28},{17,25},{21,29},{18,26},{22,30},{19,27},{23,31}} | collective-permute-start | bytes 1572872 | tf_op jit(solution)/shard_map/hidden_first_up3/ppermute | solution.py:31
  99.4 16.4 %collective-permute-start.30 = (bf16[128,2048]{1,0:T(8,128)(2,1)S(1)}, bf16[128,2048]{1,0:T(8,128)(2,1)S(1)}, u32[]{:S(2)}, u32[]{:S(2)}) collective-permute-start(bf16[128,2048]{1,0:T(8,128)(2,1)S(1)} %collective-permute-done.12), channel_id=1, source_target_pairs={{8,0},{12,4},{9,1},{13,5},{10,2},{14,6},{11,3},{15,7}} | collective-permute-start | bytes 1572872 | tf_op jit(solution)/shard_map/hidden_first_down3/ppermute | solution.py:31
  100.7 17.0 %collective-permute-start.17 = (f16[2,128,1536]{2,1,0:T(8,128)(2,1)S(1)}, f16[2,128,1536]{2,1,0:T(8,128)(2,1)S(1)}, u32[]{:S(2)}, u32[]{:S(2)}) collective-permute-start(f16[2,128,1536]{2,1,0:T(8,128)(2,1)S(1)} %get-tuple-element.63), channel_id=1, source_target_pairs={{0,8},{4,12},{8,16},{12,20},{1,9},{5,13},{9,17},{13,21},{2,10},{6,... | collective-permute-start | bytes 2359304 | tf_op jit(solution)/shard_map/dhid_last_up2/ppermute | solution.py:31
  106.0 18.5 %collective-permute-start.25 = (bf16[2,128,1536]{2,1,0:T(8,128)(2,1)S(1)}, bf16[2,128,1536]{2,1,0:T(8,128)(2,1)S(1)}, u32[]{:S(2)}, u32[]{:S(2)}) collective-permute-start(bf16[2,128,1536]{2,1,0:T(8,128)(2,1)S(1)} %collective-permute-done.23), channel_id=1, source_target_pairs={{16,24},{20,28},{17,25},{21,29},{18,26},{22,30},{19,27},{23,31}} | collective-permute-start | bytes 2359304 | tf_op jit(solution)/shard_map/hidden_last_up3/ppermute | solution.py:31
  106.9 25.7 %collective-permute-start.26 = (bf16[2,128,1536]{2,1,0:T(8,128)(2,1)S(1)}, bf16[2,128,1536]{2,1,0:T(8,128)(2,1)S(1)}, u32[]{:S(2)}, u32[]{:S(2)}) collective-permute-start(bf16[2,128,1536]{2,1,0:T(8,128)(2,1)S(1)} %collective-permute-done.24), channel_id=1, source_target_pairs={{8,0},{12,4},{9,1},{13,5},{10,2},{14,6},{11,3},{15,7}} | collective-permute-start | bytes 2359304 | tf_op jit(solution)/shard_map/hidden_last_down3/ppermute | solution.py:31
  117.3 39.7 %collective-permute-start.31 = (bf16[4,128,2048]{2,1,0:T(8,128)(2,1)S(1)}, bf16[4,128,2048]{2,1,0:T(8,128)(2,1)S(1)}, u32[]{:S(2)}, u32[]{:S(2)}) collective-permute-start(bf16[4,128,2048]{2,1,0:T(8,128)(2,1)S(1)} %get-tuple-element.85), channel_id=1, source_target_pairs={{0,4},{4,0},{8,12},{12,8},{16,20},{20,16},{24,28},{28,24},{1,5},{5... | collective-permute-start | bytes 6291464 | tf_op jit(solution)/shard_map/hidden_first_side/ppermute | solution.py:35
  118.2 27.4 %collective-permute-start.27 = (f16[2,128,1536]{2,1,0:T(8,128)(2,1)S(1)}, f16[2,128,1536]{2,1,0:T(8,128)(2,1)S(1)}, u32[]{:S(2)}, u32[]{:S(2)}) collective-permute-start(f16[2,128,1536]{2,1,0:T(8,128)(2,1)S(1)} %get-tuple-element.98), channel_id=1, source_target_pairs={{0,8},{4,12},{8,16},{12,20},{16,24},{20,28},{1,9},{5,13},{9,17},{1... | collective-permute-start | bytes 2359304 | tf_op jit(solution)/shard_map/dhid_last_up3/ppermute | solution.py:31
  123.2 22.4 %collective-permute-start.28 = (f16[2,128,1536]{2,1,0:T(8,128)(2,1)S(1)}, f16[2,128,1536]{2,1,0:T(8,128)(2,1)S(1)}, u32[]{:S(2)}, u32[]{:S(2)}) collective-permute-start(f16[2,128,1536]{2,1,0:T(8,128)(2,1)S(1)} %get-tuple-element.97), channel_id=1, source_target_pairs={{8,0},{12,4},{16,8},{20,12},{24,16},{28,20},{9,1},{13,5},{17,9},{2... | collective-permute-start | bytes 2359304 | tf_op jit(solution)/shard_map/dhid_last_down3/ppermute | solution.py:31
  124.5 19.9 %collective-permute-start.19 = (f16[128,2048]{1,0:T(8,128)(2,1)S(1)}, f16[128,2048]{1,0:T(8,128)(2,1)S(1)}, u32[]{:S(2)}, u32[]{:S(2)}) collective-permute-start(f16[128,2048]{1,0:T(8,128)(2,1)S(1)} %get-tuple-element.67), channel_id=1, source_target_pairs={{0,8},{4,12},{8,16},{12,20},{1,9},{5,13},{9,17},{13,21},{2,10},{6,... | collective-permute-start | bytes 1572872 | tf_op jit(solution)/shard_map/dhid_first_up2/ppermute | solution.py:31
  146.0 25.2 %collective-permute-start.34 = (f16[128,1536]{1,0:T(8,128)(2,1)S(1)}, f16[128,1536]{1,0:T(8,128)(2,1)S(1)}, u32[]{:S(2)}, u32[]{:S(2)}) collective-permute-start(f16[128,1536]{1,0:T(8,128)(2,1)S(1)} %fusion.37), channel_id=1, source_target_pairs={{0,4},{4,0},{8,12},{12,8},{16,20},{20,16},{24,28},{28,24},{1,5},{5... | collective-permute-start | bytes 1179656 | tf_op jit(solution)/shard_map/dhid_last_side/ppermute | solution.py:35
  (19 other events, 182.7 us)

commit v5 on v4

--- a/solution.py
+++ b/solution.py
@@ -114,7 +114,7 @@
     gather_step("first", 2)
 
     sums, arrived = {"last": (0.0, 0.0), "first": (0.0, 0.0)}, {}
-    before, sent = {}, {}
+    before, sent, ended = {}, {}, {}
 
     def sum_step(which, step, *waits):
         up, down = sums[which]
@@ -122,8 +122,10 @@
         up = along(f"dhid_{which}_up{step}", message, 1, 0, step - 1)
         message = after((parts[which][line - step] + down).astype(WIRE), *waits)
         down = along(f"dhid_{which}_down{step}", message, -1, line - step, line - 1)
-        up, down = together(up, down)
+        if which == "last" or step < line - 1:
+            up, down = together(up, down)
         before[which], arrived[which] = arrived.get(which), up
+        ended[which] = up, down
         sums[which] = up.astype(jnp.float32), down.astype(jnp.float32)
 
     sum_step("last", 1)
@@ -136,15 +138,15 @@
             return rising[which][0]
         return jnp.where(position >= k, rising[which][k], falling[which][line - k])
 
-    def settle(which, step):
-        up, down, _ = together(rising[which][step], falling[which][step], sent["last"])
+    def settle(which, step, message):
+        up, down, _ = together(rising[which][step], falling[which][step], message)
         rising[which][step], falling[which][step] = up, down
 
     for step in range(2, line):
         if step < line - 1:
             sum_step("last", step, weight_other, rising["first"][step])
-            settle("first", step + 1)
-            settle("last", step)
+            settle("first", step + 1, sent["last"])
+            settle("last", step, sent["last"])
             if step + 2 < line:
                 gather_step("first", step + 2)
             else:
@@ -154,18 +156,10 @@
             sum_step("first", step - 1, rising["first"][step])
         else:
             sum_step("last", step)
-            settle("last", step)
             sum_step("first", step - 1, before["last"])
+            settle("last", step, sent["first"])
             exchanged = after(exchanged, arrived["last"])
-            sum_step("first", step, rising["last"][step], arrived["last"], exchanged)
-
-    pair = parts["last"][0] + sums["last"][0] + sums["last"][1]
-    up, down, from_side = together(*sums["first"], across("dhid_last_side", pair[1].astype(WIRE)))
-    dhid = [parts["first"][0] + up + down, pair[0] + from_side.astype(jnp.float32)]
-    dhid = jnp.concatenate(dhid, axis=1) * (1.0 / WIRE_SCALE)
-
-    grad_up = (dhid * act_vals).astype(jnp.bfloat16)
-    grad_gate = (dhid * up_vals * sigma * (1.0 + gate_vals * (1.0 - sigma))).astype(jnp.bfloat16)
+            sum_step("first", step, rising["last"][step], arrived["last"])
 
     hidden_first = jnp.stack([blocks, exchanged], axis=1)
     hidden_last = jnp.stack([gathered("last", k) for k in range(line)])
@@ -175,6 +169,14 @@
         return summed * (tokens * dp) ** (-0.5)
 
     grad_down = jnp.concatenate([weight_grad(hidden_first), weight_grad(hidden_last)])
+    pair = parts["last"][0] + sums["last"][0] + sums["last"][1]
+    from_side = across("dhid_last_side", pair[1].astype(WIRE))
+    up, down, from_side, grad_down = together(*ended["first"], from_side, grad_down)
+    dhid = [parts["first"][0] + up + down, pair[0] + from_side.astype(jnp.float32)]
+    dhid = jnp.concatenate(dhid, axis=1) * (1.0 / WIRE_SCALE)
+
+    grad_up = (dhid * act_vals).astype(jnp.bfloat16)
+    grad_gate = (dhid * up_vals * sigma * (1.0 + gate_vals * (1.0 - sigma))).astype(jnp.bfloat16)
     return grad_gate, grad_up, grad_down
 
 

time: 176 us -> 170 us (0.966)
  waiting for transfers between devices: 68.3 us -> 57.7 us
  starting transfers between devices: 66.1 us -> 70.5 us
    ppermute x7, waiting for transfers between devices: 20 us -> 13.9 us  [across(): return lax.ppermute(value, 'dp', [(at, at ^ 1) for at in range(dp)])]
    ppermute x24, waiting for transfers between devices: 40.2 us -> 35.7 us  [along(): return lax.ppermute(value, 'dp', pairs)]
    ppermute x24, starting transfers between devices: 46.8 us -> 51.1 us  [along(): return lax.ppermute(value, 'dp', pairs)]
  transfers between devices with their start and end apart: 35 -> 35, of which waited for: 15 -> 13; matrix products, arithmetic and copies ran while one was open for 18% -> 19% of each run, Pallas kernels for 0% -> 0%
where the time goes in v5:
time: 170 us; the launch traced here: 169 us
  starting transfers between devices  70.5 us (41%)
  waiting for transfers between devices  57.7 us (34%)
  other arithmetic  19.7 us (12%)
  local copies, waits for them, and re-layouts  10.7 us (6%)
  matrix products  8.68 us (5%)
    ppermute x24, starting transfers between devices, along(): return lax.ppermute(value, 'dp', pairs)  51.1 us
    ppermute x24, waiting for transfers between devices, along(): return lax.ppermute(value, 'dp', pairs)  35.7 us
    ppermute x7, waiting for transfers between devices, across(): return lax.ppermute(value, 'dp', [(at, at ^ 1) for at in range(dp)])  13.9 us
    ppermute x7, starting transfers between devices, across(): return lax.ppermute(value, 'dp', [(at, at ^ 1) for at in range(dp)])  10.6 us
    ppermute x2, starting transfers between devices, shards(): arrived.append(lax.ppermute(piece, ('dp', 'tensor'), pairs))  7.46 us
    unnamed x18, local copies, waits for them, and re-layouts  5.84 us
    ppermute x2, waiting for transfers between devices, shards(): arrived.append(lax.ppermute(piece, ('dp', 'tensor'), pairs))  5.65 us
    dot_general x3, matrix products, product(): jnp.einsum('...f,hf->...h', left, right, preferred_element_type=jnp.float32)  4.39 us
  transfers between devices with their start and end apart: 35, of which 13 were waited for; matrix products, arithmetic and copies ran while one was open for 19% of the time, Pallas kernels for 0%

profile of v5, /device:TPU:0, one launch (start us, length us, event | category | flops | bytes accessed | tf_op | source)
XLA Modules:
  0.0 168.6 jit_solution(3504414248267703167)
XLA Ops:
  2.4 6.8 %collective-permute-start.1 = (bf16[64,1024]{1,0:T(8,128)(2,1)S(1)}, bf16[64,1024]{1,0:T(8,128)(2,1)S(1)}, u32[]{:S(2)}, u32[]{:S(2)}) collective-permute-start(bf16[64,1024]{1,0:T(8,128)(2,1)S(1)} %get-tuple-element.128), channel_id=1, source_target_pairs={{0,2},{1,10},{2,18},{3,26},{4,6},{5,14},{6,22},{7,30},{8,3},{9,11}... | collective-permute-start | bytes 393224 | tf_op jit(solution)/shard_map/cotangent_spread/ppermute | solution.py:59
  15.6 5.6 %collective-permute-done.1 = bf16[64,1024]{1,0:T(8,128)(2,1)S(1)} collective-permute-done((bf16[64,1024]{1,0:T(8,128)(2,1)S(1)}, bf16[64,1024]{1,0:T(8,128)(2,1)S(1)}, u32[]{:S(2)}, u32[]{:S(2)}) %collective-permute-start.1) | collective-permute-done | bytes 131104 | tf_op jit(solution)/shard_map/cotangent_spread/ppermute | solution.py:59
  25.7 4.1 %collective-permute-start.6 = (bf16[128,2048]{1,0:T(8,128)(2,1)S(1)}, bf16[128,2048]{1,0:T(8,128)(2,1)S(1)}, u32[]{:S(2)}, u32[]{:S(2)}) collective-permute-start(bf16[128,2048]{1,0:T(8,128)(2,1)S(1)} %get-tuple-element.51), channel_id=1, source_target_pairs={{0,8},{4,12},{8,16},{12,20},{16,24},{20,28},{1,9},{5,13},{9,17},{1... | collective-permute-start | bytes 1572872 | tf_op jit(solution)/shard_map/hidden_first_up1/ppermute | solution.py:31
  31.2 4.8 %collective-permute-done.3 = bf16[2,64,512]{2,1,0:T(8,128)(2,1)S(1)} collective-permute-done((bf16[2,64,512]{2,1,0:T(8,128)(2,1)S(1)}, bf16[2,64,512]{2,1,0:T(8,128)(2,1)S(1)}, u32[]{:S(2)}, u32[]{:S(2)}) %collective-permute-start.3) | collective-permute-done | bytes 131104 | tf_op jit(solution)/shard_map/cotangent_side/ppermute | solution.py:35
  41.1 2.3 %collective-permute-start.21 = (bf16[2,128,1536]{2,1,0:T(8,128)(2,1)}, bf16[2,128,1536]{2,1,0:T(8,128)(2,1)S(1)}, u32[]{:S(2)}, u32[]{:S(2)}) collective-permute-start(bf16[2,128,1536]{2,1,0:T(8,128)(2,1)} %get-tuple-element.123), channel_id=1, source_target_pairs={{0,8},{4,12},{8,16},{12,20},{16,24},{20,28},{1,9},{5,13},{9,17},{1... | collective-permute-start | bytes 2359304 | tf_op jit(solution)/shard_map/hidden_last_up1/ppermute | solution.py:31
  44.7 2.4 %collective-permute-done.5 = bf16[3,2,1,64,512]{4,3,1,0,2:T(8,128)(2,1)} collective-permute-done((bf16[3,2,1,64,512]{4,3,1,0,2:T(8,128)(2,1)S(1)}, bf16[3,2,1,64,512]{4,3,1,0,2:T(8,128)(2,1)}, u32[]{:S(2)}, u32[]{:S(2)}) %collective-permute-start.5) | collective-permute-done | bytes 393248 | tf_op jit(solution)/shard_map/cotangent_shares/ppermute | solution.py:85
  48.3 3.3 %collective-permute-done.8 = bf16[512,512]{1,0:T(8,128)(2,1)} collective-permute-done((bf16[512,512]{1,0:T(8,128)(2,1)}, bf16[512,512]{1,0:T(8,128)(2,1)}, u32[]{:S(2)}, u32[]{:S(2)}) %collective-permute-start.8) | collective-permute-done | bytes 524320 | tf_op jit(solution)/shard_map/weight_side/ppermute | solution.py:35
  57.1 2.7 %collective-permute-done.21 = bf16[2,128,1536]{2,1,0:T(8,128)(2,1)S(1)} collective-permute-done((bf16[2,128,1536]{2,1,0:T(8,128)(2,1)}, bf16[2,128,1536]{2,1,0:T(8,128)(2,1)S(1)}, u32[]{:S(2)}, u32[]{:S(2)}) %collective-permute-start.21) | collective-permute-done | bytes 786464 | tf_op jit(solution)/shard_map/hidden_last_up1/ppermute | solution.py:31
  60.3 5.8 %collective-permute-done.22 = bf16[2,128,1536]{2,1,0:T(8,128)(2,1)} collective-permute-done((bf16[2,128,1536]{2,1,0:T(8,128)(2,1)}, bf16[2,128,1536]{2,1,0:T(8,128)(2,1)}, u32[]{:S(2)}, u32[]{:S(2)}) %collective-permute-start.22) | collective-permute-done | bytes 786464 | tf_op jit(solution)/shard_map/hidden_last_down1/ppermute | solution.py:31
  71.4 3.6 %collective-permute-start.15 = (f16[2,128,1536]{2,1,0:T(8,128)(2,1)S(1)}, f16[2,128,1536]{2,1,0:T(8,128)(2,1)S(1)}, u32[]{:S(2)}, u32[]{:S(2)}) collective-permute-start(f16[2,128,1536]{2,1,0:T(8,128)(2,1)S(1)} %get-tuple-element.100), channel_id=1, source_target_pairs={{0,8},{4,12},{1,9},{5,13},{2,10},{6,14},{3,11},{7,15}} | collective-permute-start | bytes 2359304 | tf_op jit(solution)/shard_map/dhid_last_up1/ppermute | solution.py:31
  79.2 3.9 %collective-permute-done.10 = bf16[1024,512]{1,0:T(8,128)(2,1)S(1)} collective-permute-done((bf16[1024,512]{1,0:T(8,128)(2,1)S(1)}, bf16[1024,512]{1,0:T(8,128)(2,1)S(1)}, u32[]{:S(2)}, u32[]{:S(2)}) %collective-permute-start.10) | collective-permute-done | bytes 1048608 | tf_op jit(solution)/shard_map/weight_side/ppermute | solution.py:35
  85.3 3.0 %collective-permute-done.15 = f16[2,128,1536]{2,1,0:T(8,128)(2,1)S(1)} collective-permute-done((f16[2,128,1536]{2,1,0:T(8,128)(2,1)S(1)}, f16[2,128,1536]{2,1,0:T(8,128)(2,1)S(1)}, u32[]{:S(2)}, u32[]{:S(2)}) %collective-permute-start.15) | collective-permute-done | bytes 786464 | tf_op jit(solution)/shard_map/dhid_last_up1/ppermute | solution.py:31
  88.3 4.4 %collective-permute-start.13 = (f16[128,2048]{1,0:T(8,128)(2,1)S(1)}, f16[128,2048]{1,0:T(8,128)(2,1)S(1)}, u32[]{:S(2)}, u32[]{:S(2)}) collective-permute-start(f16[128,2048]{1,0:T(8,128)(2,1)S(1)} %get-tuple-element.58), channel_id=1, source_target_pairs={{0,8},{4,12},{1,9},{5,13},{2,10},{6,14},{3,11},{7,15}} | collective-permute-start | bytes 1572872 | tf_op jit(solution)/shard_map/dhid_first_up1/ppermute | solution.py:31
  93.9 5.5 %collective-permute-done.13 = f16[128,2048]{1,0:T(8,128)(2,1)S(1)} collective-permute-done((f16[128,2048]{1,0:T(8,128)(2,1)S(1)}, f16[128,2048]{1,0:T(8,128)(2,1)S(1)}, u32[]{:S(2)}, u32[]{:S(2)}) %collective-permute-start.13) | collective-permute-done | bytes 524320 | tf_op jit(solution)/shard_map/dhid_first_up1/ppermute | solution.py:31
  100.7 4.6 %collective-permute-start.17 = (f16[2,128,1536]{2,1,0:T(8,128)(2,1)S(1)}, f16[2,128,1536]{2,1,0:T(8,128)(2,1)S(1)}, u32[]{:S(2)}, u32[]{:S(2)}) collective-permute-start(f16[2,128,1536]{2,1,0:T(8,128)(2,1)S(1)} %get-tuple-element.62), channel_id=1, source_target_pairs={{0,8},{4,12},{8,16},{12,20},{1,9},{5,13},{9,17},{13,21},{2,10},{6,... | collective-permute-start | bytes 2359304 | tf_op jit(solution)/shard_map/dhid_last_up2/ppermute | solution.py:31
  108.2 7.6 %collective-permute-done.33 = bf16[128,2048]{1,0:T(8,128)(2,1)S(1)} collective-permute-done((bf16[128,2048]{1,0:T(8,128)(2,1)S(1)}, bf16[128,2048]{1,0:T(8,128)(2,1)S(1)}, u32[]{:S(2)}, u32[]{:S(2)}) %collective-permute-start.33) | collective-permute-done | bytes 524320 | tf_op jit(solution)/shard_map/hidden_first_down3/ppermute | solution.py:31
  118.2 4.9 %collective-permute-start.27 = (f16[2,128,1536]{2,1,0:T(8,128)(2,1)S(1)}, f16[2,128,1536]{2,1,0:T(8,128)(2,1)S(1)}, u32[]{:S(2)}, u32[]{:S(2)}) collective-permute-start(f16[2,128,1536]{2,1,0:T(8,128)(2,1)S(1)} %get-tuple-element.96), channel_id=1, source_target_pairs={{0,8},{4,12},{8,16},{12,20},{16,24},{20,28},{1,9},{5,13},{9,17},{1... | collective-permute-start | bytes 2359304 | tf_op jit(solution)/shard_map/dhid_last_up3/ppermute | solution.py:31
  124.4 4.7 %collective-permute-start.19 = (f16[128,2048]{1,0:T(8,128)(2,1)S(1)}, f16[128,2048]{1,0:T(8,128)(2,1)S(1)}, u32[]{:S(2)}, u32[]{:S(2)}) collective-permute-start(f16[128,2048]{1,0:T(8,128)(2,1)S(1)} %get-tuple-element.66), channel_id=1, source_target_pairs={{0,8},{4,12},{8,16},{12,20},{1,9},{5,13},{9,17},{13,21},{2,10},{6,... | collective-permute-start | bytes 1572872 | tf_op jit(solution)/shard_map/dhid_first_up2/ppermute | solution.py:31
  129.1 3.5 %collective-permute-done.26 = bf16[2,128,1536]{2,1,0:T(8,128)(2,1)S(1)} collective-permute-done((bf16[2,128,1536]{2,1,0:T(8,128)(2,1)S(1)}, bf16[2,128,1536]{2,1,0:T(8,128)(2,1)S(1)}, u32[]{:S(2)}, u32[]{:S(2)}) %collective-permute-start.26) | collective-permute-done | bytes 786464 | tf_op jit(solution)/shard_map/hidden_last_down3/ppermute | solution.py:31
  136.7 7.6 %collective-permute-done.19 = f16[128,2048]{1,0:T(8,128)(2,1)S(1)} collective-permute-done((f16[128,2048]{1,0:T(8,128)(2,1)S(1)}, f16[128,2048]{1,0:T(8,128)(2,1)S(1)}, u32[]{:S(2)}, u32[]{:S(2)}) %collective-permute-start.19) | collective-permute-done | bytes 524320 | tf_op jit(solution)/shard_map/dhid_first_up2/ppermute | solution.py:31
  145.7 6.3 %collective-permute-start.29 = (f16[128,2048]{1,0:T(8,128)(2,1)}, f16[128,2048]{1,0:T(8,128)(2,1)S(1)}, u32[]{:S(2)}, u32[]{:S(2)}) collective-permute-start(f16[128,2048]{1,0:T(8,128)(2,1)} %get-tuple-element.79), channel_id=1, source_target_pairs={{0,8},{4,12},{8,16},{12,20},{16,24},{20,28},{1,9},{5,13},{9,17},{1... | collective-permute-start | bytes 1572872 | tf_op jit(solution)/shard_map/dhid_first_up3/ppermute | solution.py:31
  153.7 4.9 %collective-permute-start.31 = (f16[128,1536]{1,0:T(8,128)(2,1)S(1)}, f16[128,1536]{1,0:T(8,128)(2,1)S(1)}, u32[]{:S(2)}, u32[]{:S(2)}) collective-permute-start(f16[128,1536]{1,0:T(8,128)(2,1)S(1)} %fusion.37), channel_id=1, source_target_pairs={{0,4},{4,0},{8,12},{12,8},{16,20},{20,16},{24,28},{28,24},{1,5},{5... | collective-permute-start | bytes 1179656 | tf_op jit(solution)/shard_map/dhid_last_side/ppermute | solution.py:35
  158.6 2.4 %bitcast_multiply_fusion = f32[2048,512]{1,0:T(8,128)S(1)} fusion(bf16[4,1,128,512]{3,2,1,0:T(8,128)(2,1)S(1)} %bitcast.128, bf16[4,1,128,512]{3,2,1,0:T(8,128)(2,1)S(1)} %bitcast.124, bf16[4,1,128,2048]{3,2,0,1:T(8,128)(2,1)S(1)} %bitcast.134, bf16[4,1,128,2048]{3,2,0,1:T(8,128)(2,1)S(1)} %get-tuple-element.111), kind=kOutput, calls=%fused_computation.3 | convolution fusion | flops 2151153664 | bytes 9437184 | tf_op jit(solution)/shard_map/kstc,kstf->cf/dot_general | solution.py:168
  161.1 3.9 %pad_maximum_fusion = f32[3584,512]{1,0:T(8,128)} fusion(f32[1536,512]{1,0:T(8,128)S(1)} %fusion.2, f32[2048,512]{1,0:T(8,128)S(1)} %bitcast_multiply_fusion), kind=kLoop, calls=%fused_computation | loop fusion | flops 1835008 | bytes 14680064 | tf_op jit(solution)/shard_map/concatenate | solution.py:171
  (104 shorter events, 58.5 us)
Async XLA Ops:
  2.4 18.8 %collective-permute-start.1 = (bf16[64,1024]{1,0:T(8,128)(2,1)S(1)}, bf16[64,1024]{1,0:T(8,128)(2,1)S(1)}, u32[]{:S(2)}, u32[]{:S(2)}) collective-permute-start(bf16[64,1024]{1,0:T(8,128)(2,1)S(1)} %get-tuple-element.128), channel_id=1, source_target_pairs={{0,2},{1,10},{2,18},{3,26},{4,6},{5,14},{6,22},{7,30},{8,3},{9,11}... | collective-permute-start | bytes 393224 | tf_op jit(solution)/shard_map/cotangent_spread/ppermute | solution.py:59
  15.1 20.9 %collective-permute-start.4 = (bf16[512,512]{1,0:T(8,128)(2,1)}, bf16[512,512]{1,0:T(8,128)(2,1)S(1)}, u32[]{:S(2)}, u32[]{:S(2)}) collective-permute-start(bf16[512,512]{1,0:T(8,128)(2,1)} %get-tuple-element.108), channel_id=1, source_target_pairs={{0,4},{4,0},{8,12},{12,8},{16,20},{20,16},{24,28},{28,24},{1,5},{5... | collective-permute-start | bytes 1572872 | tf_op jit(solution)/shard_map/weight_side/ppermute | solution.py:35
  25.7 17.6 %collective-permute-start.6 = (bf16[128,2048]{1,0:T(8,128)(2,1)S(1)}, bf16[128,2048]{1,0:T(8,128)(2,1)S(1)}, u32[]{:S(2)}, u32[]{:S(2)}) collective-permute-start(bf16[128,2048]{1,0:T(8,128)(2,1)S(1)} %get-tuple-element.51), channel_id=1, source_target_pairs={{0,8},{4,12},{8,16},{12,20},{16,24},{20,28},{1,9},{5,13},{9,17},{1... | collective-permute-start | bytes 1572872 | tf_op jit(solution)/shard_map/hidden_first_up1/ppermute | solution.py:31
  29.9 14.8 %collective-permute-start.7 = (bf16[128,2048]{1,0:T(8,128)(2,1)S(1)}, bf16[128,2048]{1,0:T(8,128)(2,1)}, u32[]{:S(2)}, u32[]{:S(2)}) collective-permute-start(bf16[128,2048]{1,0:T(8,128)(2,1)S(1)} %get-tuple-element.51), channel_id=1, source_target_pairs={{8,0},{12,4},{16,8},{20,12},{24,16},{28,20},{9,1},{13,5},{17,9},{2... | collective-permute-start | bytes 1572872 | tf_op jit(solution)/shard_map/hidden_first_down1/ppermute | solution.py:31
  41.1 18.7 %collective-permute-start.21 = (bf16[2,128,1536]{2,1,0:T(8,128)(2,1)}, bf16[2,128,1536]{2,1,0:T(8,128)(2,1)S(1)}, u32[]{:S(2)}, u32[]{:S(2)}) collective-permute-start(bf16[2,128,1536]{2,1,0:T(8,128)(2,1)} %get-tuple-element.123), channel_id=1, source_target_pairs={{0,8},{4,12},{8,16},{12,20},{16,24},{20,28},{1,9},{5,13},{9,17},{1... | collective-permute-start | bytes 2359304 | tf_op jit(solution)/shard_map/hidden_last_up1/ppermute | solution.py:31
  43.4 22.7 %collective-permute-start.22 = (bf16[2,128,1536]{2,1,0:T(8,128)(2,1)}, bf16[2,128,1536]{2,1,0:T(8,128)(2,1)}, u32[]{:S(2)}, u32[]{:S(2)}) collective-permute-start(bf16[2,128,1536]{2,1,0:T(8,128)(2,1)} %get-tuple-element.123), channel_id=1, source_target_pairs={{8,0},{12,4},{16,8},{20,12},{24,16},{28,20},{9,1},{13,5},{17,9},{2... | collective-permute-start | bytes 2359304 | tf_op jit(solution)/shard_map/hidden_last_down1/ppermute | solution.py:31
  51.6 14.5 %collective-permute-start.9 = (bf16[3,2,2,64,512]{4,3,1,0,2:T(8,128)(2,1)S(1)}, bf16[3,2,2,64,512]{4,3,1,0,2:T(8,128)(2,1)}, u32[]{:S(2)}, u32[]{:S(2)}) collective-permute-start(bf16[3,2,2,64,512]{4,3,1,0,2:T(8,128)(2,1)S(1)} %maximum_bitcast_fusion), channel_id=1, source_target_pairs={{0,1},{1,0},{2,3},{3,2},{4,5},{5,4},{6,7},{7,6},{8,9},{9,8},{10,11... | collective-permute-start | bytes 2359304 | tf_op jit(solution)/shard_map/cotangent_core/ppermute | solution.py:92
  54.0 21.8 %collective-permute-start.11 = (bf16[128,2048]{1,0:T(8,128)(2,1)}, bf16[128,2048]{1,0:T(8,128)(2,1)S(1)}, u32[]{:S(2)}, u32[]{:S(2)}) collective-permute-start(bf16[128,2048]{1,0:T(8,128)(2,1)} %copy-done.5), channel_id=1, source_target_pairs={{8,16},{12,20},{16,24},{20,28},{9,17},{13,21},{17,25},{21,29},{10,... | collective-permute-start | bytes 1572872 | tf_op jit(solution)/shard_map/hidden_first_up2/ppermute | solution.py:31
  54.7 21.1 %collective-permute-start.12 = (bf16[128,2048]{1,0:T(8,128)(2,1)}, bf16[128,2048]{1,0:T(8,128)(2,1)S(1)}, u32[]{:S(2)}, u32[]{:S(2)}) collective-permute-start(bf16[128,2048]{1,0:T(8,128)(2,1)} %collective-permute-done.7), channel_id=1, source_target_pairs={{8,0},{12,4},{16,8},{20,12},{9,1},{13,5},{17,9},{21,13},{10,2},{14... | collective-permute-start | bytes 1572872 | tf_op jit(solution)/shard_map/hidden_first_down2/ppermute | solution.py:31
  59.8 23.3 %collective-permute-start.10 = (bf16[1024,512]{1,0:T(8,128)(2,1)S(1)}, bf16[1024,512]{1,0:T(8,128)(2,1)S(1)}, u32[]{:S(2)}, u32[]{:S(2)}) collective-permute-start(bf16[1024,512]{1,0:T(8,128)(2,1)S(1)} %slice.79), channel_id=1, source_target_pairs={{0,4},{4,0},{8,12},{12,8},{16,20},{20,16},{24,28},{28,24},{1,5},{5... | collective-permute-start | bytes 3145736 | tf_op jit(solution)/shard_map/weight_side/ppermute | solution.py:35
  71.4 16.9 %collective-permute-start.15 = (f16[2,128,1536]{2,1,0:T(8,128)(2,1)S(1)}, f16[2,128,1536]{2,1,0:T(8,128)(2,1)S(1)}, u32[]{:S(2)}, u32[]{:S(2)}) collective-permute-start(f16[2,128,1536]{2,1,0:T(8,128)(2,1)S(1)} %get-tuple-element.100), channel_id=1, source_target_pairs={{0,8},{4,12},{1,9},{5,13},{2,10},{6,14},{3,11},{7,15}} | collective-permute-start | bytes 2359304 | tf_op jit(solution)/shard_map/dhid_last_up1/ppermute | solution.py:31
  75.0 17.7 %collective-permute-start.16 = (f16[2,128,1536]{2,1,0:T(8,128)(2,1)S(1)}, f16[2,128,1536]{2,1,0:T(8,128)(2,1)S(1)}, u32[]{:S(2)}, u32[]{:S(2)}) collective-permute-start(f16[2,128,1536]{2,1,0:T(8,128)(2,1)S(1)} %get-tuple-element.99), channel_id=1, source_target_pairs={{24,16},{28,20},{25,17},{29,21},{26,18},{30,22},{27,19},{31,23}} | collective-permute-start | bytes 2359304 | tf_op jit(solution)/shard_map/dhid_last_down1/ppermute | solution.py:31
  75.8 29.5 %collective-permute-start.23 = (bf16[2,128,1536]{2,1,0:T(8,128)(2,1)S(1)}, bf16[2,128,1536]{2,1,0:T(8,128)(2,1)S(1)}, u32[]{:S(2)}, u32[]{:S(2)}) collective-permute-start(bf16[2,128,1536]{2,1,0:T(8,128)(2,1)S(1)} %collective-permute-done.21), channel_id=1, source_target_pairs={{8,16},{12,20},{16,24},{20,28},{9,17},{13,21},{17,25},{21,29},{10,... | collective-permute-start | bytes 2359304 | tf_op jit(solution)/shard_map/hidden_last_up2/ppermute | solution.py:31
  76.5 29.5 %collective-permute-start.24 = (bf16[2,128,1536]{2,1,0:T(8,128)(2,1)}, bf16[2,128,1536]{2,1,0:T(8,128)(2,1)S(1)}, u32[]{:S(2)}, u32[]{:S(2)}) collective-permute-start(bf16[2,128,1536]{2,1,0:T(8,128)(2,1)} %collective-permute-done.22), channel_id=1, source_target_pairs={{8,0},{12,4},{16,8},{20,12},{9,1},{13,5},{17,9},{21,13},{10,2},{14... | collective-permute-start | bytes 2359304 | tf_op jit(solution)/shard_map/hidden_last_down2/ppermute | solution.py:31
  83.1 23.8 %collective-permute-start.32 = (bf16[128,2048]{1,0:T(8,128)(2,1)S(1)}, bf16[128,2048]{1,0:T(8,128)(2,1)S(1)}, u32[]{:S(2)}, u32[]{:S(2)}) collective-permute-start(bf16[128,2048]{1,0:T(8,128)(2,1)S(1)} %collective-permute-done.11), channel_id=1, source_target_pairs={{16,24},{20,28},{17,25},{21,29},{18,26},{22,30},{19,27},{23,31}} | collective-permute-start | bytes 1572872 | tf_op jit(solution)/shard_map/hidden_first_up3/ppermute | solution.py:31
  99.4 16.4 %collective-permute-start.33 = (bf16[128,2048]{1,0:T(8,128)(2,1)S(1)}, bf16[128,2048]{1,0:T(8,128)(2,1)S(1)}, u32[]{:S(2)}, u32[]{:S(2)}) collective-permute-start(bf16[128,2048]{1,0:T(8,128)(2,1)S(1)} %collective-permute-done.12), channel_id=1, source_target_pairs={{8,0},{12,4},{9,1},{13,5},{10,2},{14,6},{11,3},{15,7}} | collective-permute-start | bytes 1572872 | tf_op jit(solution)/shard_map/hidden_first_down3/ppermute | solution.py:31
  100.7 17.0 %collective-permute-start.17 = (f16[2,128,1536]{2,1,0:T(8,128)(2,1)S(1)}, f16[2,128,1536]{2,1,0:T(8,128)(2,1)S(1)}, u32[]{:S(2)}, u32[]{:S(2)}) collective-permute-start(f16[2,128,1536]{2,1,0:T(8,128)(2,1)S(1)} %get-tuple-element.62), channel_id=1, source_target_pairs={{0,8},{4,12},{8,16},{12,20},{1,9},{5,13},{9,17},{13,21},{2,10},{6,... | collective-permute-start | bytes 2359304 | tf_op jit(solution)/shard_map/dhid_last_up2/ppermute | solution.py:31
  106.0 18.4 %collective-permute-start.25 = (bf16[2,128,1536]{2,1,0:T(8,128)(2,1)S(1)}, bf16[2,128,1536]{2,1,0:T(8,128)(2,1)S(1)}, u32[]{:S(2)}, u32[]{:S(2)}) collective-permute-start(bf16[2,128,1536]{2,1,0:T(8,128)(2,1)S(1)} %collective-permute-done.23), channel_id=1, source_target_pairs={{16,24},{20,28},{17,25},{21,29},{18,26},{22,30},{19,27},{23,31}} | collective-permute-start | bytes 2359304 | tf_op jit(solution)/shard_map/hidden_last_up3/ppermute | solution.py:31
  106.9 25.7 %collective-permute-start.26 = (bf16[2,128,1536]{2,1,0:T(8,128)(2,1)S(1)}, bf16[2,128,1536]{2,1,0:T(8,128)(2,1)S(1)}, u32[]{:S(2)}, u32[]{:S(2)}) collective-permute-start(bf16[2,128,1536]{2,1,0:T(8,128)(2,1)S(1)} %collective-permute-done.24), channel_id=1, source_target_pairs={{8,0},{12,4},{9,1},{13,5},{10,2},{14,6},{11,3},{15,7}} | collective-permute-start | bytes 2359304 | tf_op jit(solution)/shard_map/hidden_last_down3/ppermute | solution.py:31
  117.3 41.3 %collective-permute-start.34 = (bf16[4,128,2048]{2,1,0:T(8,128)(2,1)S(1)}, bf16[4,128,2048]{2,1,0:T(8,128)(2,1)S(1)}, u32[]{:S(2)}, u32[]{:S(2)}) collective-permute-start(bf16[4,128,2048]{2,1,0:T(8,128)(2,1)S(1)} %get-tuple-element.88), channel_id=1, source_target_pairs={{0,4},{4,0},{8,12},{12,8},{16,20},{20,16},{24,28},{28,24},{1,5},{5... | collective-permute-start | bytes 6291464 | tf_op jit(solution)/shard_map/hidden_first_side/ppermute | solution.py:35
  118.2 27.5 %collective-permute-start.27 = (f16[2,128,1536]{2,1,0:T(8,128)(2,1)S(1)}, f16[2,128,1536]{2,1,0:T(8,128)(2,1)S(1)}, u32[]{:S(2)}, u32[]{:S(2)}) collective-permute-start(f16[2,128,1536]{2,1,0:T(8,128)(2,1)S(1)} %get-tuple-element.96), channel_id=1, source_target_pairs={{0,8},{4,12},{8,16},{12,20},{16,24},{20,28},{1,9},{5,13},{9,17},{1... | collective-permute-start | bytes 2359304 | tf_op jit(solution)/shard_map/dhid_last_up3/ppermute | solution.py:31
  123.1 22.6 %collective-permute-start.28 = (f16[2,128,1536]{2,1,0:T(8,128)(2,1)S(1)}, f16[2,128,1536]{2,1,0:T(8,128)(2,1)S(1)}, u32[]{:S(2)}, u32[]{:S(2)}) collective-permute-start(f16[2,128,1536]{2,1,0:T(8,128)(2,1)S(1)} %get-tuple-element.95), channel_id=1, source_target_pairs={{8,0},{12,4},{16,8},{20,12},{24,16},{28,20},{9,1},{13,5},{17,9},{2... | collective-permute-start | bytes 2359304 | tf_op jit(solution)/shard_map/dhid_last_down3/ppermute | solution.py:31
  124.4 19.9 %collective-permute-start.19 = (f16[128,2048]{1,0:T(8,128)(2,1)S(1)}, f16[128,2048]{1,0:T(8,128)(2,1)S(1)}, u32[]{:S(2)}, u32[]{:S(2)}) collective-permute-start(f16[128,2048]{1,0:T(8,128)(2,1)S(1)} %get-tuple-element.66), channel_id=1, source_target_pairs={{0,8},{4,12},{8,16},{12,20},{1,9},{5,13},{9,17},{13,21},{2,10},{6,... | collective-permute-start | bytes 1572872 | tf_op jit(solution)/shard_map/dhid_first_up2/ppermute | solution.py:31
  145.7 19.3 %collective-permute-start.29 = (f16[128,2048]{1,0:T(8,128)(2,1)}, f16[128,2048]{1,0:T(8,128)(2,1)S(1)}, u32[]{:S(2)}, u32[]{:S(2)}) collective-permute-start(f16[128,2048]{1,0:T(8,128)(2,1)} %get-tuple-element.79), channel_id=1, source_target_pairs={{0,8},{4,12},{8,16},{12,20},{16,24},{20,28},{1,9},{5,13},{9,17},{1... | collective-permute-start | bytes 1572872 | tf_op jit(solution)/shard_map/dhid_first_up3/ppermute | solution.py:31
  (19 other events, 185.3 us)

commit v6 on v5

--- a/solution.py
+++ b/solution.py
@@ -78,7 +78,7 @@
     weight_other.append(across("weight_side", after(weight_first[bounds[1] :], weight_other[1])))
     last_up, last_down = together(last_up, last_down)
 
-    own = after(jnp.stack([mine, other, theirs])[:, :, None], weight_other[0])
+    own = after(jnp.stack([mine, other, theirs])[:, :, None], weight_other[0], both_last)
     bit = tensor // 2
     while bit > 1:
         with jax.named_scope("cotangent_shares"):

time: 170 us -> 177 us (1.041)
  waiting for transfers between devices: 57.7 us -> 68.2 us
  other arithmetic: 19.7 us -> 16.8 us
    ppermute x7, waiting for transfers between devices: 13.9 us -> 19.3 us  [across(): return lax.ppermute(value, 'dp', [(at, at ^ 1) for at in range(dp)])]
    ppermute x24, waiting for transfers between devices: 35.7 us -> 39.4 us  [along(): return lax.ppermute(value, 'dp', pairs)]
    ppermute x1, waiting for transfers between devices: 2.41 us -> 4.55 us  [shards(): lax.ppermute(own, 'tensor', [(at, at ^ bit) for at in range(tensor)])]
    unnamed x18 -> x12, local copies, waits for them, and re-layouts: 5.84 us -> 3.97 us
  transfers between devices with their start and end apart: 35 -> 35, of which waited for: 13 -> 14; matrix products, arithmetic and copies ran while one was open for 19% -> 17% of each run, Pallas kernels for 0% -> 0%
where the time goes in v6:
time: 177 us; the launch traced here: 176 us
  starting transfers between devices  70.9 us (40%)
  waiting for transfers between devices  68.2 us (39%)
  other arithmetic  16.8 us (9%)
  local copies, waits for them, and re-layouts  9.41 us (5%)
  matrix products  8.8 us (5%)
    ppermute x24, starting transfers between devices, along(): return lax.ppermute(value, 'dp', pairs)  52.2 us
    ppermute x24, waiting for transfers between devices, along(): return lax.ppermute(value, 'dp', pairs)  39.4 us
    ppermute x7, waiting for transfers between devices, across(): return lax.ppermute(value, 'dp', [(at, at ^ 1) for at in range(dp)])  19.3 us
    ppermute x7, starting transfers between devices, across(): return lax.ppermute(value, 'dp', [(at, at ^ 1) for at in range(dp)])  9.95 us
    ppermute x2, starting transfers between devices, shards(): arrived.append(lax.ppermute(piece, ('dp', 'tensor'), pairs))  7.46 us
    ppermute x2, waiting for transfers between devices, shards(): arrived.append(lax.ppermute(piece, ('dp', 'tensor'), pairs))  4.94 us
    ppermute x1, waiting for transfers between devices, shards(): lax.ppermute(own, 'tensor', [(at, at ^ bit) for at in range(tensor)])  4.55 us
    dot_general x3, matrix products, product(): jnp.einsum('...f,hf->...h', left, right, preferred_element_type=jnp.float32)  4.46 us
  transfers between devices with their start and end apart: 35, of which 14 were waited for; matrix products, arithmetic and copies ran while one was open for 17% of the time, Pallas kernels for 0%

profile of v6, /device:TPU:0, one launch (start us, length us, event | category | flops | bytes accessed | tf_op | source)
XLA Modules:
  0.0 175.5 jit_solution(8377997350728084573)
XLA Ops:
  2.4 6.8 %collective-permute-start.1 = (bf16[64,1024]{1,0:T(8,128)(2,1)S(1)}, bf16[64,1024]{1,0:T(8,128)(2,1)S(1)}, u32[]{:S(2)}, u32[]{:S(2)}) collective-permute-start(bf16[64,1024]{1,0:T(8,128)(2,1)S(1)} %get-tuple-element.128), channel_id=1, source_target_pairs={{0,2},{1,10},{2,18},{3,26},{4,6},{5,14},{6,22},{7,30},{8,3},{9,11}... | collective-permute-start | bytes 393224 | tf_op jit(solution)/shard_map/cotangent_spread/ppermute | solution.py:59
  9.2 2.0 %fusion.16 = bf16[128,3584]{1,0:T(8,128)(2,1)S(1)} fusion(bf16[128,3584]{1,0:T(8,128)(2,1)} %param.6, bf16[128,3584]{1,0:T(8,128)(2,1)} %param.5), kind=kLoop, calls=%fused_computation.26 | loop fusion | flops 3670016 | bytes 2752512 | tf_op jit(solution)/shard_map/convert_element_type | solution.py:41
  13.5 2.1 %fusion.46 = (bf16[512,512]{1,0:T(8,128)(2,1)}, bf16[512,512]{1,0:T(8,128)(2,1)S(1)}) fusion(bf16[3584,512]{1,0:T(8,128)(2,1)} %param.7), kind=kLoop, calls=%fused_computation.108 | loop fusion | bytes 2097152 | tf_op jit(solution)/shard_map/slice | solution.py:77
  16.3 4.9 %collective-permute-done.1 = bf16[64,1024]{1,0:T(8,128)(2,1)S(1)} collective-permute-done((bf16[64,1024]{1,0:T(8,128)(2,1)S(1)}, bf16[64,1024]{1,0:T(8,128)(2,1)S(1)}, u32[]{:S(2)}, u32[]{:S(2)}) %collective-permute-start.1) | collective-permute-done | bytes 131104 | tf_op jit(solution)/shard_map/cotangent_spread/ppermute | solution.py:59
  21.2 2.9 %collective-permute-start.6 = (bf16[128,2048]{1,0:T(8,128)(2,1)S(1)}, bf16[128,2048]{1,0:T(8,128)(2,1)}, u32[]{:S(2)}, u32[]{:S(2)}) collective-permute-start(bf16[128,2048]{1,0:T(8,128)(2,1)S(1)} %get-tuple-element.51), channel_id=1, source_target_pairs={{0,8},{4,12},{8,16},{12,20},{16,24},{20,28},{1,9},{5,13},{9,17},{1... | collective-permute-start | bytes 1572872 | tf_op jit(solution)/shard_map/hidden_first_up1/ppermute | solution.py:31
  28.5 8.3 %collective-permute-done.3 = bf16[2,64,512]{2,1,0:T(8,128)(2,1)S(1)} collective-permute-done((bf16[2,64,512]{2,1,0:T(8,128)(2,1)S(1)}, bf16[2,64,512]{2,1,0:T(8,128)(2,1)S(1)}, u32[]{:S(2)}, u32[]{:S(2)}) %collective-permute-start.3) | collective-permute-done | bytes 131104 | tf_op jit(solution)/shard_map/cotangent_side/ppermute | solution.py:35
  39.7 2.3 %collective-permute-start.21 = (bf16[2,128,1536]{2,1,0:T(8,128)(2,1)}, bf16[2,128,1536]{2,1,0:T(8,128)(2,1)S(1)}, u32[]{:S(2)}, u32[]{:S(2)}) collective-permute-start(bf16[2,128,1536]{2,1,0:T(8,128)(2,1)} %get-tuple-element.123), channel_id=1, source_target_pairs={{0,8},{4,12},{8,16},{12,20},{16,24},{20,28},{1,9},{5,13},{9,17},{1... | collective-permute-start | bytes 2359304 | tf_op jit(solution)/shard_map/hidden_last_up1/ppermute | solution.py:31
  43.3 4.5 %collective-permute-done.5 = bf16[3,2,1,64,512]{4,3,1,0,2:T(8,128)(2,1)S(1)} collective-permute-done((bf16[3,2,1,64,512]{4,3,1,0,2:T(8,128)(2,1)S(1)}, bf16[3,2,1,64,512]{4,3,1,0,2:T(8,128)(2,1)S(1)}, u32[]{:S(2)}, u32[]{:S(2)}) %collective-permute-start.5) | collective-permute-done | bytes 393248 | tf_op jit(solution)/shard_map/cotangent_shares/ppermute | solution.py:85
  48.0 4.5 %collective-permute-done.8 = bf16[512,512]{1,0:T(8,128)(2,1)} collective-permute-done((bf16[512,512]{1,0:T(8,128)(2,1)}, bf16[512,512]{1,0:T(8,128)(2,1)}, u32[]{:S(2)}, u32[]{:S(2)}) %collective-permute-start.8) | collective-permute-done | bytes 524320 | tf_op jit(solution)/shard_map/weight_side/ppermute | solution.py:35
  59.6 4.1 %collective-permute-done.22 = bf16[2,128,1536]{2,1,0:T(8,128)(2,1)} collective-permute-done((bf16[2,128,1536]{2,1,0:T(8,128)(2,1)}, bf16[2,128,1536]{2,1,0:T(8,128)(2,1)}, u32[]{:S(2)}, u32[]{:S(2)}) %collective-permute-start.22) | collective-permute-done | bytes 786464 | tf_op jit(solution)/shard_map/hidden_last_down1/ppermute | solution.py:31
  69.1 3.4 %collective-permute-start.15 = (f16[2,128,1536]{2,1,0:T(8,128)(2,1)S(1)}, f16[2,128,1536]{2,1,0:T(8,128)(2,1)S(1)}, u32[]{:S(2)}, u32[]{:S(2)}) collective-permute-start(f16[2,128,1536]{2,1,0:T(8,128)(2,1)S(1)} %get-tuple-element.100), channel_id=1, source_target_pairs={{0,8},{4,12},{1,9},{5,13},{2,10},{6,14},{3,11},{7,15}} | collective-permute-start | bytes 2359304 | tf_op jit(solution)/shard_map/dhid_last_up1/ppermute | solution.py:31
  77.1 6.5 %collective-permute-done.10 = bf16[1024,512]{1,0:T(8,128)(2,1)S(1)} collective-permute-done((bf16[1024,512]{1,0:T(8,128)(2,1)S(1)}, bf16[1024,512]{1,0:T(8,128)(2,1)S(1)}, u32[]{:S(2)}, u32[]{:S(2)}) %collective-permute-start.10) | collective-permute-done | bytes 1048608 | tf_op jit(solution)/shard_map/weight_side/ppermute | solution.py:35
  86.9 4.4 %collective-permute-start.13 = (f16[128,2048]{1,0:T(8,128)(2,1)S(1)}, f16[128,2048]{1,0:T(8,128)(2,1)S(1)}, u32[]{:S(2)}, u32[]{:S(2)}) collective-permute-start(f16[128,2048]{1,0:T(8,128)(2,1)S(1)} %get-tuple-element.58), channel_id=1, source_target_pairs={{0,8},{4,12},{1,9},{5,13},{2,10},{6,14},{3,11},{7,15}} | collective-permute-start | bytes 1572872 | tf_op jit(solution)/shard_map/dhid_first_up1/ppermute | solution.py:31
  92.4 9.0 %collective-permute-done.13 = f16[128,2048]{1,0:T(8,128)(2,1)S(1)} collective-permute-done((f16[128,2048]{1,0:T(8,128)(2,1)S(1)}, f16[128,2048]{1,0:T(8,128)(2,1)S(1)}, u32[]{:S(2)}, u32[]{:S(2)}) %collective-permute-start.13) | collective-permute-done | bytes 524320 | tf_op jit(solution)/shard_map/dhid_first_up1/ppermute | solution.py:31
  102.7 4.6 %collective-permute-start.17 = (f16[2,128,1536]{2,1,0:T(8,128)(2,1)S(1)}, f16[2,128,1536]{2,1,0:T(8,128)(2,1)S(1)}, u32[]{:S(2)}, u32[]{:S(2)}) collective-permute-start(f16[2,128,1536]{2,1,0:T(8,128)(2,1)S(1)} %get-tuple-element.62), channel_id=1, source_target_pairs={{0,8},{4,12},{8,16},{12,20},{1,9},{5,13},{9,17},{13,21},{2,10},{6,... | collective-permute-start | bytes 2359304 | tf_op jit(solution)/shard_map/dhid_last_up2/ppermute | solution.py:31
  110.2 8.0 %collective-permute-done.33 = bf16[128,2048]{1,0:T(8,128)(2,1)S(1)} collective-permute-done((bf16[128,2048]{1,0:T(8,128)(2,1)S(1)}, bf16[128,2048]{1,0:T(8,128)(2,1)S(1)}, u32[]{:S(2)}, u32[]{:S(2)}) %collective-permute-start.33) | collective-permute-done | bytes 524320 | tf_op jit(solution)/shard_map/hidden_first_down3/ppermute | solution.py:31
  122.6 7.4 %collective-permute-start.27 = (f16[2,128,1536]{2,1,0:T(8,128)(2,1)S(1)}, f16[2,128,1536]{2,1,0:T(8,128)(2,1)S(1)}, u32[]{:S(2)}, u32[]{:S(2)}) collective-permute-start(f16[2,128,1536]{2,1,0:T(8,128)(2,1)S(1)} %get-tuple-element.96), channel_id=1, source_target_pairs={{0,8},{4,12},{8,16},{12,20},{16,24},{20,28},{1,9},{5,13},{9,17},{1... | collective-permute-start | bytes 2359304 | tf_op jit(solution)/shard_map/dhid_last_up3/ppermute | solution.py:31
  131.3 4.7 %collective-permute-start.19 = (f16[128,2048]{1,0:T(8,128)(2,1)S(1)}, f16[128,2048]{1,0:T(8,128)(2,1)S(1)}, u32[]{:S(2)}, u32[]{:S(2)}) collective-permute-start(f16[128,2048]{1,0:T(8,128)(2,1)S(1)} %get-tuple-element.66), channel_id=1, source_target_pairs={{0,8},{4,12},{8,16},{12,20},{1,9},{5,13},{9,17},{13,21},{2,10},{6,... | collective-permute-start | bytes 1572872 | tf_op jit(solution)/shard_map/dhid_first_up2/ppermute | solution.py:31
  140.2 14.8 %collective-permute-done.19 = f16[128,2048]{1,0:T(8,128)(2,1)S(1)} collective-permute-done((f16[128,2048]{1,0:T(8,128)(2,1)S(1)}, f16[128,2048]{1,0:T(8,128)(2,1)S(1)}, u32[]{:S(2)}, u32[]{:S(2)}) %collective-permute-start.19) | collective-permute-done | bytes 524320 | tf_op jit(solution)/shard_map/dhid_first_up2/ppermute | solution.py:31
  155.3 6.3 %collective-permute-start.29 = (f16[128,2048]{1,0:T(8,128)(2,1)S(1)}, f16[128,2048]{1,0:T(8,128)(2,1)S(1)}, u32[]{:S(2)}, u32[]{:S(2)}) collective-permute-start(f16[128,2048]{1,0:T(8,128)(2,1)S(1)} %get-tuple-element.79), channel_id=1, source_target_pairs={{0,8},{4,12},{8,16},{12,20},{16,24},{20,28},{1,9},{5,13},{9,17},{1... | collective-permute-start | bytes 1572872 | tf_op jit(solution)/shard_map/dhid_first_up3/ppermute | solution.py:31
  163.4 2.1 %collective-permute-start.31 = (f16[128,1536]{1,0:T(8,128)(2,1)S(1)}, f16[128,1536]{1,0:T(8,128)(2,1)S(1)}, u32[]{:S(2)}, u32[]{:S(2)}) collective-permute-start(f16[128,1536]{1,0:T(8,128)(2,1)S(1)} %fusion.37), channel_id=1, source_target_pairs={{0,4},{4,0},{8,12},{12,8},{16,20},{20,16},{24,28},{28,24},{1,5},{5... | collective-permute-start | bytes 1179656 | tf_op jit(solution)/shard_map/dhid_last_side/ppermute | solution.py:35
  165.5 2.5 %bitcast_multiply_fusion = f32[2048,512]{1,0:T(8,128)S(1)} fusion(bf16[4,1,128,512]{3,2,1,0:T(8,128)(2,1)S(1)} %bitcast.128, bf16[4,1,128,512]{3,2,1,0:T(8,128)(2,1)S(1)} %bitcast.124, bf16[4,1,128,2048]{3,2,0,1:T(8,128)(2,1)S(1)} %bitcast.134, bf16[4,1,128,2048]{3,2,0,1:T(8,128)(2,1)S(1)} %get-tuple-element.111), kind=kOutput, calls=%fused_computation.3 | convolution fusion | flops 2151153664 | bytes 9437184 | tf_op jit(solution)/shard_map/kstc,kstf->cf/dot_general | solution.py:168
  167.9 3.9 %pad_maximum_fusion = f32[3584,512]{1,0:T(8,128)} fusion(f32[1536,512]{1,0:T(8,128)S(1)} %fusion.2, f32[2048,512]{1,0:T(8,128)S(1)} %bitcast_multiply_fusion), kind=kLoop, calls=%fused_computation | loop fusion | flops 1835008 | bytes 14680064 | tf_op jit(solution)/shard_map/concatenate | solution.py:171
  173.3 2.2 %multiply_convert_fusion = (bf16[128,3584]{1,0:T(8,128)(2,1)}, bf16[128,3584]{1,0:T(8,128)(2,1)}) fusion(f32[128,1536]{1,0:T(8,128)S(1)} %fusion.34, f32[128,2048]{1,0:T(8,128)S(1)} %fusion.31, bf16[128,3584]{1,0:T(8,128)(2,1)S(1)} %copy-done.1, bf16[128,3584]{1,0:T(8,128)(2,1)S(1)} %copy-done.2), kind=kLoop, calls=%fused_computation.35 | loop fusion | flops 7798784 | bytes 5505024 | tf_op jit(solution)/shard_map/convert_element_type | solution.py:178
  (98 shorter events, 51.9 us)
Async XLA Ops:
  2.4 18.8 %collective-permute-start.1 = (bf16[64,1024]{1,0:T(8,128)(2,1)S(1)}, bf16[64,1024]{1,0:T(8,128)(2,1)S(1)}, u32[]{:S(2)}, u32[]{:S(2)}) collective-permute-start(bf16[64,1024]{1,0:T(8,128)(2,1)S(1)} %get-tuple-element.128), channel_id=1, source_target_pairs={{0,2},{1,10},{2,18},{3,26},{4,6},{5,14},{6,22},{7,30},{8,3},{9,11}... | collective-permute-start | bytes 393224 | tf_op jit(solution)/shard_map/cotangent_spread/ppermute | solution.py:59
  15.6 21.3 %collective-permute-start.4 = (bf16[512,512]{1,0:T(8,128)(2,1)S(1)}, bf16[512,512]{1,0:T(8,128)(2,1)S(1)}, u32[]{:S(2)}, u32[]{:S(2)}) collective-permute-start(bf16[512,512]{1,0:T(8,128)(2,1)S(1)} %get-tuple-element.108), channel_id=1, source_target_pairs={{0,4},{4,0},{8,12},{12,8},{16,20},{20,16},{24,28},{28,24},{1,5},{5... | collective-permute-start | bytes 1572872 | tf_op jit(solution)/shard_map/weight_side/ppermute | solution.py:35
  21.2 20.8 %collective-permute-start.6 = (bf16[128,2048]{1,0:T(8,128)(2,1)S(1)}, bf16[128,2048]{1,0:T(8,128)(2,1)}, u32[]{:S(2)}, u32[]{:S(2)}) collective-permute-start(bf16[128,2048]{1,0:T(8,128)(2,1)S(1)} %get-tuple-element.51), channel_id=1, source_target_pairs={{0,8},{4,12},{8,16},{12,20},{16,24},{20,28},{1,9},{5,13},{9,17},{1... | collective-permute-start | bytes 1572872 | tf_op jit(solution)/shard_map/hidden_first_up1/ppermute | solution.py:31
  24.1 19.2 %collective-permute-start.7 = (bf16[128,2048]{1,0:T(8,128)(2,1)S(1)}, bf16[128,2048]{1,0:T(8,128)(2,1)}, u32[]{:S(2)}, u32[]{:S(2)}) collective-permute-start(bf16[128,2048]{1,0:T(8,128)(2,1)S(1)} %get-tuple-element.51), channel_id=1, source_target_pairs={{8,0},{12,4},{16,8},{20,12},{24,16},{28,20},{9,1},{13,5},{17,9},{2... | collective-permute-start | bytes 1572872 | tf_op jit(solution)/shard_map/hidden_first_down1/ppermute | solution.py:31
  39.7 18.7 %collective-permute-start.21 = (bf16[2,128,1536]{2,1,0:T(8,128)(2,1)}, bf16[2,128,1536]{2,1,0:T(8,128)(2,1)S(1)}, u32[]{:S(2)}, u32[]{:S(2)}) collective-permute-start(bf16[2,128,1536]{2,1,0:T(8,128)(2,1)} %get-tuple-element.123), channel_id=1, source_target_pairs={{0,8},{4,12},{8,16},{12,20},{16,24},{20,28},{1,9},{5,13},{9,17},{1... | collective-permute-start | bytes 2359304 | tf_op jit(solution)/shard_map/hidden_last_up1/ppermute | solution.py:31
  42.0 21.7 %collective-permute-start.22 = (bf16[2,128,1536]{2,1,0:T(8,128)(2,1)}, bf16[2,128,1536]{2,1,0:T(8,128)(2,1)}, u32[]{:S(2)}, u32[]{:S(2)}) collective-permute-start(bf16[2,128,1536]{2,1,0:T(8,128)(2,1)} %get-tuple-element.123), channel_id=1, source_target_pairs={{8,0},{12,4},{16,8},{20,12},{24,16},{28,20},{9,1},{13,5},{17,9},{2... | collective-permute-start | bytes 2359304 | tf_op jit(solution)/shard_map/hidden_last_down1/ppermute | solution.py:31
  54.9 18.3 %collective-permute-start.11 = (bf16[128,2048]{1,0:T(8,128)(2,1)}, bf16[128,2048]{1,0:T(8,128)(2,1)S(1)}, u32[]{:S(2)}, u32[]{:S(2)}) collective-permute-start(bf16[128,2048]{1,0:T(8,128)(2,1)} %collective-permute-done.6), channel_id=1, source_target_pairs={{8,16},{12,20},{16,24},{20,28},{9,17},{13,21},{17,25},{21,29},{10,... | collective-permute-start | bytes 1572872 | tf_op jit(solution)/shard_map/hidden_first_up2/ppermute | solution.py:31
  55.6 18.1 %collective-permute-start.12 = (bf16[128,2048]{1,0:T(8,128)(2,1)}, bf16[128,2048]{1,0:T(8,128)(2,1)S(1)}, u32[]{:S(2)}, u32[]{:S(2)}) collective-permute-start(bf16[128,2048]{1,0:T(8,128)(2,1)} %collective-permute-done.7), channel_id=1, source_target_pairs={{8,0},{12,4},{16,8},{20,12},{9,1},{13,5},{17,9},{21,13},{10,2},{14... | collective-permute-start | bytes 1572872 | tf_op jit(solution)/shard_map/hidden_first_down2/ppermute | solution.py:31
  58.4 25.2 %collective-permute-start.10 = (bf16[1024,512]{1,0:T(8,128)(2,1)S(1)}, bf16[1024,512]{1,0:T(8,128)(2,1)S(1)}, u32[]{:S(2)}, u32[]{:S(2)}) collective-permute-start(bf16[1024,512]{1,0:T(8,128)(2,1)S(1)} %slice.79), channel_id=1, source_target_pairs={{0,4},{4,0},{8,12},{12,8},{16,20},{20,16},{24,28},{28,24},{1,5},{5... | collective-permute-start | bytes 3145736 | tf_op jit(solution)/shard_map/weight_side/ppermute | solution.py:35
  69.1 17.8 %collective-permute-start.15 = (f16[2,128,1536]{2,1,0:T(8,128)(2,1)S(1)}, f16[2,128,1536]{2,1,0:T(8,128)(2,1)S(1)}, u32[]{:S(2)}, u32[]{:S(2)}) collective-permute-start(f16[2,128,1536]{2,1,0:T(8,128)(2,1)S(1)} %get-tuple-element.100), channel_id=1, source_target_pairs={{0,8},{4,12},{1,9},{5,13},{2,10},{6,14},{3,11},{7,15}} | collective-permute-start | bytes 2359304 | tf_op jit(solution)/shard_map/dhid_last_up1/ppermute | solution.py:31
  72.4 18.9 %collective-permute-start.16 = (f16[2,128,1536]{2,1,0:T(8,128)(2,1)S(1)}, f16[2,128,1536]{2,1,0:T(8,128)(2,1)S(1)}, u32[]{:S(2)}, u32[]{:S(2)}) collective-permute-start(f16[2,128,1536]{2,1,0:T(8,128)(2,1)S(1)} %get-tuple-element.99), channel_id=1, source_target_pairs={{24,16},{28,20},{25,17},{29,21},{26,18},{30,22},{27,19},{31,23}} | collective-permute-start | bytes 2359304 | tf_op jit(solution)/shard_map/dhid_last_down1/ppermute | solution.py:31
  73.8 33.6 %collective-permute-start.23 = (bf16[2,128,1536]{2,1,0:T(8,128)(2,1)S(1)}, bf16[2,128,1536]{2,1,0:T(8,128)(2,1)S(1)}, u32[]{:S(2)}, u32[]{:S(2)}) collective-permute-start(bf16[2,128,1536]{2,1,0:T(8,128)(2,1)S(1)} %collective-permute-done.21), channel_id=1, source_target_pairs={{8,16},{12,20},{16,24},{20,28},{9,17},{13,21},{17,25},{21,29},{10,... | collective-permute-start | bytes 2359304 | tf_op jit(solution)/shard_map/hidden_last_up2/ppermute | solution.py:31
  74.5 33.6 %collective-permute-start.24 = (bf16[2,128,1536]{2,1,0:T(8,128)(2,1)}, bf16[2,128,1536]{2,1,0:T(8,128)(2,1)S(1)}, u32[]{:S(2)}, u32[]{:S(2)}) collective-permute-start(bf16[2,128,1536]{2,1,0:T(8,128)(2,1)} %collective-permute-done.22), channel_id=1, source_target_pairs={{8,0},{12,4},{16,8},{20,12},{9,1},{13,5},{17,9},{21,13},{10,2},{14... | collective-permute-start | bytes 2359304 | tf_op jit(solution)/shard_map/hidden_last_down2/ppermute | solution.py:31
  83.6 25.3 %collective-permute-start.32 = (bf16[128,2048]{1,0:T(8,128)(2,1)S(1)}, bf16[128,2048]{1,0:T(8,128)(2,1)S(1)}, u32[]{:S(2)}, u32[]{:S(2)}) collective-permute-start(bf16[128,2048]{1,0:T(8,128)(2,1)S(1)} %collective-permute-done.11), channel_id=1, source_target_pairs={{16,24},{20,28},{17,25},{21,29},{18,26},{22,30},{19,27},{23,31}} | collective-permute-start | bytes 1572872 | tf_op jit(solution)/shard_map/hidden_first_up3/ppermute | solution.py:31
  101.4 16.7 %collective-permute-start.33 = (bf16[128,2048]{1,0:T(8,128)(2,1)S(1)}, bf16[128,2048]{1,0:T(8,128)(2,1)S(1)}, u32[]{:S(2)}, u32[]{:S(2)}) collective-permute-start(bf16[128,2048]{1,0:T(8,128)(2,1)S(1)} %collective-permute-done.12), channel_id=1, source_target_pairs={{8,0},{12,4},{9,1},{13,5},{10,2},{14,6},{11,3},{15,7}} | collective-permute-start | bytes 1572872 | tf_op jit(solution)/shard_map/hidden_first_down3/ppermute | solution.py:31
  102.7 19.3 %collective-permute-start.17 = (f16[2,128,1536]{2,1,0:T(8,128)(2,1)S(1)}, f16[2,128,1536]{2,1,0:T(8,128)(2,1)S(1)}, u32[]{:S(2)}, u32[]{:S(2)}) collective-permute-start(f16[2,128,1536]{2,1,0:T(8,128)(2,1)S(1)} %get-tuple-element.62), channel_id=1, source_target_pairs={{0,8},{4,12},{8,16},{12,20},{1,9},{5,13},{9,17},{13,21},{2,10},{6,... | collective-permute-start | bytes 2359304 | tf_op jit(solution)/shard_map/dhid_last_up2/ppermute | solution.py:31
  108.1 23.2 %collective-permute-start.25 = (bf16[2,128,1536]{2,1,0:T(8,128)(2,1)S(1)}, bf16[2,128,1536]{2,1,0:T(8,128)(2,1)S(1)}, u32[]{:S(2)}, u32[]{:S(2)}) collective-permute-start(bf16[2,128,1536]{2,1,0:T(8,128)(2,1)S(1)} %collective-permute-done.23), channel_id=1, source_target_pairs={{16,24},{20,28},{17,25},{21,29},{18,26},{22,30},{19,27},{23,31}} | collective-permute-start | bytes 2359304 | tf_op jit(solution)/shard_map/hidden_last_up3/ppermute | solution.py:31
  108.9 27.2 %collective-permute-start.26 = (bf16[2,128,1536]{2,1,0:T(8,128)(2,1)S(1)}, bf16[2,128,1536]{2,1,0:T(8,128)(2,1)S(1)}, u32[]{:S(2)}, u32[]{:S(2)}) collective-permute-start(bf16[2,128,1536]{2,1,0:T(8,128)(2,1)S(1)} %collective-permute-done.24), channel_id=1, source_target_pairs={{8,0},{12,4},{9,1},{13,5},{10,2},{14,6},{11,3},{15,7}} | collective-permute-start | bytes 2359304 | tf_op jit(solution)/shard_map/hidden_last_down3/ppermute | solution.py:31
  119.7 45.8 %collective-permute-start.34 = (bf16[4,128,2048]{2,1,0:T(8,128)(2,1)S(1)}, bf16[4,128,2048]{2,1,0:T(8,128)(2,1)S(1)}, u32[]{:S(2)}, u32[]{:S(2)}) collective-permute-start(bf16[4,128,2048]{2,1,0:T(8,128)(2,1)S(1)} %get-tuple-element.88), channel_id=1, source_target_pairs={{0,4},{4,0},{8,12},{12,8},{16,20},{20,16},{24,28},{28,24},{1,5},{5... | collective-permute-start | bytes 6291464 | tf_op jit(solution)/shard_map/hidden_first_side/ppermute | solution.py:35
  122.6 32.7 %collective-permute-start.27 = (f16[2,128,1536]{2,1,0:T(8,128)(2,1)S(1)}, f16[2,128,1536]{2,1,0:T(8,128)(2,1)S(1)}, u32[]{:S(2)}, u32[]{:S(2)}) collective-permute-start(f16[2,128,1536]{2,1,0:T(8,128)(2,1)S(1)} %get-tuple-element.96), channel_id=1, source_target_pairs={{0,8},{4,12},{8,16},{12,20},{16,24},{20,28},{1,9},{5,13},{9,17},{1... | collective-permute-start | bytes 2359304 | tf_op jit(solution)/shard_map/dhid_last_up3/ppermute | solution.py:31
  130.0 25.3 %collective-permute-start.28 = (f16[2,128,1536]{2,1,0:T(8,128)(2,1)S(1)}, f16[2,128,1536]{2,1,0:T(8,128)(2,1)S(1)}, u32[]{:S(2)}, u32[]{:S(2)}) collective-permute-start(f16[2,128,1536]{2,1,0:T(8,128)(2,1)S(1)} %get-tuple-element.95), channel_id=1, source_target_pairs={{8,0},{12,4},{16,8},{20,12},{24,16},{28,20},{9,1},{13,5},{17,9},{2... | collective-permute-start | bytes 2359304 | tf_op jit(solution)/shard_map/dhid_last_down3/ppermute | solution.py:31
  131.3 23.6 %collective-permute-start.19 = (f16[128,2048]{1,0:T(8,128)(2,1)S(1)}, f16[128,2048]{1,0:T(8,128)(2,1)S(1)}, u32[]{:S(2)}, u32[]{:S(2)}) collective-permute-start(f16[128,2048]{1,0:T(8,128)(2,1)S(1)} %get-tuple-element.66), channel_id=1, source_target_pairs={{0,8},{4,12},{8,16},{12,20},{1,9},{5,13},{9,17},{13,21},{2,10},{6,... | collective-permute-start | bytes 1572872 | tf_op jit(solution)/shard_map/dhid_first_up2/ppermute | solution.py:31
  136.1 18.9 %collective-permute-start.20 = (f16[128,2048]{1,0:T(8,128)(2,1)S(1)}, f16[128,2048]{1,0:T(8,128)(2,1)S(1)}, u32[]{:S(2)}, u32[]{:S(2)}) collective-permute-start(f16[128,2048]{1,0:T(8,128)(2,1)S(1)} %get-tuple-element.68), channel_id=1, source_target_pairs={{16,8},{20,12},{24,16},{28,20},{17,9},{21,13},{25,17},{29,21},{18,... | collective-permute-start | bytes 1572872 | tf_op jit(solution)/shard_map/dhid_first_down2/ppermute | solution.py:31
  155.3 16.5 %collective-permute-start.29 = (f16[128,2048]{1,0:T(8,128)(2,1)S(1)}, f16[128,2048]{1,0:T(8,128)(2,1)S(1)}, u32[]{:S(2)}, u32[]{:S(2)}) collective-permute-start(f16[128,2048]{1,0:T(8,128)(2,1)S(1)} %get-tuple-element.79), channel_id=1, source_target_pairs={{0,8},{4,12},{8,16},{12,20},{16,24},{20,28},{1,9},{5,13},{9,17},{1... | collective-permute-start | bytes 1572872 | tf_op jit(solution)/shard_map/dhid_first_up3/ppermute | solution.py:31
  (16 other events, 163.8 us)

commit v7 on v5

--- a/solution.py
+++ b/solution.py
@@ -4,7 +4,7 @@
 from jax.sharding import PartitionSpec as P
 
 WIRE = jnp.float16
-WIRE_SCALE = 16.0
+WIRE_SCALE = 32.0
 
 
 def after(value, *others):

time: 170 us -> 170 us (level)
  no operation moved by 1% of the time
where the time goes in v7:
time: 170 us; the launch traced here: 169 us
  starting transfers between devices  70.5 us (41%)
  waiting for transfers between devices  57.7 us (34%)
  other arithmetic  19.7 us (12%)
  local copies, waits for them, and re-layouts  10.7 us (6%)
  matrix products  8.68 us (5%)
    ppermute x24, starting transfers between devices, along(): return lax.ppermute(value, 'dp', pairs)  51.1 us
    ppermute x24, waiting for transfers between devices, along(): return lax.ppermute(value, 'dp', pairs)  35.7 us
    ppermute x7, waiting for transfers between devices, across(): return lax.ppermute(value, 'dp', [(at, at ^ 1) for at in range(dp)])  13.9 us
    ppermute x7, starting transfers between devices, across(): return lax.ppermute(value, 'dp', [(at, at ^ 1) for at in range(dp)])  10.6 us
    ppermute x2, starting transfers between devices, shards(): arrived.append(lax.ppermute(piece, ('dp', 'tensor'), pairs))  7.46 us
    unnamed x18, local copies, waits for them, and re-layouts  5.84 us
    ppermute x2, waiting for transfers between devices, shards(): arrived.append(lax.ppermute(piece, ('dp', 'tensor'), pairs))  5.65 us
    dot_general x3, matrix products, product(): jnp.einsum('...f,hf->...h', left, right, preferred_element_type=jnp.float32)  4.39 us
  transfers between devices with their start and end apart: 35, of which 13 were waited for; matrix products, arithmetic and copies ran while one was open for 19% of the time, Pallas kernels for 0%

profile of v7, /device:TPU:0, one launch (start us, length us, event | category | flops | bytes accessed | tf_op | source)
XLA Modules:
  0.0 168.6 jit_solution(2644604457221472495)
XLA Ops:
  2.4 6.8 %collective-permute-start.1 = (bf16[64,1024]{1,0:T(8,128)(2,1)S(1)}, bf16[64,1024]{1,0:T(8,128)(2,1)S(1)}, u32[]{:S(2)}, u32[]{:S(2)}) collective-permute-start(bf16[64,1024]{1,0:T(8,128)(2,1)S(1)} %get-tuple-element.128), channel_id=1, source_target_pairs={{0,2},{1,10},{2,18},{3,26},{4,6},{5,14},{6,22},{7,30},{8,3},{9,11}... | collective-permute-start | bytes 393224 | tf_op jit(solution)/shard_map/cotangent_spread/ppermute | solution.py:59
  15.6 5.6 %collective-permute-done.1 = bf16[64,1024]{1,0:T(8,128)(2,1)S(1)} collective-permute-done((bf16[64,1024]{1,0:T(8,128)(2,1)S(1)}, bf16[64,1024]{1,0:T(8,128)(2,1)S(1)}, u32[]{:S(2)}, u32[]{:S(2)}) %collective-permute-start.1) | collective-permute-done | bytes 131104 | tf_op jit(solution)/shard_map/cotangent_spread/ppermute | solution.py:59
  25.7 4.1 %collective-permute-start.6 = (bf16[128,2048]{1,0:T(8,128)(2,1)S(1)}, bf16[128,2048]{1,0:T(8,128)(2,1)S(1)}, u32[]{:S(2)}, u32[]{:S(2)}) collective-permute-start(bf16[128,2048]{1,0:T(8,128)(2,1)S(1)} %get-tuple-element.51), channel_id=1, source_target_pairs={{0,8},{4,12},{8,16},{12,20},{16,24},{20,28},{1,9},{5,13},{9,17},{1... | collective-permute-start | bytes 1572872 | tf_op jit(solution)/shard_map/hidden_first_up1/ppermute | solution.py:31
  31.2 4.8 %collective-permute-done.3 = bf16[2,64,512]{2,1,0:T(8,128)(2,1)S(1)} collective-permute-done((bf16[2,64,512]{2,1,0:T(8,128)(2,1)S(1)}, bf16[2,64,512]{2,1,0:T(8,128)(2,1)S(1)}, u32[]{:S(2)}, u32[]{:S(2)}) %collective-permute-start.3) | collective-permute-done | bytes 131104 | tf_op jit(solution)/shard_map/cotangent_side/ppermute | solution.py:35
  41.1 2.3 %collective-permute-start.21 = (bf16[2,128,1536]{2,1,0:T(8,128)(2,1)}, bf16[2,128,1536]{2,1,0:T(8,128)(2,1)S(1)}, u32[]{:S(2)}, u32[]{:S(2)}) collective-permute-start(bf16[2,128,1536]{2,1,0:T(8,128)(2,1)} %get-tuple-element.123), channel_id=1, source_target_pairs={{0,8},{4,12},{8,16},{12,20},{16,24},{20,28},{1,9},{5,13},{9,17},{1... | collective-permute-start | bytes 2359304 | tf_op jit(solution)/shard_map/hidden_last_up1/ppermute | solution.py:31
  44.7 2.4 %collective-permute-done.5 = bf16[3,2,1,64,512]{4,3,1,0,2:T(8,128)(2,1)} collective-permute-done((bf16[3,2,1,64,512]{4,3,1,0,2:T(8,128)(2,1)S(1)}, bf16[3,2,1,64,512]{4,3,1,0,2:T(8,128)(2,1)}, u32[]{:S(2)}, u32[]{:S(2)}) %collective-permute-start.5) | collective-permute-done | bytes 393248 | tf_op jit(solution)/shard_map/cotangent_shares/ppermute | solution.py:85
  48.3 3.3 %collective-permute-done.8 = bf16[512,512]{1,0:T(8,128)(2,1)} collective-permute-done((bf16[512,512]{1,0:T(8,128)(2,1)}, bf16[512,512]{1,0:T(8,128)(2,1)}, u32[]{:S(2)}, u32[]{:S(2)}) %collective-permute-start.8) | collective-permute-done | bytes 524320 | tf_op jit(solution)/shard_map/weight_side/ppermute | solution.py:35
  57.1 2.7 %collective-permute-done.21 = bf16[2,128,1536]{2,1,0:T(8,128)(2,1)S(1)} collective-permute-done((bf16[2,128,1536]{2,1,0:T(8,128)(2,1)}, bf16[2,128,1536]{2,1,0:T(8,128)(2,1)S(1)}, u32[]{:S(2)}, u32[]{:S(2)}) %collective-permute-start.21) | collective-permute-done | bytes 786464 | tf_op jit(solution)/shard_map/hidden_last_up1/ppermute | solution.py:31
  60.3 5.8 %collective-permute-done.22 = bf16[2,128,1536]{2,1,0:T(8,128)(2,1)} collective-permute-done((bf16[2,128,1536]{2,1,0:T(8,128)(2,1)}, bf16[2,128,1536]{2,1,0:T(8,128)(2,1)}, u32[]{:S(2)}, u32[]{:S(2)}) %collective-permute-start.22) | collective-permute-done | bytes 786464 | tf_op jit(solution)/shard_map/hidden_last_down1/ppermute | solution.py:31
  71.4 3.6 %collective-permute-start.15 = (f16[2,128,1536]{2,1,0:T(8,128)(2,1)S(1)}, f16[2,128,1536]{2,1,0:T(8,128)(2,1)S(1)}, u32[]{:S(2)}, u32[]{:S(2)}) collective-permute-start(f16[2,128,1536]{2,1,0:T(8,128)(2,1)S(1)} %get-tuple-element.100), channel_id=1, source_target_pairs={{0,8},{4,12},{1,9},{5,13},{2,10},{6,14},{3,11},{7,15}} | collective-permute-start | bytes 2359304 | tf_op jit(solution)/shard_map/dhid_last_up1/ppermute | solution.py:31
  79.2 3.9 %collective-permute-done.10 = bf16[1024,512]{1,0:T(8,128)(2,1)S(1)} collective-permute-done((bf16[1024,512]{1,0:T(8,128)(2,1)S(1)}, bf16[1024,512]{1,0:T(8,128)(2,1)S(1)}, u32[]{:S(2)}, u32[]{:S(2)}) %collective-permute-start.10) | collective-permute-done | bytes 1048608 | tf_op jit(solution)/shard_map/weight_side/ppermute | solution.py:35
  85.3 3.0 %collective-permute-done.15 = f16[2,128,1536]{2,1,0:T(8,128)(2,1)S(1)} collective-permute-done((f16[2,128,1536]{2,1,0:T(8,128)(2,1)S(1)}, f16[2,128,1536]{2,1,0:T(8,128)(2,1)S(1)}, u32[]{:S(2)}, u32[]{:S(2)}) %collective-permute-start.15) | collective-permute-done | bytes 786464 | tf_op jit(solution)/shard_map/dhid_last_up1/ppermute | solution.py:31
  88.3 4.4 %collective-permute-start.13 = (f16[128,2048]{1,0:T(8,128)(2,1)S(1)}, f16[128,2048]{1,0:T(8,128)(2,1)S(1)}, u32[]{:S(2)}, u32[]{:S(2)}) collective-permute-start(f16[128,2048]{1,0:T(8,128)(2,1)S(1)} %get-tuple-element.58), channel_id=1, source_target_pairs={{0,8},{4,12},{1,9},{5,13},{2,10},{6,14},{3,11},{7,15}} | collective-permute-start | bytes 1572872 | tf_op jit(solution)/shard_map/dhid_first_up1/ppermute | solution.py:31
  93.9 5.5 %collective-permute-done.13 = f16[128,2048]{1,0:T(8,128)(2,1)S(1)} collective-permute-done((f16[128,2048]{1,0:T(8,128)(2,1)S(1)}, f16[128,2048]{1,0:T(8,128)(2,1)S(1)}, u32[]{:S(2)}, u32[]{:S(2)}) %collective-permute-start.13) | collective-permute-done | bytes 524320 | tf_op jit(solution)/shard_map/dhid_first_up1/ppermute | solution.py:31
  100.7 4.6 %collective-permute-start.17 = (f16[2,128,1536]{2,1,0:T(8,128)(2,1)S(1)}, f16[2,128,1536]{2,1,0:T(8,128)(2,1)S(1)}, u32[]{:S(2)}, u32[]{:S(2)}) collective-permute-start(f16[2,128,1536]{2,1,0:T(8,128)(2,1)S(1)} %get-tuple-element.62), channel_id=1, source_target_pairs={{0,8},{4,12},{8,16},{12,20},{1,9},{5,13},{9,17},{13,21},{2,10},{6,... | collective-permute-start | bytes 2359304 | tf_op jit(solution)/shard_map/dhid_last_up2/ppermute | solution.py:31
  108.2 7.6 %collective-permute-done.33 = bf16[128,2048]{1,0:T(8,128)(2,1)S(1)} collective-permute-done((bf16[128,2048]{1,0:T(8,128)(2,1)S(1)}, bf16[128,2048]{1,0:T(8,128)(2,1)S(1)}, u32[]{:S(2)}, u32[]{:S(2)}) %collective-permute-start.33) | collective-permute-done | bytes 524320 | tf_op jit(solution)/shard_map/hidden_first_down3/ppermute | solution.py:31
  118.2 4.9 %collective-permute-start.27 = (f16[2,128,1536]{2,1,0:T(8,128)(2,1)S(1)}, f16[2,128,1536]{2,1,0:T(8,128)(2,1)S(1)}, u32[]{:S(2)}, u32[]{:S(2)}) collective-permute-start(f16[2,128,1536]{2,1,0:T(8,128)(2,1)S(1)} %get-tuple-element.96), channel_id=1, source_target_pairs={{0,8},{4,12},{8,16},{12,20},{16,24},{20,28},{1,9},{5,13},{9,17},{1... | collective-permute-start | bytes 2359304 | tf_op jit(solution)/shard_map/dhid_last_up3/ppermute | solution.py:31
  124.4 4.7 %collective-permute-start.19 = (f16[128,2048]{1,0:T(8,128)(2,1)S(1)}, f16[128,2048]{1,0:T(8,128)(2,1)S(1)}, u32[]{:S(2)}, u32[]{:S(2)}) collective-permute-start(f16[128,2048]{1,0:T(8,128)(2,1)S(1)} %get-tuple-element.66), channel_id=1, source_target_pairs={{0,8},{4,12},{8,16},{12,20},{1,9},{5,13},{9,17},{13,21},{2,10},{6,... | collective-permute-start | bytes 1572872 | tf_op jit(solution)/shard_map/dhid_first_up2/ppermute | solution.py:31
  129.1 3.5 %collective-permute-done.26 = bf16[2,128,1536]{2,1,0:T(8,128)(2,1)S(1)} collective-permute-done((bf16[2,128,1536]{2,1,0:T(8,128)(2,1)S(1)}, bf16[2,128,1536]{2,1,0:T(8,128)(2,1)S(1)}, u32[]{:S(2)}, u32[]{:S(2)}) %collective-permute-start.26) | collective-permute-done | bytes 786464 | tf_op jit(solution)/shard_map/hidden_last_down3/ppermute | solution.py:31
  136.7 7.6 %collective-permute-done.19 = f16[128,2048]{1,0:T(8,128)(2,1)S(1)} collective-permute-done((f16[128,2048]{1,0:T(8,128)(2,1)S(1)}, f16[128,2048]{1,0:T(8,128)(2,1)S(1)}, u32[]{:S(2)}, u32[]{:S(2)}) %collective-permute-start.19) | collective-permute-done | bytes 524320 | tf_op jit(solution)/shard_map/dhid_first_up2/ppermute | solution.py:31
  145.7 6.3 %collective-permute-start.29 = (f16[128,2048]{1,0:T(8,128)(2,1)}, f16[128,2048]{1,0:T(8,128)(2,1)S(1)}, u32[]{:S(2)}, u32[]{:S(2)}) collective-permute-start(f16[128,2048]{1,0:T(8,128)(2,1)} %get-tuple-element.79), channel_id=1, source_target_pairs={{0,8},{4,12},{8,16},{12,20},{16,24},{20,28},{1,9},{5,13},{9,17},{1... | collective-permute-start | bytes 1572872 | tf_op jit(solution)/shard_map/dhid_first_up3/ppermute | solution.py:31
  153.7 4.9 %collective-permute-start.31 = (f16[128,1536]{1,0:T(8,128)(2,1)S(1)}, f16[128,1536]{1,0:T(8,128)(2,1)S(1)}, u32[]{:S(2)}, u32[]{:S(2)}) collective-permute-start(f16[128,1536]{1,0:T(8,128)(2,1)S(1)} %fusion.37), channel_id=1, source_target_pairs={{0,4},{4,0},{8,12},{12,8},{16,20},{20,16},{24,28},{28,24},{1,5},{5... | collective-permute-start | bytes 1179656 | tf_op jit(solution)/shard_map/dhid_last_side/ppermute | solution.py:35
  158.6 2.4 %bitcast_multiply_fusion = f32[2048,512]{1,0:T(8,128)S(1)} fusion(bf16[4,1,128,512]{3,2,1,0:T(8,128)(2,1)S(1)} %bitcast.128, bf16[4,1,128,512]{3,2,1,0:T(8,128)(2,1)S(1)} %bitcast.124, bf16[4,1,128,2048]{3,2,0,1:T(8,128)(2,1)S(1)} %bitcast.134, bf16[4,1,128,2048]{3,2,0,1:T(8,128)(2,1)S(1)} %get-tuple-element.111), kind=kOutput, calls=%fused_computation.3 | convolution fusion | flops 2151153664 | bytes 9437184 | tf_op jit(solution)/shard_map/kstc,kstf->cf/dot_general | solution.py:168
  161.1 3.9 %pad_maximum_fusion = f32[3584,512]{1,0:T(8,128)} fusion(f32[1536,512]{1,0:T(8,128)S(1)} %fusion.2, f32[2048,512]{1,0:T(8,128)S(1)} %bitcast_multiply_fusion), kind=kLoop, calls=%fused_computation | loop fusion | flops 1835008 | bytes 14680064 | tf_op jit(solution)/shard_map/concatenate | solution.py:171
  (104 shorter events, 58.5 us)
Async XLA Ops:
  2.4 18.8 %collective-permute-start.1 = (bf16[64,1024]{1,0:T(8,128)(2,1)S(1)}, bf16[64,1024]{1,0:T(8,128)(2,1)S(1)}, u32[]{:S(2)}, u32[]{:S(2)}) collective-permute-start(bf16[64,1024]{1,0:T(8,128)(2,1)S(1)} %get-tuple-element.128), channel_id=1, source_target_pairs={{0,2},{1,10},{2,18},{3,26},{4,6},{5,14},{6,22},{7,30},{8,3},{9,11}... | collective-permute-start | bytes 393224 | tf_op jit(solution)/shard_map/cotangent_spread/ppermute | solution.py:59
  15.1 20.9 %collective-permute-start.4 = (bf16[512,512]{1,0:T(8,128)(2,1)}, bf16[512,512]{1,0:T(8,128)(2,1)S(1)}, u32[]{:S(2)}, u32[]{:S(2)}) collective-permute-start(bf16[512,512]{1,0:T(8,128)(2,1)} %get-tuple-element.108), channel_id=1, source_target_pairs={{0,4},{4,0},{8,12},{12,8},{16,20},{20,16},{24,28},{28,24},{1,5},{5... | collective-permute-start | bytes 1572872 | tf_op jit(solution)/shard_map/weight_side/ppermute | solution.py:35
  25.7 17.6 %collective-permute-start.6 = (bf16[128,2048]{1,0:T(8,128)(2,1)S(1)}, bf16[128,2048]{1,0:T(8,128)(2,1)S(1)}, u32[]{:S(2)}, u32[]{:S(2)}) collective-permute-start(bf16[128,2048]{1,0:T(8,128)(2,1)S(1)} %get-tuple-element.51), channel_id=1, source_target_pairs={{0,8},{4,12},{8,16},{12,20},{16,24},{20,28},{1,9},{5,13},{9,17},{1... | collective-permute-start | bytes 1572872 | tf_op jit(solution)/shard_map/hidden_first_up1/ppermute | solution.py:31
  29.9 14.8 %collective-permute-start.7 = (bf16[128,2048]{1,0:T(8,128)(2,1)S(1)}, bf16[128,2048]{1,0:T(8,128)(2,1)}, u32[]{:S(2)}, u32[]{:S(2)}) collective-permute-start(bf16[128,2048]{1,0:T(8,128)(2,1)S(1)} %get-tuple-element.51), channel_id=1, source_target_pairs={{8,0},{12,4},{16,8},{20,12},{24,16},{28,20},{9,1},{13,5},{17,9},{2... | collective-permute-start | bytes 1572872 | tf_op jit(solution)/shard_map/hidden_first_down1/ppermute | solution.py:31
  41.1 18.7 %collective-permute-start.21 = (bf16[2,128,1536]{2,1,0:T(8,128)(2,1)}, bf16[2,128,1536]{2,1,0:T(8,128)(2,1)S(1)}, u32[]{:S(2)}, u32[]{:S(2)}) collective-permute-start(bf16[2,128,1536]{2,1,0:T(8,128)(2,1)} %get-tuple-element.123), channel_id=1, source_target_pairs={{0,8},{4,12},{8,16},{12,20},{16,24},{20,28},{1,9},{5,13},{9,17},{1... | collective-permute-start | bytes 2359304 | tf_op jit(solution)/shard_map/hidden_last_up1/ppermute | solution.py:31
  43.4 22.7 %collective-permute-start.22 = (bf16[2,128,1536]{2,1,0:T(8,128)(2,1)}, bf16[2,128,1536]{2,1,0:T(8,128)(2,1)}, u32[]{:S(2)}, u32[]{:S(2)}) collective-permute-start(bf16[2,128,1536]{2,1,0:T(8,128)(2,1)} %get-tuple-element.123), channel_id=1, source_target_pairs={{8,0},{12,4},{16,8},{20,12},{24,16},{28,20},{9,1},{13,5},{17,9},{2... | collective-permute-start | bytes 2359304 | tf_op jit(solution)/shard_map/hidden_last_down1/ppermute | solution.py:31
  51.6 14.5 %collective-permute-start.9 = (bf16[3,2,2,64,512]{4,3,1,0,2:T(8,128)(2,1)S(1)}, bf16[3,2,2,64,512]{4,3,1,0,2:T(8,128)(2,1)}, u32[]{:S(2)}, u32[]{:S(2)}) collective-permute-start(bf16[3,2,2,64,512]{4,3,1,0,2:T(8,128)(2,1)S(1)} %maximum_bitcast_fusion), channel_id=1, source_target_pairs={{0,1},{1,0},{2,3},{3,2},{4,5},{5,4},{6,7},{7,6},{8,9},{9,8},{10,11... | collective-permute-start | bytes 2359304 | tf_op jit(solution)/shard_map/cotangent_core/ppermute | solution.py:92
  54.0 21.8 %collective-permute-start.11 = (bf16[128,2048]{1,0:T(8,128)(2,1)}, bf16[128,2048]{1,0:T(8,128)(2,1)S(1)}, u32[]{:S(2)}, u32[]{:S(2)}) collective-permute-start(bf16[128,2048]{1,0:T(8,128)(2,1)} %copy-done.5), channel_id=1, source_target_pairs={{8,16},{12,20},{16,24},{20,28},{9,17},{13,21},{17,25},{21,29},{10,... | collective-permute-start | bytes 1572872 | tf_op jit(solution)/shard_map/hidden_first_up2/ppermute | solution.py:31
  54.7 21.1 %collective-permute-start.12 = (bf16[128,2048]{1,0:T(8,128)(2,1)}, bf16[128,2048]{1,0:T(8,128)(2,1)S(1)}, u32[]{:S(2)}, u32[]{:S(2)}) collective-permute-start(bf16[128,2048]{1,0:T(8,128)(2,1)} %collective-permute-done.7), channel_id=1, source_target_pairs={{8,0},{12,4},{16,8},{20,12},{9,1},{13,5},{17,9},{21,13},{10,2},{14... | collective-permute-start | bytes 1572872 | tf_op jit(solution)/shard_map/hidden_first_down2/ppermute | solution.py:31
  59.8 23.3 %collective-permute-start.10 = (bf16[1024,512]{1,0:T(8,128)(2,1)S(1)}, bf16[1024,512]{1,0:T(8,128)(2,1)S(1)}, u32[]{:S(2)}, u32[]{:S(2)}) collective-permute-start(bf16[1024,512]{1,0:T(8,128)(2,1)S(1)} %slice.79), channel_id=1, source_target_pairs={{0,4},{4,0},{8,12},{12,8},{16,20},{20,16},{24,28},{28,24},{1,5},{5... | collective-permute-start | bytes 3145736 | tf_op jit(solution)/shard_map/weight_side/ppermute | solution.py:35
  71.4 16.9 %collective-permute-start.15 = (f16[2,128,1536]{2,1,0:T(8,128)(2,1)S(1)}, f16[2,128,1536]{2,1,0:T(8,128)(2,1)S(1)}, u32[]{:S(2)}, u32[]{:S(2)}) collective-permute-start(f16[2,128,1536]{2,1,0:T(8,128)(2,1)S(1)} %get-tuple-element.100), channel_id=1, source_target_pairs={{0,8},{4,12},{1,9},{5,13},{2,10},{6,14},{3,11},{7,15}} | collective-permute-start | bytes 2359304 | tf_op jit(solution)/shard_map/dhid_last_up1/ppermute | solution.py:31
  75.0 17.7 %collective-permute-start.16 = (f16[2,128,1536]{2,1,0:T(8,128)(2,1)S(1)}, f16[2,128,1536]{2,1,0:T(8,128)(2,1)S(1)}, u32[]{:S(2)}, u32[]{:S(2)}) collective-permute-start(f16[2,128,1536]{2,1,0:T(8,128)(2,1)S(1)} %get-tuple-element.99), channel_id=1, source_target_pairs={{24,16},{28,20},{25,17},{29,21},{26,18},{30,22},{27,19},{31,23}} | collective-permute-start | bytes 2359304 | tf_op jit(solution)/shard_map/dhid_last_down1/ppermute | solution.py:31
  75.8 29.5 %collective-permute-start.23 = (bf16[2,128,1536]{2,1,0:T(8,128)(2,1)S(1)}, bf16[2,128,1536]{2,1,0:T(8,128)(2,1)S(1)}, u32[]{:S(2)}, u32[]{:S(2)}) collective-permute-start(bf16[2,128,1536]{2,1,0:T(8,128)(2,1)S(1)} %collective-permute-done.21), channel_id=1, source_target_pairs={{8,16},{12,20},{16,24},{20,28},{9,17},{13,21},{17,25},{21,29},{10,... | collective-permute-start | bytes 2359304 | tf_op jit(solution)/shard_map/hidden_last_up2/ppermute | solution.py:31
  76.5 29.5 %collective-permute-start.24 = (bf16[2,128,1536]{2,1,0:T(8,128)(2,1)}, bf16[2,128,1536]{2,1,0:T(8,128)(2,1)S(1)}, u32[]{:S(2)}, u32[]{:S(2)}) collective-permute-start(bf16[2,128,1536]{2,1,0:T(8,128)(2,1)} %collective-permute-done.22), channel_id=1, source_target_pairs={{8,0},{12,4},{16,8},{20,12},{9,1},{13,5},{17,9},{21,13},{10,2},{14... | collective-permute-start | bytes 2359304 | tf_op jit(solution)/shard_map/hidden_last_down2/ppermute | solution.py:31
  83.1 23.8 %collective-permute-start.32 = (bf16[128,2048]{1,0:T(8,128)(2,1)S(1)}, bf16[128,2048]{1,0:T(8,128)(2,1)S(1)}, u32[]{:S(2)}, u32[]{:S(2)}) collective-permute-start(bf16[128,2048]{1,0:T(8,128)(2,1)S(1)} %collective-permute-done.11), channel_id=1, source_target_pairs={{16,24},{20,28},{17,25},{21,29},{18,26},{22,30},{19,27},{23,31}} | collective-permute-start | bytes 1572872 | tf_op jit(solution)/shard_map/hidden_first_up3/ppermute | solution.py:31
  99.4 16.4 %collective-permute-start.33 = (bf16[128,2048]{1,0:T(8,128)(2,1)S(1)}, bf16[128,2048]{1,0:T(8,128)(2,1)S(1)}, u32[]{:S(2)}, u32[]{:S(2)}) collective-permute-start(bf16[128,2048]{1,0:T(8,128)(2,1)S(1)} %collective-permute-done.12), channel_id=1, source_target_pairs={{8,0},{12,4},{9,1},{13,5},{10,2},{14,6},{11,3},{15,7}} | collective-permute-start | bytes 1572872 | tf_op jit(solution)/shard_map/hidden_first_down3/ppermute | solution.py:31
  100.7 17.0 %collective-permute-start.17 = (f16[2,128,1536]{2,1,0:T(8,128)(2,1)S(1)}, f16[2,128,1536]{2,1,0:T(8,128)(2,1)S(1)}, u32[]{:S(2)}, u32[]{:S(2)}) collective-permute-start(f16[2,128,1536]{2,1,0:T(8,128)(2,1)S(1)} %get-tuple-element.62), channel_id=1, source_target_pairs={{0,8},{4,12},{8,16},{12,20},{1,9},{5,13},{9,17},{13,21},{2,10},{6,... | collective-permute-start | bytes 2359304 | tf_op jit(solution)/shard_map/dhid_last_up2/ppermute | solution.py:31
  106.0 18.4 %collective-permute-start.25 = (bf16[2,128,1536]{2,1,0:T(8,128)(2,1)S(1)}, bf16[2,128,1536]{2,1,0:T(8,128)(2,1)S(1)}, u32[]{:S(2)}, u32[]{:S(2)}) collective-permute-start(bf16[2,128,1536]{2,1,0:T(8,128)(2,1)S(1)} %collective-permute-done.23), channel_id=1, source_target_pairs={{16,24},{20,28},{17,25},{21,29},{18,26},{22,30},{19,27},{23,31}} | collective-permute-start | bytes 2359304 | tf_op jit(solution)/shard_map/hidden_last_up3/ppermute | solution.py:31
  106.9 25.7 %collective-permute-start.26 = (bf16[2,128,1536]{2,1,0:T(8,128)(2,1)S(1)}, bf16[2,128,1536]{2,1,0:T(8,128)(2,1)S(1)}, u32[]{:S(2)}, u32[]{:S(2)}) collective-permute-start(bf16[2,128,1536]{2,1,0:T(8,128)(2,1)S(1)} %collective-permute-done.24), channel_id=1, source_target_pairs={{8,0},{12,4},{9,1},{13,5},{10,2},{14,6},{11,3},{15,7}} | collective-permute-start | bytes 2359304 | tf_op jit(solution)/shard_map/hidden_last_down3/ppermute | solution.py:31
  117.3 41.3 %collective-permute-start.34 = (bf16[4,128,2048]{2,1,0:T(8,128)(2,1)S(1)}, bf16[4,128,2048]{2,1,0:T(8,128)(2,1)S(1)}, u32[]{:S(2)}, u32[]{:S(2)}) collective-permute-start(bf16[4,128,2048]{2,1,0:T(8,128)(2,1)S(1)} %get-tuple-element.88), channel_id=1, source_target_pairs={{0,4},{4,0},{8,12},{12,8},{16,20},{20,16},{24,28},{28,24},{1,5},{5... | collective-permute-start | bytes 6291464 | tf_op jit(solution)/shard_map/hidden_first_side/ppermute | solution.py:35
  118.2 27.5 %collective-permute-start.27 = (f16[2,128,1536]{2,1,0:T(8,128)(2,1)S(1)}, f16[2,128,1536]{2,1,0:T(8,128)(2,1)S(1)}, u32[]{:S(2)}, u32[]{:S(2)}) collective-permute-start(f16[2,128,1536]{2,1,0:T(8,128)(2,1)S(1)} %get-tuple-element.96), channel_id=1, source_target_pairs={{0,8},{4,12},{8,16},{12,20},{16,24},{20,28},{1,9},{5,13},{9,17},{1... | collective-permute-start | bytes 2359304 | tf_op jit(solution)/shard_map/dhid_last_up3/ppermute | solution.py:31
  123.1 22.6 %collective-permute-start.28 = (f16[2,128,1536]{2,1,0:T(8,128)(2,1)S(1)}, f16[2,128,1536]{2,1,0:T(8,128)(2,1)S(1)}, u32[]{:S(2)}, u32[]{:S(2)}) collective-permute-start(f16[2,128,1536]{2,1,0:T(8,128)(2,1)S(1)} %get-tuple-element.95), channel_id=1, source_target_pairs={{8,0},{12,4},{16,8},{20,12},{24,16},{28,20},{9,1},{13,5},{17,9},{2... | collective-permute-start | bytes 2359304 | tf_op jit(solution)/shard_map/dhid_last_down3/ppermute | solution.py:31
  124.4 19.9 %collective-permute-start.19 = (f16[128,2048]{1,0:T(8,128)(2,1)S(1)}, f16[128,2048]{1,0:T(8,128)(2,1)S(1)}, u32[]{:S(2)}, u32[]{:S(2)}) collective-permute-start(f16[128,2048]{1,0:T(8,128)(2,1)S(1)} %get-tuple-element.66), channel_id=1, source_target_pairs={{0,8},{4,12},{8,16},{12,20},{1,9},{5,13},{9,17},{13,21},{2,10},{6,... | collective-permute-start | bytes 1572872 | tf_op jit(solution)/shard_map/dhid_first_up2/ppermute | solution.py:31
  145.7 19.3 %collective-permute-start.29 = (f16[128,2048]{1,0:T(8,128)(2,1)}, f16[128,2048]{1,0:T(8,128)(2,1)S(1)}, u32[]{:S(2)}, u32[]{:S(2)}) collective-permute-start(f16[128,2048]{1,0:T(8,128)(2,1)} %get-tuple-element.79), channel_id=1, source_target_pairs={{0,8},{4,12},{8,16},{12,20},{16,24},{20,28},{1,9},{5,13},{9,17},{1... | collective-permute-start | bytes 1572872 | tf_op jit(solution)/shard_map/dhid_first_up3/ppermute | solution.py:31
  (19 other events, 185.3 us)
